TPU v7x, 32 devices: a whole 2x2x4 slice. The times are simulated.
32 devices in a mesh: dp: 16 (over z, y, core), tensor: 2 (over x).
Axes of the slice: x: 2, y: 2, z: 4, core: 2. Of those that a mesh axis runs over, the one named last changes fastest.
Arguments:
- inputs: bfloat16 [16, 1024, 1024], P('dp', 'tensor'), may hold values from -6 to 6
- conditioning: bfloat16 [16, 1024], P('dp'), may hold values from -6 to 6
- mod_weight: bfloat16 [1024, 6, 1024], P(None, None, 'tensor'), may hold values from -0.1875 to 0.1875
- mod_bias: float32 [6, 1024], P(None, 'tensor'), may hold values from -1.8 to 1.8
- qkv_weight: bfloat16 [1024, 3, 1024], P(None, None, 'tensor'), may hold values from -0.1875 to 0.1875
- out_weight: bfloat16 [1024, 1024], P('tensor'), may hold values from -0.75 to 0.75
- up_projection_weight: bfloat16 [1024, 4096], P(None, 'tensor'), may hold values from -0.1875 to 0.1875
- down_projection_weight: bfloat16 [4096, 1024], P('tensor'), may hold values from -0.09375 to 0.09375
- cotangent: bfloat16 [16, 1024, 1024], P('dp', 'tensor'), may hold values from -6 to 6
Outputs:
- block_out: bfloat16 [16, 1024, 1024], P('dp', 'tensor')
- grad_inputs: bfloat16 [16, 1024, 1024], P('dp', 'tensor')
- grad_conditioning: float32 [16, 1024], P('dp')
- grad_mod_weight: float32 [1024, 6, 1024], P(None, None, 'tensor')
- grad_mod_bias: float32 [6, 1024], P(None, 'tensor')
- grad_qkv_weight: float32 [1024, 3, 1024], P(None, None, 'tensor')
- grad_out_weight: float32 [1024, 1024], P('tensor')
- grad_up_weight: float32 [1024, 4096], P(None, 'tensor')
- grad_down_weight: float32 [4096, 1024], P('tensor')
All inputs are finite; a program needn't handle non-finite values.
Results may differ from a plain program's by a relative error of at most 0.023.
Values may be sent and summed in bfloat16 or wider, within the bound.
A program may use at most 192 MiB of HBM per device.

v0:
```python
import jax
import jax.numpy as jnp
from jax import lax
from jax.sharding import PartitionSpec as P

HD = 64


norm_eps = 1e-06


def modulate(values_in, offset, stretch):
    center = jnp.mean(values_in, axis=-1, keepdims=True)
    deviate = values_in - center
    spread = jnp.mean(deviate * deviate, axis=-1, keepdims=True)
    return deviate * lax.rsqrt(spread + norm_eps) * (1.0 + stretch) + offset


def gelu_tanh(values_in):
    return jax.nn.gelu(values_in, approximate=True)


def attend_forward(query, keys, values, scale_factor, block_rows):
    length = query.shape[0]
    blocks = query.reshape(length // block_rows, block_rows, query.shape[1], query.shape[2])

    def one_block(qblock):
        scores = (
            jnp.einsum("qhd,khd->hqk", qblock, keys, preferred_element_type=jnp.float32)
            * scale_factor
        )
        row_peak = jnp.max(scores, axis=-1, keepdims=True)
        exponent = jnp.exp(scores - row_peak)
        row_total = jnp.sum(exponent, axis=-1, keepdims=True)
        shares = (exponent / row_total).astype(jnp.bfloat16)
        result = jnp.einsum("hqk,khd->qhd", shares, values, preferred_element_type=jnp.float32)
        return (result, row_peak[..., 0] + jnp.log(row_total[..., 0]))

    results, log_totals = lax.map(one_block, blocks)
    return (results.reshape(query.shape), log_totals)


def attend_backward(query, keys, values, grad_out, log_totals, scale_factor, block_rows):
    length, head_count, head_size = query.shape
    block_count = length // block_rows
    qblocks = query.reshape(block_count, block_rows, head_count, head_size)
    gblocks = grad_out.reshape(block_count, block_rows, head_count, head_size)

    def one_block(running, pieces):
        grad_keys, grad_values = running
        qblock, gblock, lblock = pieces
        scores = (
            jnp.einsum("qhd,khd->hqk", qblock, keys, preferred_element_type=jnp.float32)
            * scale_factor
        )
        shares = jnp.exp(scores - lblock[..., None])
        grad_shares = jnp.einsum("qhd,khd->hqk", gblock, values, preferred_element_type=jnp.float32)
        inner_sum = jnp.sum(shares * grad_shares, axis=-1, keepdims=True)
        grad_scores = (shares * (grad_shares - inner_sum)).astype(jnp.bfloat16)
        grad_query = (
            jnp.einsum("hqk,khd->qhd", grad_scores, keys, preferred_element_type=jnp.float32)
            * scale_factor
        )
        grad_keys = (
            grad_keys
            + jnp.einsum("hqk,qhd->khd", grad_scores, qblock, preferred_element_type=jnp.float32)
            * scale_factor
        )
        grad_values = grad_values + jnp.einsum(
            "hqk,qhd->khd", shares.astype(jnp.bfloat16), gblock, preferred_element_type=jnp.float32
        )
        return ((grad_keys, grad_values), grad_query.astype(jnp.bfloat16))

    zeroes = jnp.zeros((length, head_count, head_size), jnp.float32)
    finals, grad_query = lax.scan(one_block, (zeroes, zeroes), (qblocks, gblocks, log_totals))
    return (
        grad_query.reshape(query.shape),
        finals[0].astype(jnp.bfloat16),
        finals[1].astype(jnp.bfloat16),
    )


def body(
    inputs,
    conditioning,
    mod_weight,
    mod_bias,
    qkv_weight,
    out_weight,
    up_projection_weight,
    down_projection_weight,
    cotangent,
):
    latent_rows, local_len, width = inputs.shape
    local_cols = qkv_weight.shape[2]
    head_count = local_cols // HD
    length = local_len * lax.axis_size("tensor")
    block_rows = min(512, length)
    scale_factor = HD ** (-0.5)
    cond_float = conditioning.astype(jnp.float32)
    cond_silu, back_silu = jax.vjp(jax.nn.silu, cond_float)
    cond_act = cond_silu.astype(jnp.bfloat16)
    mod_local = (
        jnp.einsum("ld,dkc->lkc", cond_act, mod_weight, preferred_element_type=jnp.float32)
        + mod_bias[None]
    )
    modulation = lax.all_gather(mod_local, "tensor", axis=2, tiled=True)
    shift_one = modulation[:, 0:1, :]
    scale_one = modulation[:, 1:2, :]
    gate_one = modulation[:, 2:3, :]
    shift_two = modulation[:, 3:4, :]
    scale_two = modulation[:, 4:5, :]
    gate_two = modulation[:, 5:6, :]
    inputs_float = inputs.astype(jnp.float32)
    normed_float, back_one = jax.vjp(modulate, inputs_float, shift_one, scale_one)
    normed_one = normed_float.astype(jnp.bfloat16)
    normed_all = lax.all_gather(normed_one, "tensor", axis=1, tiled=True)
    projected = jnp.einsum(
        "lsd,dkc->lskc", normed_all, qkv_weight, preferred_element_type=jnp.float32
    ).astype(jnp.bfloat16)
    shaped = projected.reshape(latent_rows, length, 3, head_count, HD)

    def forward_latent(pieces):
        return attend_forward(pieces[:, 0], pieces[:, 1], pieces[:, 2], scale_factor, block_rows)

    attended, log_totals = lax.map(forward_latent, shaped)
    attended = attended.reshape(latent_rows, length, local_cols).astype(jnp.bfloat16)
    attn_terms = jnp.einsum("lsc,cd->lsd", attended, out_weight, preferred_element_type=jnp.float32)
    branch_attn = lax.psum_scatter(
        attn_terms.astype(jnp.bfloat16), "tensor", scatter_dimension=1, tiled=True
    ).astype(jnp.float32)
    middle = inputs_float + gate_one * branch_attn
    normed_float_two, back_two = jax.vjp(modulate, middle, shift_two, scale_two)
    normed_two = normed_float_two.astype(jnp.bfloat16)
    grad_out = cotangent.astype(jnp.float32)
    normed_second_gathered, cot_all = (
        lax.all_gather(normed_two, "tensor", axis=1, tiled=True),
        lax.all_gather(cotangent, "tensor", axis=1, tiled=True),
    )
    hidden_pre = jnp.einsum(
        "vwb,bj->vwj",
        normed_second_gathered,
        up_projection_weight,
        preferred_element_type=jnp.float32,
    )
    hidden_float, back_gelu = jax.vjp(gelu_tanh, hidden_pre)
    hidden_activation = hidden_float.astype(jnp.bfloat16)
    mlp_terms = jnp.einsum(
        "ewy,yz->ewz", hidden_activation, down_projection_weight, preferred_element_type=jnp.float32
    )
    branch_mlp = lax.psum_scatter(
        mlp_terms.astype(jnp.bfloat16), "tensor", scatter_dimension=1, tiled=True
    ).astype(jnp.float32)
    grad_feedforward = (gate_two * cot_all.astype(jnp.float32)).astype(jnp.bfloat16)
    grad_down_projection = jnp.einsum(
        "noi,nok->ik", hidden_activation, grad_feedforward, preferred_element_type=jnp.float32
    )
    grad_activation = jnp.einsum(
        "euz,hz->euh", grad_feedforward, down_projection_weight, preferred_element_type=jnp.float32
    )
    grad_preactivation = back_gelu(grad_activation)[0].astype(jnp.bfloat16)
    grad_up = jnp.einsum(
        "pae,paz->ez",
        normed_second_gathered,
        grad_preactivation,
        preferred_element_type=jnp.float32,
    )
    normed_terms = jnp.einsum(
        "qmt,zt->qmz", grad_preactivation, up_projection_weight, preferred_element_type=jnp.float32
    )
    grad_normed_two = lax.psum_scatter(
        normed_terms.astype(jnp.bfloat16), "tensor", scatter_dimension=1, tiled=True
    ).astype(jnp.float32)
    block_out = (middle + gate_two * branch_mlp).astype(jnp.bfloat16)
    grad_gate_two = jnp.sum(grad_out * branch_mlp, axis=1, keepdims=True)
    middle_back, grad_shift_two, grad_scale_two = back_two(grad_normed_two)
    grad_middle = grad_out + middle_back
    grad_gate_one = jnp.sum(grad_middle * branch_attn, axis=1, keepdims=True)
    grad_attn = (gate_one * grad_middle).astype(jnp.bfloat16)
    grad_attn_all = lax.all_gather(grad_attn, "tensor", axis=1, tiled=True)
    grad_out_weight = jnp.einsum(
        "lsc,lsd->cd", attended, grad_attn_all, preferred_element_type=jnp.float32
    )
    grad_attended = jnp.einsum(
        "lsd,cd->lsc", grad_attn_all, out_weight, preferred_element_type=jnp.float32
    ).astype(jnp.bfloat16)
    grad_shaped = grad_attended.reshape(latent_rows, length, head_count, HD)

    def backward_latent(pieces):
        qkv_rows, grad_rows, totals_rows = pieces
        return attend_backward(
            qkv_rows[:, 0],
            qkv_rows[:, 1],
            qkv_rows[:, 2],
            grad_rows,
            totals_rows,
            scale_factor,
            block_rows,
        )

    grad_query, grad_keys, grad_values = lax.map(backward_latent, (shaped, grad_shaped, log_totals))
    grad_qkv = jnp.stack((grad_query, grad_keys, grad_values), axis=2).reshape(
        latent_rows, length, 3, local_cols
    )
    grad_qkv_weight = jnp.einsum(
        "lsd,lskc->dkc", normed_all, grad_qkv, preferred_element_type=jnp.float32
    )
    normed_one_terms = jnp.einsum(
        "lskc,dkc->lsd", grad_qkv, qkv_weight, preferred_element_type=jnp.float32
    )
    grad_normed_one = lax.psum_scatter(
        normed_one_terms.astype(jnp.bfloat16), "tensor", scatter_dimension=1, tiled=True
    ).astype(jnp.float32)
    inputs_back, grad_shift_one, grad_scale_one = back_one(grad_normed_one)
    grad_inputs = (grad_middle + inputs_back).astype(jnp.bfloat16)
    modulation_terms = jnp.concatenate(
        (
            grad_shift_one,
            grad_scale_one,
            grad_gate_one,
            grad_shift_two,
            grad_scale_two,
            grad_gate_two,
        ),
        axis=1,
    )
    grad_modulation = lax.psum_scatter(
        modulation_terms.astype(jnp.bfloat16), "tensor", scatter_dimension=2, tiled=True
    )
    grad_mod_weight = jnp.einsum(
        "ld,lkc->dkc", cond_act, grad_modulation, preferred_element_type=jnp.float32
    )
    grad_mod_bias = jnp.sum(grad_modulation.astype(jnp.float32), axis=0)
    cond_terms = jnp.einsum(
        "lkc,dkc->ld", grad_modulation, mod_weight, preferred_element_type=jnp.float32
    )
    grad_cond_act = lax.psum(cond_terms, "tensor")
    grad_conditioning = back_silu(grad_cond_act)[0]
    summed = (
        lax.psum(grad_mod_weight.astype(jnp.bfloat16), "dp").astype(jnp.float32),
        lax.psum(grad_mod_bias.astype(jnp.bfloat16), "dp").astype(jnp.float32),
        lax.psum(grad_qkv_weight.astype(jnp.bfloat16), "dp").astype(jnp.float32),
        lax.psum(grad_out_weight.astype(jnp.bfloat16), "dp").astype(jnp.float32),
        lax.psum(grad_up.astype(jnp.bfloat16), "dp").astype(jnp.float32),
        lax.psum(grad_down_projection.astype(jnp.bfloat16), "dp").astype(jnp.float32),
    )
    return (
        block_out,
        grad_inputs,
        grad_conditioning,
        summed[0],
        summed[1],
        summed[2],
        summed[3],
        summed[4],
        summed[5],
    )


def solution(mesh):
    return jax.shard_map(
        body,
        mesh=mesh,
        in_specs=(
            P("dp", "tensor", None),
            P("dp", None),
            P(None, None, "tensor"),
            P(None, "tensor"),
            P(None, None, "tensor"),
            P("tensor", None),
            P(None, "tensor"),
            P("tensor", None),
            P("dp", "tensor", None),
        ),
        out_specs=(
            P("dp", "tensor", None),
            P("dp", "tensor", None),
            P("dp", None),
            P(None, None, "tensor"),
            P(None, "tensor"),
            P(None, None, "tensor"),
            P("tensor", None),
            P(None, "tensor"),
            P("tensor", None),
        ),
        check_vma=False,
    )
```

profile of v0, /device:TPU:0, one launch (start us, length us, event | category | flops | bytes accessed | tf_op | source)
XLA Modules:
  0.0 880.1 jit_solution(7205849105312256641)
XLA Ops:
  11.8 3.8 fusion.88
  15.7 5.3 all-gather
  23.7 35.0 %all-gather.6.cloned.1.call-done = bf16[1,1024,1024]{2,1,0:T(8,128)(2,1)} async-done(((bf16[1,512,1024]{2,1,0:T(8,128)(2,1)}), bf16[1,1024,1024]{2,1,0:T(8,128)(2,1)}) %all-gather.6.cloned.1.call-update) | async-done | bytes 2097168 | tf_op jit(solution)/shard_map/all_gather | solution.py:117
  58.7 5.3 convolution_convert_fusion.3
  65.8 2.6 squeeze.44
  68.4 2.4 copy.25
  70.8 25.3 %while.47 = (s32[]{:T(128)}, bf16[2,512,8,64]{1,3,2,0:T(8,128)(2,1)}, f32[2,8,512]{2,1,0:T(8,128)S(1)}, bf16[2,512,8,64]{1,3,2,0:T(8,128)(2,1)}, bf16[1024,8,64]...) while((s32[]{:T(128)}, bf16[2,512,8,64]{1,3,2,0:T(8,128)(2,1)}, f32[2,8,512]{2,1,0:T(8,128)S(1)}, ...), condition=%wide.region_5.6_spmd, body=%wide.region_2.5_spmd.sunk | while | flops 1111486464 | bytes 66715828 | solution.py:39
  70.8 3.8 multiply_reduce_fusion.5
  74.7 3.4 fusion.135
  78.2 4.3 fusion.136
  83.5 3.9 multiply_reduce_fusion.5
  87.3 3.4 fusion.135
  90.8 4.3 fusion.136
  99.8 2.6 convert_bitcast_fusion.2
  103.0 31.5 %reduce-scatter.6.cloned.1.call-done = bf16[1,512,1024]{2,1,0:T(8,128)(2,1)} async-done(((bf16[1,1024,1024]{2,1,0:T(8,128)(2,1)}), bf16[1,512,1024]{2,1,0:T(8,128)(2,1)}) %reduce-scatter.6.cloned.1.call-update) | async-done | bytes 1048592 | tf_op jit(solution)/shard_map/reduce_scatter | solution.py:129
  140.9 32.6 %all-gather.8.cloned.1.call-done = bf16[1,1024,1024]{2,1,0:T(8,128)(2,1)} async-done(((bf16[1,512,1024]{2,1,0:T(8,128)(2,1)}), bf16[1,1024,1024]{2,1,0:T(8,128)(2,1)}) %all-gather.8.cloned.1.call-update) | async-done | bytes 2097168 | tf_op jit(solution)/shard_map/all_gather | solution.py:137
  173.6 10.9 %fusion.66 = f32[1024,2048]{1,0:T(8,128)} fusion(bf16[1024,2048]{1,0:T(8,128)(2,1)} %param.19, bf16[1,1024,1024]{2,1,0:T(8,128)(2,1)} %all-gather.8.cloned.1.call-done), kind=kOutput, calls=%fused_computation.99 | convolution fusion | flops 4294967296 | bytes 14680064 | tf_op jit(solution)/shard_map/vwb,bj->vwj/dot_general | solution.py:140
  184.4 23.7 %all-gather.10.cloned.1.call-done = bf16[1,1024,1024]{2,1,0:T(8,128)(2,1)} async-done(((bf16[1,512,1024]{2,1,0:T(8,128)(2,1)}), bf16[1,1024,1024]{2,1,0:T(8,128)(2,1)}) %all-gather.10.cloned.1.call-update) | async-done | bytes 2097168 | tf_op jit(solution)/shard_map/all_gather | solution.py:138
  208.2 12.8 %fusion.40 = bf16[1024,2048]{1,0:T(8,128)(2,1)S(1)} fusion(f32[1024,2048]{1,0:T(8,128)} %fusion.66, bf16[2048,1024]{1,0:T(8,128)(2,1)} %param.20, bf16[1,1024,1024]{2,1,0:T(8,128)(2,1)} %all-gather.10.cloned.1.call-done, f32[1024]{0:T(1024)S(1)} %bitcast.199), kind=kOutput, calls=%fused_computation.51 | convolution fusion | flops 4340056064 | bytes 18878464 | tf_op jit(solution)/shard_map/euz,hz->euh/dot_general | solution.py:158
  223.0 5.7 convert_bitcast_fusion
  229.0 11.0 %convert_bitcast_fusion.1 = bf16[1,1024,1024]{2,1,0:T(8,128)(2,1)} fusion(bf16[2048,1024]{1,0:T(8,128)(2,1)} %param.20, f32[1024,2048]{1,0:T(8,128)} %fusion.66), kind=kOutput, calls=%fused_computation.106 | convolution fusion | flops 4314890240 | bytes 14680064 | tf_op jit(solution)/shard_map/ewy,yz->ewz/dot_general | solution.py:148
  240.0 20.7 %reduce-scatter.10.cloned.1.call-done = bf16[1,512,1024]{2,1,0:T(8,128)(2,1)} async-done(((bf16[1,1024,1024]{2,1,0:T(8,128)(2,1)}), bf16[1,512,1024]{2,1,0:T(8,128)(2,1)}) %reduce-scatter.10.cloned.1.call-update) | async-done | bytes 1048592 | tf_op jit(solution)/shard_map/reduce_scatter | solution.py:171
  260.7 2.7 fusion.51
  265.4 29.8 %reduce-scatter.8.cloned.1.call-done = bf16[1,512,1024]{2,1,0:T(8,128)(2,1)} async-done(((bf16[1,1024,1024]{2,1,0:T(8,128)(2,1)}), bf16[1,512,1024]{2,1,0:T(8,128)(2,1)}) %reduce-scatter.8.cloned.1.call-update) | async-done | bytes 1048592 | tf_op jit(solution)/shard_map/reduce_scatter | solution.py:151
  295.3 5.1 fusion.52
  303.0 33.2 %all-gather.12.cloned.1.call-done = bf16[1,1024,1024]{2,1,0:T(8,128)(2,1)} async-done(((bf16[1,512,1024]{2,1,0:T(8,128)(2,1)}), bf16[1,1024,1024]{2,1,0:T(8,128)(2,1)}) %all-gather.12.cloned.1.call-update) | async-done | bytes 2097168 | tf_op jit(solution)/shard_map/all_gather | solution.py:180
  336.2 4.1 fusion.78
  340.3 4.1 reshape.412
  344.4 3.3 copy.29
  347.7 88.8 %while.48 = (s32[]{:T(128)}, f32[1024,8,64]{0,2,1:T(8,128)}, f32[1024,8,64]{0,2,1:T(8,128)}, bf16[2,512,8,64]{1,3,2,0:T(8,128)(2,1)}, bf16[2,512,8,64]{1,3,2,0:T...) while((s32[]{:T(128)}, f32[1024,8,64]{0,2,1:T(8,128)}, ...), condition=%wide.region_15.16_spmd.clone, body=%wide.region_13.15_spmd.clone.sunk | while | flops 2737827840 | bytes 261734864 | solution.py:75
  347.7 3.9 fusion.146
  351.7 5.7 copy-done.1
  357.4 3.9 bitcast_add_fusion.6
  361.3 12.5 %multiply_reduce_fusion.6 = (f32[8,512]{1,0:T(8,128)S(1)}, f32[8,512,1024]{2,1,0:T(8,128)}) fusion(f32[8,512,1024]{2,1,0:T(8,128)} %copy-done.1, f32[8,512]{1,0:T(8,128)S(1)} %dynamic-slice_bitcast_fusion.2, bf16[1024,8,64]{0,2,1:T(8,128)(2,1)} %get-tuple-element.392, bf16[2,512,8,64]{1,3,2,0:T(8,128)(2,1)S(1)} %copy-done.11, s32[]{:T(128)S(6)} %copy.64), kind=kOutput, calls=%fused_computation.14.clone.1 | convolution fusion | flops 553644032 | bytes 35160068 | tf_op jit(solution)/shard_map/while/body/eval_jaxpr/while/body/eval_jaxpr/qhd,khd->hqk/dot_general | solution.py:57
  373.8 12.5 %multiply_convert_fusion.8 = bf16[8,512,1024]{2,1,0:T(8,128)(2,1)S(1)} fusion(f32[8,512,1024]{2,1,0:T(8,128)} %get-tuple-element.339, f32[8,512,1024]{2,1,0:T(8,128)} %copy-done.1, f32[8,512]{1,0:T(8,128)S(1)} %get-tuple-element.340, f32[8,512]{1,0:T(8,128)S(1)} %dynamic-slice_bitcast_fusion.2), kind=kLoop, calls=%fused_computation.13.clone.1 | loop fusion | flops 20971520 | bytes 41975808 | tf_op jit(solution)/shard_map/while/body/eval_jaxpr/while/body/eval_jaxpr/convert_element_type | solution.py:59
  386.3 2.7 fusion.147
  392.1 3.9 fusion.146
  396.0 5.7 copy-done.1
  401.8 3.9 bitcast_add_fusion.6
  405.7 12.5 %multiply_reduce_fusion.6 = (f32[8,512]{1,0:T(8,128)S(1)}, f32[8,512,1024]{2,1,0:T(8,128)}) fusion(f32[8,512,1024]{2,1,0:T(8,128)} %copy-done.1, f32[8,512]{1,0:T(8,128)S(1)} %dynamic-slice_bitcast_fusion.2, bf16[1024,8,64]{0,2,1:T(8,128)(2,1)} %get-tuple-element.392, bf16[2,512,8,64]{1,3,2,0:T(8,128)(2,1)S(1)} %copy-done.11, s32[]{:T(128)S(6)} %copy.64), kind=kOutput, calls=%fused_computation.14.clone.1 | convolution fusion | flops 553644032 | bytes 35160068 | tf_op jit(solution)/shard_map/while/body/eval_jaxpr/while/body/eval_jaxpr/qhd,khd->hqk/dot_general | solution.py:57
  418.1 12.5 %multiply_convert_fusion.8 = bf16[8,512,1024]{2,1,0:T(8,128)(2,1)S(1)} fusion(f32[8,512,1024]{2,1,0:T(8,128)} %get-tuple-element.339, f32[8,512,1024]{2,1,0:T(8,128)} %copy-done.1, f32[8,512]{1,0:T(8,128)S(1)} %get-tuple-element.340, f32[8,512]{1,0:T(8,128)S(1)} %dynamic-slice_bitcast_fusion.2), kind=kLoop, calls=%fused_computation.13.clone.1 | loop fusion | flops 20971520 | bytes 41975808 | tf_op jit(solution)/shard_map/while/body/eval_jaxpr/while/body/eval_jaxpr/convert_element_type | solution.py:59
  430.7 2.7 fusion.147
  436.5 3.5 copy.41
  440.0 4.1 reshape.413
  444.1 2.7 convert_element_type.189
  449.1 2.7 convert_element_type.190
  454.1 6.6 fusion.75
  461.2 9.6 %convolution_convert_fusion.1 = bf16[1024,2048]{1,0:T(8,128)(2,1)} fusion(bf16[1024,2048]{1,0:T(8,128)(2,1)} %copy-done.50, bf16[1,1024,1024]{2,1,0:T(8,128)(2,1)} %all-gather.8.cloned.1.call-done), kind=kOutput, calls=%fused_computation.56 | convolution fusion | flops 4297064448 | bytes 10485760 | tf_op jit(solution)/shard_map/pae,paz->ez/dot_general | solution.py:162
  470.8 11.5 %convolution_convert_fusion = bf16[2048,1024]{1,0:T(8,128)(2,1)} fusion(bf16[1,1024,1024]{2,1,0:T(8,128)(2,1)S(1)} %copy-done.48, f32[1024]{0:T(1024)S(1)} %bitcast.201, f32[1024,2048]{1,0:T(8,128)} %fusion.66), kind=kOutput, calls=%fused_computation.55 | convolution fusion | flops 4319084544 | bytes 14684160 | tf_op jit(solution)/shard_map/noi,nok->ik/dot_general | solution.py:155
  483.9 7.8 convolution_convert_fusion.2
  496.2 2.7 fusion.57
  499.7 4.2 fusion.81
  503.8 5.7 reduce-scatter.14.cloned.1.call-done
  510.3 4.7 multiply_convert_fusion.1
  515.0 3.9 add_convert_fusion
  518.9 35.6 %psum.51 = bf16[6,512]{1,0:T(8,128)(2,1)S(1)} all-reduce(bf16[6,512]{1,0:T(8,128)(2,1)S(1)} %bitcast.196), channel_id=1, replica_groups=mesh['dp'=16,'tensor'=2] {'dp'}, use_global_device_ids=true, to_apply=%region_28.29 | all-reduce | flops 3072 | bytes 12288 | tf_op jit(solution)/shard_map/psum | solution.py:241
  555.1 4.6 convolution_bitcast_fusion
  559.7 4.9 psum.49
  565.2 283.0 %all-reduce.3.cloned.1.call-done = (bf16[1024,6,512]{2,0,1:T(8,128)(2,1)}, bf16[1024,3,512]{2,0,1:T(8,128)(2,1)}, bf16[512,1024]{1,0:T(8,128)(2,1)}, bf16[1024,2048]{1,0:T(8,128)(2,1)}, bf16[2048,1024]{1,0:T(8,128)(2,1)}) async-done(((bf16[1024,6,512]{2,0,1:T(8,128)(2,1)}, bf16[1024,3,512]{2,0,1:T(8,128)(2,1)}, bf16[512,1024]{1,0:T(8,128)(2,1)}, bf16[1024,2048]{1,0:T(8,128)(2,1)}, ...) | async-done | bytes 18874384 | tf_op jit(solution)/shard_map/psum | solution.py:240
  848.3 2.8 convert_element_type.201
  851.1 9.5 %convert_element_type.196 = f32[1024,6,512]{2,0,1:T(8,128)} convert(bf16[1024,6,512]{2,0,1:T(8,128)(2,1)} %get-tuple-element.217) | non-fusion elementwise | flops 3145728 | bytes 18874368 | tf_op jit(solution)/shard_map/convert_element_type | solution.py:240
  860.5 3.6 convert_element_type.199
  864.2 4.4 convert_element_type.203
  868.6 4.4 convert_element_type.205
  (196 shorter events, 48.4 us)
Async XLA Ops:
  7.2 51.5 %copy-start = (bf16[1024,3,512]{2,0,1:T(8,128)(2,1)S(1)}, bf16[1024,3,512]{2,0,1:T(8,128)(2,1)}, u32[]{:S(2)}) copy-start(bf16[1024,3,512]{2,0,1:T(8,128)(2,1)} %param.17) | copy-start | bytes 9437188
  7.2 51.5 %all-gather.6.cloned.1.call-start = ((), (), s32[]{:S(2)}) async-start(), calls=%async_computation.5 | async-start | bytes 3145728 | tf_op jit(solution)/shard_map/all_gather | solution.py:117
  8.8 12.8 %copy-start.30 = (f32[512]{0:T(512)}, f32[512]{0:T(512)S(1)}, u32[]{:S(2)}) copy-start(f32[512]{0:T(512)S(1)} %broadcast_multiply_fusion.1) | copy-start | bytes 6148
  10.5 11.1 %copy-start.35 = (f32[512]{0:T(512)}, f32[512]{0:T(512)S(1)}, u32[]{:S(2)}) copy-start(f32[512]{0:T(512)S(1)} %fusion.91) | copy-start | bytes 6148
  11.8 3.8 copy-start.33
  11.8 3.8 copy-start.42
  11.8 10.3 %copy-start.5 = (bf16[1,512,1024]{2,1,0:T(8,128)(2,1)S(1)}, bf16[1,512,1024]{2,1,0:T(8,128)(2,1)}, u32[]{:S(2)}) copy-start(bf16[1,512,1024]{2,1,0:T(8,128)(2,1)} %param.13) | copy-start | bytes 3145732
  23.6 110.8 %reduce-scatter.6.cloned.1.call-start = ((), (), s32[]{:S(2)}) async-start(), calls=%async_computation.6 | async-start | bytes 3145728 | tf_op jit(solution)/shard_map/reduce_scatter | solution.py:129
  74.7 3.5 copy-start.12
  74.7 3.5 copy-start.23
  87.3 3.5 copy-start.12
  87.3 3.5 copy-start.23
  96.1 3.6 copy-start.49
  99.8 34.6 %copy-start.25 = (f32[1,1,1024]{2,1,0:T(1,128)S(1)}, f32[1,1,1024]{2,1,0:T(1,128)}, u32[]{:S(2)}) copy-start(f32[1,1,1024]{2,1,0:T(1,128)} %get-tuple-element.240) | copy-start | bytes 12292
  102.4 36.2 %copy-start.26 = (f32[1,1,1024]{2,1,0:T(1,128)S(1)}, f32[1,1,1024]{2,1,0:T(1,128)}, u32[]{:S(2)}) copy-start(f32[1,1,1024]{2,1,0:T(1,128)} %get-tuple-element.237) | copy-start | bytes 12292
  102.4 36.2 %copy-start.41 = (f32[1,1,1024]{2,1,0:T(1,128)S(1)}, f32[1,1,1024]{2,1,0:T(1,128)}, u32[]{:S(2)}) copy-start(f32[1,1,1024]{2,1,0:T(1,128)} %get-tuple-element.236) | copy-start | bytes 12292
  102.4 71.1 %all-gather.8.cloned.1.call-start = ((), (), s32[]{:S(2)}) async-start(), calls=%async_computation.7 | async-start | bytes 3145728 | tf_op jit(solution)/shard_map/all_gather | solution.py:137
  134.4 4.3 copy-start.6
  134.4 4.3 copy-start.13
  140.3 67.9 %all-gather.10.cloned.1.call-start = ((), (), s32[]{:S(2)}) async-start(), calls=%async_computation.9 | async-start | bytes 3145728 | tf_op jit(solution)/shard_map/all_gather | solution.py:138
  140.9 67.3 %copy-start.39 = (f32[1,1,1024]{2,1,0:T(1,128)S(1)}, f32[1,1,1024]{2,1,0:T(1,128)}, u32[]{:S(2)}) copy-start(f32[1,1,1024]{2,1,0:T(1,128)} %get-tuple-element.235) | copy-start | bytes 12292
  140.9 119.9 %reduce-scatter.10.cloned.1.call-start = ((), (), s32[]{:S(2)}) async-start(), calls=%async_computation.10 | async-start | bytes 3145728 | tf_op jit(solution)/shard_map/reduce_scatter | solution.py:171
  208.2 14.8 %copy-start.47 = (bf16[1024,2048]{1,0:T(8,128)(2,1)S(1)}, bf16[1024,2048]{1,0:T(8,128)(2,1)}, u32[]{:S(2)}) copy-start(bf16[1024,2048]{1,0:T(8,128)(2,1)} %param.19) | copy-start | bytes 12582916
  221.0 2.0 copy-start.50
  228.7 66.5 %reduce-scatter.8.cloned.1.call-start = ((), (), s32[]{:S(2)}) async-start(), calls=%async_computation.8 | async-start | bytes 3145728 | tf_op jit(solution)/shard_map/reduce_scatter | solution.py:151
  240.0 96.2 %all-gather.12.cloned.1.call-start = ((), (), s32[]{:S(2)}) async-start(), calls=%async_computation.11 | async-start | bytes 3145728 | tf_op jit(solution)/shard_map/all_gather | solution.py:180
  260.7 2.7 copy-start.7
  260.7 2.7 copy-start.14
  260.7 2.8 copy-start.16
  303.0 189.7 %reduce-scatter.12.cloned.1.call-start = ((), (), s32[]{:S(2)}) async-start(), calls=%async_computation.12 | async-start | bytes 3145728 | tf_op jit(solution)/shard_map/reduce_scatter | solution.py:211
  347.7 9.7 %copy-start.9 = (f32[1024,8,64]{0,2,1:T(8,128)S(1)}, f32[1024,8,64]{0,2,1:T(8,128)}, u32[]{:S(2)}) copy-start(f32[1024,8,64]{0,2,1:T(8,128)} %get-tuple-element.375) | copy-start | bytes 6291460 | tf_op jit(solution)/shard_map/while/body/eval_jaxpr/while
  347.7 9.7 %copy-start.11 = (bf16[2,512,8,64]{1,3,2,0:T(8,128)(2,1)S(1)}, bf16[2,512,8,64]{1,3,2,0:T(8,128)(2,1)}, u32[]{:S(2)}) copy-start(bf16[2,512,8,64]{1,3,2,0:T(8,128)(2,1)} %get-tuple-element.391) | copy-start | bytes 3145732 | tf_op jit(solution)/shard_map/while/body/eval_jaxpr/while
  351.6 5.7 copy-start.1
  361.3 12.5 %copy-start.10 = (f32[1024,8,64]{0,2,1:T(8,128)}, f32[1024,8,64]{0,2,1:T(8,128)S(1)}, u32[]{:S(2)}) copy-start(f32[1024,8,64]{0,2,1:T(8,128)S(1)} %bitcast_add_fusion.6) | copy-start | bytes 6291460 | tf_op jit(solution)/shard_map/while/body/eval_jaxpr/while
  373.8 12.5 %copy-start.2 = (bf16[1024,8,64]{0,2,1:T(8,128)(2,1)S(1)}, bf16[1024,8,64]{0,2,1:T(8,128)(2,1)}, u32[]{:S(2)}) copy-start(bf16[1024,8,64]{0,2,1:T(8,128)(2,1)} %get-tuple-element.389) | copy-start | bytes 3145732 | tf_op jit(solution)/shard_map/while/body/eval_jaxpr/while
  373.8 12.5 %copy-start.20 = (bf16[2,512,8,64]{1,3,2,0:T(8,128)(2,1)S(1)}, bf16[2,512,8,64]{1,3,2,0:T(8,128)(2,1)}, u32[]{:S(2)}) copy-start(bf16[2,512,8,64]{1,3,2,0:T(8,128)(2,1)} %get-tuple-element.376) | copy-start | bytes 3145732 | tf_op jit(solution)/shard_map/while/body/eval_jaxpr/while
  386.3 2.7 copy-start.3
  386.3 2.7 copy-start.8
  392.1 9.7 %copy-start.9 = (f32[1024,8,64]{0,2,1:T(8,128)S(1)}, f32[1024,8,64]{0,2,1:T(8,128)}, u32[]{:S(2)}) copy-start(f32[1024,8,64]{0,2,1:T(8,128)} %get-tuple-element.375) | copy-start | bytes 6291460 | tf_op jit(solution)/shard_map/while/body/eval_jaxpr/while
  392.1 9.7 %copy-start.11 = (bf16[2,512,8,64]{1,3,2,0:T(8,128)(2,1)S(1)}, bf16[2,512,8,64]{1,3,2,0:T(8,128)(2,1)}, u32[]{:S(2)}) copy-start(bf16[2,512,8,64]{1,3,2,0:T(8,128)(2,1)} %get-tuple-element.391) | copy-start | bytes 3145732 | tf_op jit(solution)/shard_map/while/body/eval_jaxpr/while
  396.0 5.7 copy-start.1
  405.7 12.5 %copy-start.10 = (f32[1024,8,64]{0,2,1:T(8,128)}, f32[1024,8,64]{0,2,1:T(8,128)S(1)}, u32[]{:S(2)}) copy-start(f32[1024,8,64]{0,2,1:T(8,128)S(1)} %bitcast_add_fusion.6) | copy-start | bytes 6291460 | tf_op jit(solution)/shard_map/while/body/eval_jaxpr/while
  418.1 12.5 %copy-start.2 = (bf16[1024,8,64]{0,2,1:T(8,128)(2,1)S(1)}, bf16[1024,8,64]{0,2,1:T(8,128)(2,1)}, u32[]{:S(2)}) copy-start(bf16[1024,8,64]{0,2,1:T(8,128)(2,1)} %get-tuple-element.389) | copy-start | bytes 3145732 | tf_op jit(solution)/shard_map/while/body/eval_jaxpr/while
  418.1 12.5 %copy-start.20 = (bf16[2,512,8,64]{1,3,2,0:T(8,128)(2,1)S(1)}, bf16[2,512,8,64]{1,3,2,0:T(8,128)(2,1)}, u32[]{:S(2)}) copy-start(bf16[2,512,8,64]{1,3,2,0:T(8,128)(2,1)} %get-tuple-element.376) | copy-start | bytes 3145732 | tf_op jit(solution)/shard_map/while/body/eval_jaxpr/while
  430.7 2.7 copy-start.3
  430.7 2.7 copy-start.8
  454.1 7.1 copy-start.45
  460.7 48.9 %reduce-scatter.14.cloned.1.call-start = ((), (), s32[]{:S(2)}) async-start(), calls=%async_computation.13 | async-start | bytes 24576 | tf_op jit(solution)/shard_map/reduce_scatter | solution.py:227
  461.2 9.6 %copy-start.40 = (f32[1,1,1024]{2,1,0:T(1,128)S(1)}, f32[1,1,1024]{2,1,0:T(1,128)}, u32[]{:S(2)}) copy-start(f32[1,1,1024]{2,1,0:T(1,128)} %get-tuple-element.235) | copy-start | bytes 12292
  461.2 9.6 %copy-start.48 = (bf16[1,1024,1024]{2,1,0:T(8,128)(2,1)S(1)}, bf16[1,1024,1024]{2,1,0:T(8,128)(2,1)}, u32[]{:S(2)}) copy-start(bf16[1,1024,1024]{2,1,0:T(8,128)(2,1)} %all-gather.10.cloned.1.call-done) | copy-start | bytes 6291460
  470.8 13.0 %copy-start.46 = (bf16[1024]{0:T(1024)(128)(2,1)S(1)}, bf16[1024]{0:T(1024)(128)(2,1)}, u32[]{:S(2)}) copy-start(bf16[1024]{0:T(1024)(128)(2,1)} %get-tuple-element.183) | copy-start | bytes 6148
  470.8 13.0 %copy-start.44 = (bf16[1024]{0:T(1024)(128)(2,1)S(1)}, bf16[1024]{0:T(1024)(128)(2,1)}, u32[]{:S(2)}) copy-start(bf16[1024]{0:T(1024)(128)(2,1)} %get-tuple-element.224) | copy-start | bytes 6148
  470.8 13.0 %copy-start.43 = (bf16[1024]{0:T(1024)(128)(2,1)S(1)}, bf16[1024]{0:T(1024)(128)(2,1)}, u32[]{:S(2)}) copy-start(bf16[1024]{0:T(1024)(128)(2,1)} %get-tuple-element.234) | copy-start | bytes 6148
  483.8 8.8 %copy-start.28 = (f32[1,1,1024]{2,1,0:T(1,128)S(1)}, f32[1,1,1024]{2,1,0:T(1,128)}, u32[]{:S(2)}) copy-start(f32[1,1,1024]{2,1,0:T(1,128)} %copy-done.27) | copy-start | bytes 12292
  483.8 8.8 %copy-start.31 = (f32[512]{0:T(512)S(1)}, f32[512]{0:T(512)}, u32[]{:S(2)}) copy-start(f32[512]{0:T(512)} %copy-done.30) | copy-start | bytes 6148
  483.9 10.9 %copy-start.38 = (f32[512]{0:T(512)S(1)}, f32[512]{0:T(512)}, u32[]{:S(2)}) copy-start(f32[512]{0:T(512)} %copy-done.37) | copy-start | bytes 6148
  491.7 4.5 copy-start.36
  499.6 348.7 %all-reduce.3.cloned.1.call-start = ((), (), s32[]{:S(2)}) async-start(), calls=%async_computation.14 | async-start | bytes 37748736 | tf_op jit(solution)/shard_map/psum | solution.py:240
  515.0 3.9 copy-start.29
  555.1 9.5 %copy-start.32 = (bf16[1,1024]{1,0:T(2,128)(2,1)S(1)}, bf16[1,1024]{1,0:T(2,128)(2,1)}, u32[]{:S(2)}) copy-start(bf16[1,1024]{1,0:T(2,128)(2,1)} %param.14) | copy-start | bytes 6148
  555.1 9.5 %copy-start.34 = (f32[1,1024]{1,0:T(1,128)S(1)}, f32[1,1024]{1,0:T(1,128)}, u32[]{:S(2)}) copy-start(f32[1,1024]{1,0:T(1,128)} %copy-done.33) | copy-start | bytes 12292
  851.1 9.5 %copy-start.19 = (bf16[1024,3,512]{2,0,1:T(8,128)(2,1)S(1)}, bf16[1024,3,512]{2,0,1:T(8,128)(2,1)}, u32[]{:S(2)}) copy-start(bf16[1024,3,512]{2,0,1:T(8,128)(2,1)} %get-tuple-element.218) | copy-start | bytes 9437188
  860.5 3.6 copy-start.18
  864.2 4.5 copy-start.17
  (10 other events, 12.4 us)
Sparse Core Ops, SparseCore 0:
  23.7 34.9 all-gather.5
  102.6 31.8 reduce-scatter.5
  140.4 33.1 all-gather.7
  175.0 33.1 all-gather.9
  228.9 31.8 reduce-scatter.9
  263.4 31.8 reduce-scatter.7
  303.1 33.0 all-gather.11
  460.8 31.8 reduce-scatter.11
  499.7 9.7 reduce-scatter.13
  515.5 332.7 all-reduce.2
where the time goes:
time: 889 us; the launch traced here: 880 us
  waiting for transfers between devices  497 us (56%)
  matrix products  166 us (19%)
  other arithmetic  104 us (12%)
  local copies, waits for them, and re-layouts  50.7 us (6%)
  blocking collectives  45.8 us (5%)
  between operations  14.8 us (2%)
    psum x1, waiting for transfers between devices, body(): lax.psum(grad_mod_weight.astype(jnp.bfloat16), 'dp').astype(jnp.float32)  283 us
    psum x1, blocking collectives, body(): lax.psum(grad_mod_bias.astype(jnp.bfloat16), 'dp').astype(jnp.float32)  35.6 us
    all_gather x1, waiting for transfers between devices, body(): normed_all = lax.all_gather(normed_one, 'tensor', axis=1, tiled=True)  35 us
    all_gather x1, waiting for transfers between devices, body(): grad_attn_all = lax.all_gather(grad_attn, 'tensor', axis=1, tiled=True)  33.2 us
    all_gather x1, waiting for transfers between devices, body(): lax.all_gather(normed_two, 'tensor', axis=1, tiled=True)  32.6 us
    reduce_scatter x1, waiting for transfers between devices, body(): lax.psum_scatter(attn_terms.astype(jnp.bfloat16), 'tensor', scatter_dimen...  31.5 us
    reduce_scatter x1, waiting for transfers between devices, body(): lax.psum_scatter(mlp_terms.astype(jnp.bfloat16), 'tensor', scatter_dimens...  29.8 us
    convert_element_type x2, other arithmetic, one_block(): grad_scores = (shares * (grad_shares - inner_sum)).astype(jnp.bfloat16)  25 us
  transfers between devices with their start and end apart: 10, of which 10 were waited for; matrix products, arithmetic and copies ran while one was open for 8% of the time, Pallas kernels for 0%

commit v1 on v0

--- a/solution.py
+++ b/solution.py
@@ -1,6 +1,8 @@
 import jax
 import jax.numpy as jnp
 from jax import lax
+from jax.experimental import pallas as pl
+from jax.experimental.pallas import tpu as pltpu
 from jax.sharding import PartitionSpec as P
 
 HD = 64
@@ -80,7 +82,7 @@
     )
 
 
-def body(
+def body_general(
     inputs,
     conditioning,
     mod_weight,
@@ -256,6 +258,290 @@
         summed[5],
     )
 
+LOG2E = 1.4426950408889634
+ATT_ROWS = 512
+
+
+def attn_fwd_kernel(qkv_ref, out_ref, lse_ref):
+    length = qkv_ref.shape[1]
+    fold = LOG2E * HD ** (-0.5)
+    for head in range(2):
+        cols = pl.ds(head * HD, HD)
+        keys = qkv_ref[1, :, cols]
+        values = qkv_ref[2, :, cols]
+        for start in range(0, length, ATT_ROWS):
+            rows = pl.ds(start, ATT_ROWS)
+            query = qkv_ref[0, rows, cols]
+            scores = lax.dot_general(
+                query, keys, (((1,), (1,)), ((), ())), preferred_element_type=jnp.float32
+            )
+            peak = jnp.max(scores, axis=-1, keepdims=True)
+            exponent = jnp.exp2((scores - peak) * fold)
+            total = jnp.sum(exponent, axis=-1, keepdims=True)
+            shares = (exponent * (1.0 / total)).astype(jnp.bfloat16)
+            result = jnp.dot(shares, values, preferred_element_type=jnp.float32)
+            out_ref[rows, cols] = result.astype(jnp.bfloat16)
+            log_total = peak * fold + jnp.log2(total)
+            flat = jnp.transpose(jnp.broadcast_to(log_total, (ATT_ROWS, 128)))
+            lse_ref[0, head : head + 1, rows] = flat[0:1]
+
+
+def attn_bwd_kernel(qkv_ref, grad_ref, lse_ref, out_ref):
+    length = qkv_ref.shape[1]
+    scale = HD ** (-0.5)
+    fold = LOG2E * scale
+    for head in range(2):
+        cols = pl.ds(head * HD, HD)
+        query = qkv_ref[0, :, cols]
+        grad = grad_ref[:, cols]
+        lse = lse_ref[0, head : head + 1, :]
+        keys = qkv_ref[1, :, cols]
+        values = qkv_ref[2, :, cols]
+        dk = jnp.zeros((length, HD), jnp.float32)
+        dv = jnp.zeros((length, HD), jnp.float32)
+        for start in range(0, length, ATT_ROWS):
+            qblock = query[start : start + ATT_ROWS]
+            gblock = grad[start : start + ATT_ROWS]
+            scores = lax.dot_general(
+                keys, qblock, (((1,), (1,)), ((), ())), preferred_element_type=jnp.float32
+            )
+            probs = jnp.exp2(scores * fold - lse[:, start : start + ATT_ROWS])
+            dprobs = lax.dot_general(
+                values, gblock, (((1,), (1,)), ((), ())), preferred_element_type=jnp.float32
+            )
+            inner = jnp.sum(probs * dprobs, axis=0, keepdims=True)
+            dscores = (probs * (dprobs - inner)).astype(jnp.bfloat16)
+            dv = dv + jnp.dot(probs.astype(jnp.bfloat16), gblock, preferred_element_type=jnp.float32)
+            dk = dk + jnp.dot(dscores, qblock, preferred_element_type=jnp.float32)
+            dq = lax.dot_general(
+                dscores, keys, (((0,), (0,)), ((), ())), preferred_element_type=jnp.float32
+            )
+            out_ref[0, pl.ds(start, ATT_ROWS), cols] = (dq * scale).astype(jnp.bfloat16)
+        out_ref[1, :, cols] = (dk * scale).astype(jnp.bfloat16)
+        out_ref[2, :, cols] = dv.astype(jnp.bfloat16)
+
+
+def attn_forward(qkv, first, pairs):
+    _, length, _ = qkv.shape
+    return pl.pallas_call(
+        attn_fwd_kernel,
+        grid=(pairs,),
+        in_specs=[pl.BlockSpec((3, length, 2 * HD), lambda i: (0, 0, first + i))],
+        out_specs=[
+            pl.BlockSpec((length, 2 * HD), lambda i: (0, i)),
+            pl.BlockSpec((1, 8, length), lambda i: (i, 0, 0)),
+        ],
+        out_shape=[
+            jax.ShapeDtypeStruct((length, pairs * 2 * HD), jnp.bfloat16),
+            jax.ShapeDtypeStruct((pairs, 8, length), jnp.float32),
+        ],
+        compiler_params=pltpu.CompilerParams(vmem_limit_bytes=48 * 1024 * 1024),
+        cost_estimate=pl.CostEstimate(
+            flops=pairs * 2 * 4 * length * length * HD * 4,
+            bytes_accessed=pairs * 8 * length * 2 * HD,
+            transcendentals=pairs * 2 * length * length,
+        ),
+        name="attn_fwd",
+    )(qkv)
+
+
+def attn_backward(qkv, grad, lse):
+    _, length, local = qkv.shape
+    pairs = local // (2 * HD)
+    return pl.pallas_call(
+        attn_bwd_kernel,
+        grid=(pairs,),
+        in_specs=[
+            pl.BlockSpec((3, length, 2 * HD), lambda i: (0, 0, i)),
+            pl.BlockSpec((length, 2 * HD), lambda i: (0, i)),
+            pl.BlockSpec((1, 8, length), lambda i: (i, 0, 0)),
+        ],
+        out_specs=pl.BlockSpec((3, length, 2 * HD), lambda i: (0, 0, i)),
+        out_shape=jax.ShapeDtypeStruct((3, length, local), jnp.bfloat16),
+        compiler_params=pltpu.CompilerParams(vmem_limit_bytes=48 * 1024 * 1024),
+        cost_estimate=pl.CostEstimate(
+            flops=pairs * 2 * 10 * length * length * HD * 4,
+            bytes_accessed=pairs * 14 * length * 2 * HD,
+            transcendentals=pairs * 2 * length * length,
+        ),
+        name="attn_bwd",
+    )(qkv, grad, lse)
+
+
+def swap(values_in):
+    return lax.ppermute(values_in, "tensor", ((0, 1), (1, 0)))
+
+
+def dot_f32(left, right, dims):
+    return lax.dot_general(left, right, (dims, ((), ())), preferred_element_type=jnp.float32)
+
+
+NN = ((1,), (0,))
+NT = ((1,), (1,))
+TN = ((0,), (0,))
+
+
+def body_pair(
+    inputs,
+    conditioning,
+    mod_weight,
+    mod_bias,
+    qkv_weight,
+    out_weight,
+    up_projection_weight,
+    down_projection_weight,
+    cotangent,
+):
+    bf16 = jnp.bfloat16
+    mine = lax.axis_index("tensor")
+    x_own = inputs[0]
+    half, width = x_own.shape
+    local_cols = qkv_weight.shape[2]
+    pairs = local_cols // (2 * HD)
+    x_peer = swap(x_own)
+    cond_silu, back_silu = jax.vjp(jax.nn.silu, conditioning.astype(jnp.float32))
+    cond_act = cond_silu.astype(bf16)
+    mod_own = (
+        jnp.einsum("ld,dkc->lkc", cond_act, mod_weight, preferred_element_type=jnp.float32)
+        + mod_bias[None]
+    )[0]
+    mod_peer = swap(mod_own)
+    modulation = jnp.where(
+        mine == 0,
+        jnp.concatenate((mod_own, mod_peer), axis=1),
+        jnp.concatenate((mod_peer, mod_own), axis=1),
+    )
+    shift_one, scale_one, gate_one, shift_two, scale_two, gate_two = (
+        modulation[k : k + 1] for k in range(6)
+    )
+    xf_own = x_own.astype(jnp.float32)
+    normed_own_f, back_one = jax.vjp(modulate, xf_own, shift_one, scale_one)
+    normed_own = normed_own_f.astype(bf16)
+    cot_later, out_later, x_peer = lax.optimization_barrier((cotangent[0], out_weight, x_peer))
+    cot_peer = swap(cot_later)
+    out_peer = swap(out_later)
+    xf_peer = x_peer.astype(jnp.float32)
+    normed_peer = modulate(xf_peer, shift_one, scale_one).astype(bf16)
+    normed_one = jnp.concatenate((normed_own, normed_peer), axis=0)
+    qkv = jnp.einsum(
+        "sd,dkc->ksc", normed_one, qkv_weight, preferred_element_type=jnp.float32
+    ).astype(bf16)
+    att_a, lse_a = attn_forward(qkv, 0, pairs // 2)
+    far_a = swap(att_a)
+    att_b, lse_b = attn_forward(qkv, pairs // 2, pairs - pairs // 2)
+    far_b = swap(att_b)
+    lse = jnp.concatenate((lse_a, lse_b), axis=0)
+    attended = jnp.concatenate((att_a, att_b), axis=1)
+    far = jnp.concatenate((far_a, far_b), axis=1)
+    both = jnp.concatenate(
+        (attended, jnp.concatenate((far[half:], far[:half]), axis=0)), axis=1
+    )
+    branch_attn = dot_f32(both, jnp.concatenate((out_weight, out_peer), axis=0), NN)
+    branch_own = branch_attn[:half]
+    middle_own = xf_own + gate_one * branch_own
+    middle_peer = xf_peer + gate_one * branch_attn[half:]
+    normed_two_f, back_two = jax.vjp(modulate, middle_own, shift_two, scale_two)
+    normed_two = jnp.concatenate(
+        (normed_two_f.astype(bf16), modulate(middle_peer, shift_two, scale_two).astype(bf16)),
+        axis=0,
+    )
+    grad_out = cotangent[0].astype(jnp.float32)
+    grad_mlp = jnp.concatenate(
+        (
+            (gate_two * grad_out).astype(bf16),
+            (gate_two * cot_peer.astype(jnp.float32)).astype(bf16),
+        ),
+        axis=0,
+    )
+    hidden_pre = dot_f32(normed_two, up_projection_weight, NN)
+    hidden_f, back_gelu = jax.vjp(gelu_tanh, hidden_pre)
+    hidden_act = hidden_f.astype(bf16)
+    grad_act = dot_f32(grad_mlp, down_projection_weight, NT)
+    grad_pre = back_gelu(grad_act)[0].astype(bf16)
+    two_recv = swap(dot_f32(grad_pre[half:], up_projection_weight, NT).astype(bf16))
+    two_own = dot_f32(grad_pre[:half], up_projection_weight, NT)
+    grad_down = dot_f32(hidden_act, grad_mlp, TN).astype(bf16)
+    grad_up = dot_f32(normed_two, grad_pre, TN).astype(bf16)
+    grad_down, grad_up, two_recv = lax.optimization_barrier((grad_down, grad_up, two_recv))
+    sum_down, sum_up = lax.psum((grad_down, grad_up), "dp")
+    grad_normed_two = two_own + two_recv.astype(jnp.float32)
+    middle_back, grad_shift_two, grad_scale_two = back_two(grad_normed_two)
+    grad_middle = grad_out + middle_back
+    grad_gate_one = jnp.sum(grad_middle * branch_own, axis=0, keepdims=True)
+    ga_own = (gate_one * grad_middle).astype(bf16)
+    ga_peer = swap(ga_own)
+    mlp_far = dot_f32(hidden_act[half:], down_projection_weight, NN).astype(bf16)
+    mlp_own = dot_f32(hidden_act[:half], down_projection_weight, NN)
+    mlp_far, ga_peer = lax.optimization_barrier((mlp_far, ga_peer))
+    branch_mlp = mlp_own + swap(mlp_far).astype(jnp.float32)
+    grad_attn = jnp.concatenate((ga_own, ga_peer), axis=0)
+    grad_attended = dot_f32(grad_attn, out_weight, NT).astype(bf16)
+    grad_out_weight = dot_f32(attended, grad_attn, TN).astype(bf16)
+    grad_qkv = attn_backward(qkv, grad_attended, lse)
+    one_recv = swap(
+        jnp.einsum(
+            "ksc,dkc->sd", grad_qkv[:, half:], qkv_weight, preferred_element_type=jnp.float32
+        ).astype(bf16)
+    )
+    one_own = jnp.einsum(
+        "ksc,dkc->sd", grad_qkv[:, :half], qkv_weight, preferred_element_type=jnp.float32
+    )
+    grad_qkv_weight = jnp.einsum(
+        "sd,ksc->dkc", normed_one, grad_qkv, preferred_element_type=jnp.float32
+    ).astype(bf16)
+    grad_qkv_weight, grad_out_weight, sum_down, sum_up = lax.optimization_barrier(
+        (grad_qkv_weight, grad_out_weight, sum_down, sum_up)
+    )
+    sum_qkv, sum_out = lax.psum((grad_qkv_weight, grad_out_weight), "dp")
+    block_out = (middle_own + gate_two * branch_mlp).astype(bf16)
+    grad_gate_two = jnp.sum(grad_out * branch_mlp, axis=0, keepdims=True)
+    grad_normed_one = one_own + one_recv.astype(jnp.float32)
+    inputs_back, grad_shift_one, grad_scale_one = back_one(grad_normed_one)
+    grad_inputs = (grad_middle + inputs_back).astype(bf16)
+    mod_terms = jnp.concatenate(
+        (
+            grad_shift_one,
+            grad_scale_one,
+            grad_gate_one,
+            grad_shift_two,
+            grad_scale_two,
+            grad_gate_two,
+        ),
+        axis=0,
+    )
+    left, right = mod_terms[:, :local_cols], mod_terms[:, local_cols:]
+    mod_keep = jnp.where(mine == 0, left, right)
+    mod_send = jnp.where(mine == 0, right, left).astype(bf16)
+    grad_mod = (mod_keep + swap(mod_send).astype(jnp.float32)).astype(bf16)[None]
+    cond_all = lax.all_gather(cond_act, "dp", axis=0, tiled=True)
+    mod_all = lax.all_gather(grad_mod, "dp", axis=0, tiled=True)
+    grad_mod_weight = jnp.einsum(
+        "ld,lkc->dkc", cond_all, mod_all, preferred_element_type=jnp.float32
+    )
+    grad_mod_bias = jnp.sum(mod_all.astype(jnp.float32), axis=0)
+    cond_terms = jnp.einsum(
+        "lkc,dkc->ld", grad_mod, mod_weight, preferred_element_type=jnp.float32
+    )
+    grad_conditioning = back_silu(cond_terms + swap(cond_terms))[0]
+    return (
+        block_out[None],
+        grad_inputs[None],
+        grad_conditioning,
+        grad_mod_weight,
+        grad_mod_bias,
+        sum_qkv.astype(jnp.float32),
+        sum_out.astype(jnp.float32),
+        sum_up.astype(jnp.float32),
+        sum_down.astype(jnp.float32),
+    )
+
+
+def body(inputs, conditioning, mod_weight, mod_bias, qkv_weight, *rest):
+    fits = inputs.shape[1] % 256 == 0 and qkv_weight.shape[2] % (4 * HD) == 0
+    if lax.axis_size("tensor") == 2 and inputs.shape[0] == 1 and fits:
+        return body_pair(inputs, conditioning, mod_weight, mod_bias, qkv_weight, *rest)
+    return body_general(inputs, conditioning, mod_weight, mod_bias, qkv_weight, *rest)
+
 
 def solution(mesh):
     return jax.shard_map(

time: 889 us -> 477 us (0.54)
  waiting for transfers between devices: 497 us -> 207 us
  matrix products: 166 us -> 94.3 us
  other arithmetic: 104 us -> 47.6 us
  Pallas kernels: 0 us -> 45.9 us
  local copies, waits for them, and re-layouts: 50.7 us -> 9.42 us
  starting transfers between devices: 1.51 us -> 15.4 us
    psum x1 -> x2, waiting for transfers between devices: 283 us -> 134 us  [the longest x1 86.5 us: body_pair(): sum_down, sum_up = lax.psum((grad_down, grad_up), 'dp')]
    all_gather x4 -> x0, waiting for transfers between devices: 125 us -> none  [the longest x1 35 us: body(): normed_all = lax.all_gather(normed_one, 'tensor', axis=1, tiled=True)]
    reduce_scatter x5 -> x0, waiting for transfers between devices: 88.7 us -> none  [the longest x1 31.5 us: body(): lax.psum_scatter(attn_terms.astype(jnp.bfloat16), 'tensor', scatter_dimen...]
    ppermute x0 -> x12, waiting for transfers between devices: none -> 73.5 us  [swap(): return lax.ppermute(values_in, 'tensor', ((0, 1), (1, 0)))]
    dot_general x28 -> x18, matrix products: 166 us -> 94.3 us  [the longest x11 62.8 us: dot_f32(): lax.dot_general(left, right, (dims, ((), ())), preferred_element_type=jnp...]
    convert_element_type x16 -> x10, other arithmetic: 69.9 us -> 20.1 us  [the longest x1 4.45 us: body_pair(): sum_up.astype(jnp.float32)]
    pallas_call x0 -> x3, Pallas kernels: none -> 45.9 us  [the longest x1 29.4 us: attn_backward(): pl.pallas_call(attn_bwd_kernel, grid=(pairs,), in_specs=[pl.BlockSpec((3,...]
    psum x2 -> x0, blocking collectives: 40.5 us -> none  [the longest x1 35.6 us: body(): lax.psum(grad_mod_bias.astype(jnp.bfloat16), 'dp').astype(jnp.float32)]
  transfers between devices with their start and end apart: 10 -> 14, of which waited for: 10 -> 8; matrix products, arithmetic and copies ran while one was open for 8% -> 21% of each run, Pallas kernels for 0% -> 10%
where the time goes in v1:
time: 477 us; the launch traced here: 473 us
  waiting for transfers between devices  207 us (43%)
  matrix products  94.3 us (20%)
  other arithmetic  47.6 us (10%)
  Pallas kernels  45.9 us (10%)
  blocking collectives  38.6 us (8%)
  starting transfers between devices  15.4 us (3%)
  between operations  14.9 us (3%)
  local copies, waits for them, and re-layouts  9.42 us (2%)
    psum x1, waiting for transfers between devices, body_pair(): sum_down, sum_up = lax.psum((grad_down, grad_up), 'dp')  86.5 us
    ppermute x12, waiting for transfers between devices, swap(): return lax.ppermute(values_in, 'tensor', ((0, 1), (1, 0)))  73.5 us
    dot_general x11, matrix products, dot_f32(): lax.dot_general(left, right, (dims, ((), ())), preferred_element_type=jnp...  62.8 us
    psum x1, waiting for transfers between devices, body_pair(): sum_qkv, sum_out = lax.psum((grad_qkv_weight, grad_out_weight), 'dp')  47 us
    pallas_call x1, Pallas kernels, attn_backward(): pl.pallas_call(attn_bwd_kernel, grid=(pairs,), in_specs=[pl.BlockSpec((3,...  29.4 us
    all_gather x1, blocking collectives, body_pair(): cond_all = lax.all_gather(cond_act, 'dp', axis=0, tiled=True)  21 us
    all_gather x1, blocking collectives, body_pair(): mod_all = lax.all_gather(grad_mod, 'dp', axis=0, tiled=True)  17.6 us
    pallas_call x2, Pallas kernels, attn_forward(): pl.pallas_call(attn_fwd_kernel, grid=(pairs,), in_specs=[pl.BlockSpec((3,...  16.5 us
  transfers between devices with their start and end apart: 14, of which 8 were waited for; matrix products, arithmetic and copies ran while one was open for 21% of the time, Pallas kernels for 10%

profile of v1, /device:TPU:0, one launch (start us, length us, event | category | flops | bytes accessed | tf_op | source)
XLA Modules:
  0.0 473.2 jit_solution(15041758202235972784)
XLA Ops:
  7.2 1.5 convert_bitcast_fusion.1
  8.7 3.7 fusion.69
  12.4 3.0 collective-permute-start
  15.5 1.5 convert_reduce_fusion.1
  17.0 1.6 fusion.22
  18.7 21.7 %collective-permute-done.1 = bf16[512,1024]{1,0:T(8,128)(2,1)} collective-permute-done((bf16[512,1024]{1,0:T(8,128)(2,1)}, bf16[512,1024]{1,0:T(8,128)(2,1)}, u32[]{:S(2)}, u32[]{:S(2)}) %collective-permute-start.1) | collective-permute-done | bytes 1048608 | tf_op jit(solution)/shard_map/ppermute | solution.py:372
  40.4 1.4 convert_reduce_fusion
  41.8 1.6 fusion.18
  43.5 0.6 collective-permute-start.4
  44.1 2.4 fusion.16
  46.5 1.0 copy-done.17
  47.8 4.7 convert_bitcast_fusion.qkv_ref
  52.5 8.0 %attn_fwd.2 = (bf16[1024,256]{1,0:T(8,128)(2,1)S(1)}, f32[2,8,1024]{2,1,0:T(8,128)S(1)}) custom-call(bf16[3,1024,512]{2,1,0:T(8,128)(2,1)S(1)} %convert_bitcast_fusion.qkv_ref), custom_call_target="tpu_custom_call" | custom-call | flops 4294967296 | bytes 2097152 | tf_op jit(solution)/shard_map/attn_fwd/pallas_call | solution.py:326
  60.5 1.6 collective-permute-start.2
  62.1 8.5 %attn_fwd.3 = (bf16[1024,256]{1,0:T(8,128)(2,1)S(1)}, f32[2,8,1024]{2,1,0:T(8,128)S(1)}) custom-call(bf16[3,1024,512]{2,1,0:T(8,128)(2,1)S(1)} %convert_bitcast_fusion.qkv_ref), custom_call_target="tpu_custom_call" | custom-call | flops 4294967296 | bytes 2097152 | tf_op jit(solution)/shard_map/attn_fwd/pallas_call | solution.py:326
  70.6 0.6 collective-permute-start.3
  71.2 1.5 collective-permute-start.5
  72.7 8.2 %collective-permute-done.2 = bf16[1024,256]{1,0:T(8,128)(2,1)S(1)} collective-permute-done((bf16[1024,256]{1,0:T(8,128)(2,1)S(1)}, bf16[1024,256]{1,0:T(8,128)(2,1)S(1)}, u32[]{:S(2)}, u32[]{:S(2)}) %collective-permute-start.2) | collective-permute-done | bytes 524320 | tf_op jit(solution)/shard_map/ppermute | solution.py:372
  80.9 11.2 %collective-permute-done.3 = bf16[1024,256]{1,0:T(8,128)(2,1)S(1)} collective-permute-done((bf16[1024,256]{1,0:T(8,128)(2,1)S(1)}, bf16[1024,256]{1,0:T(8,128)(2,1)S(1)}, u32[]{:S(2)}, u32[]{:S(2)}) %collective-permute-start.3) | collective-permute-done | bytes 524320 | tf_op jit(solution)/shard_map/ppermute | solution.py:372
  92.3 2.3 fusion.34
  94.6 2.4 fusion.60
  97.0 1.7 multiply_reduce_fusion.3
  98.7 2.4 fusion.85
  102.5 1.6 copy-done.26
  104.1 9.1 %multiply_convert_fusion = (bf16[1024,2048]{1,0:T(8,128)(2,1)S(1)}, f32[1024,2048]{1,0:T(8,128)}) fusion(bf16[1024,2048]{1,0:T(8,128)(2,1)S(1)} %copy-done.26, bf16[512,1024]{1,0:T(8,128)(2,1)S(1)} %get-tuple-element.59, bf16[512,1024]{1,0:T(8,128)(2,1)S(1)} %add_convert_fusion.3), kind=kOutput, calls=%fused_computation.9 | convolution fusion | flops 4318035968 | bytes 18874368 | tf_op jit(solution)/shard_map/dot_general | solution.py:376
  113.8 3.1 copy-done.27
  116.9 13.3 %fusion.6 = bf16[1024,2048]{1,0:T(8,128)(2,1)} fusion(f32[1024,2048]{1,0:T(8,128)} %get-tuple-element.75, bf16[2048,1024]{1,0:T(8,128)(2,1)S(1)} %copy-done.27, bf16[512,1024]{1,0:T(8,128)(2,1)S(1)} %get-tuple-element.73, bf16[512,1024]{1,0:T(8,128)(2,1)S(1)} %get-tuple-element.72), kind=kOutput, calls=%fused_computation.8 | convolution fusion | flops 4341104640 | bytes 18874368 | tf_op jit(solution)/shard_map/dot_general | solution.py:376
  130.2 5.1 %fusion.50 = bf16[512,1024]{1,0:T(8,128)(2,1)} fusion(bf16[1024,2048]{1,0:T(8,128)(2,1)S(1)} %copy-done.26, bf16[1024,2048]{1,0:T(8,128)(2,1)} %fusion.6), kind=kOutput, calls=%fused_computation.88 | convolution fusion | flops 2148007936 | bytes 7340032 | tf_op jit(solution)/shard_map/dot_general | solution.py:376
  135.8 6.1 %convolution_convert_fusion = bf16[1024,2048]{1,0:T(8,128)(2,1)} fusion(bf16[1024,2048]{1,0:T(8,128)(2,1)S(1)} %copy-done.34, bf16[512,1024]{1,0:T(8,128)(2,1)S(1)} %get-tuple-element.59, bf16[512,1024]{1,0:T(8,128)(2,1)S(1)} %add_convert_fusion.3), kind=kOutput, calls=%fused_computation.10 | convolution fusion | flops 4301258752 | bytes 10485760 | tf_op jit(solution)/shard_map/dot_general | solution.py:376
  142.0 6.1 %convolution_convert_fusion.1 = bf16[2048,1024]{1,0:T(8,128)(2,1)} fusion(bf16[1024,2048]{1,0:T(8,128)(2,1)S(1)} %get-tuple-element.74, bf16[512,1024]{1,0:T(8,128)(2,1)S(1)} %get-tuple-element.73, bf16[512,1024]{1,0:T(8,128)(2,1)S(1)} %get-tuple-element.72), kind=kOutput, calls=%fused_computation.11 | convolution fusion | flops 4301258752 | bytes 10485760 | tf_op jit(solution)/shard_map/dot_general | solution.py:376
  148.1 7.8 %collective-permute-done.6 = bf16[512,1024]{1,0:T(8,128)(2,1)} collective-permute-done((bf16[512,1024]{1,0:T(8,128)(2,1)}, bf16[512,1024]{1,0:T(8,128)(2,1)}, u32[]{:S(2)}, u32[]{:S(2)}) %collective-permute-start.6) | collective-permute-done | bytes 1048608 | tf_op jit(solution)/shard_map/ppermute | solution.py:372
  155.9 6.6 %multiply_reduce_fusion = (f32[1024]{0:T(1024)S(1)}, f32[512]{0:T(512)S(1)}, f32[1024]{0:T(1024)S(1)}, f32[512,1024]{1,0:T(8,128)S(1)}) fusion(f32[512,1024]{1,0:T(8,128)} %copy-done.7, f32[512]{0:T(512)S(1)} %fusion.73, f32[512]{0:T(512)S(1)} %broadcast_multiply_fusion.1, bf16[512,1024]{1,0:T(8,128)(2,1)} %collective-permute-done.6, ...), kind=kOutput, calls=%fused_computation.70 | convolution fusion | flops 2152723968 | bytes 11552768 | tf_op jit(solution)/shard_map/dot_general | solution.py:376
  162.6 2.2 fusion.84
  164.9 1.4 multiply_convert_fusion.1
  166.5 1.5 collective-permute-start.7
  168.3 3.4 fusion.47
  172.0 14.9 %collective-permute-done.7 = bf16[512,1024]{1,0:T(8,128)(2,1)} collective-permute-done((bf16[512,1024]{1,0:T(8,128)(2,1)}, bf16[512,1024]{1,0:T(8,128)(2,1)}, u32[]{:S(2)}, u32[]{:S(2)}) %collective-permute-start.7) | collective-permute-done | bytes 1048608 | tf_op jit(solution)/shard_map/ppermute | solution.py:372
  186.9 3.2 convolution_convert_fusion.4.grad_ref
  190.1 29.4 %attn_bwd.1 = bf16[3,1024,512]{2,1,0:T(8,128)(2,1)S(1)} custom-call(bf16[3,1024,512]{2,1,0:T(8,128)(2,1)} %copy-done.6, bf16[1024,512]{1,0:T(8,128)(2,1)S(1)} %convolution_convert_fusion.4.grad_ref, f32[4,8,1024]{2,1,0:T(8,128)S(1)} %pad_maximum_fusion.11.lse_ref), custom_call_target="tpu_custom_call" | custom-call | flops 21474836480 | bytes 7340032 | tf_op jit(solution)/shard_map/attn_bwd/pallas_call | solution.py:351
  219.6 2.8 bitcast_convert_fusion
  222.4 1.8 collective-permute-start.9
  224.7 3.6 fusion.32
  228.4 1.7 collective-permute-start.8
  230.1 3.9 convolution_convert_fusion.3
  234.0 5.1 %convolution_convert_fusion.2 = bf16[1024,3,512]{2,0,1:T(8,128)(2,1)} fusion(bf16[3,1024,512]{2,1,0:T(8,128)(2,1)S(1)} %attn_bwd.1, bf16[512,1024]{1,0:T(8,128)(2,1)S(1)} %copy-done.20, bf16[512,1024]{1,0:T(8,128)(2,1)S(1)} %copy-done.18), kind=kOutput, calls=%fused_computation.32 | convolution fusion | flops 3226992640 | bytes 8388608 | tf_op jit(solution)/shard_map/sd,ksc->dkc/dot_general | solution.py:489
  239.1 9.7 %collective-permute-done.9 = bf16[512,1024]{1,0:T(8,128)(2,1)} collective-permute-done((bf16[512,1024]{1,0:T(8,128)(2,1)}, bf16[512,1024]{1,0:T(8,128)(2,1)}, u32[]{:S(2)}, u32[]{:S(2)}) %collective-permute-start.9) | collective-permute-done | bytes 1048608 | tf_op jit(solution)/shard_map/ppermute | solution.py:372
  248.8 4.0 fusion.23
  252.9 1.3 copy-done.13
  254.2 2.2 fusion.17
  256.4 86.5 %all-reduce.7.cloned.1.call-done = (bf16[2048,1024]{1,0:T(8,128)(2,1)}, bf16[1024,2048]{1,0:T(8,128)(2,1)}) async-done(((bf16[2048,1024]{1,0:T(8,128)(2,1)}, bf16[1024,2048]{1,0:T(8,128)(2,1)}), (bf16[2048,1024]{1,0:T(8,128)(2,1)}, bf16[1024,2048]{1,0:T(8,128)(2,1)})) %all-reduce.7.cloned.1.call-update) | async-done | bytes 8388624 | tf_op jit(solution)/shard_map/psum | solution.py:466
  343.0 7.1 %fusion.25 = (f32[1024]{0:T(1024)S(1)}, f32[1024]{0:T(1024)S(1)}, bf16[1,512,1024]{2,1,0:T(8,128)(2,1)}, bf16[1,512,1024]{2,1,0:T(8,128)(2,1)}) fusion(f32[512,1024]{1,0:T(8,128)} %fusion.32, bf16[512,1024]{1,0:T(8,128)(2,1)} %collective-permute-done.8, bf16[1,512,1024]{2,1,0:T(8,128)(2,1)} %param.17, f32[1024,1024]{1,0:T(8,128)} %copy-done.9, ...), kind=kLoop, calls=%fused_computation.43 | loop fusion | flops 11532288 | bytes 15755264 | tf_op jit(solution)/shard_map/reduce_sum | solution.py:497
  350.2 1.5 collective-permute-start.10
  351.7 21.0 %all-gather.1 = bf16[16,1,1024]{2,1,0:T(2,128)(2,1)S(1)} all-gather(bf16[1,1,1024]{2,1,0:T(2,128)(2,1)S(1)} %copy-done.24), channel_id=1, replica_groups=mesh['dp'=16,'tensor'=2] {'dp'}, dimensions={0}, use_global_device_ids=true | all-gather | bytes 34816 | tf_op jit(solution)/shard_map/all_gather | solution.py:516
  372.7 4.6 convolution_bitcast_fusion
  377.2 0.7 collective-permute-start.11
  378.0 17.6 %all-gather.2 = bf16[16,6,512]{2,1,0:T(8,128)(2,1)S(1)} all-gather(bf16[1,6,512]{2,1,0:T(8,128)(2,1)S(1)} %bitcast.87), channel_id=2, replica_groups=mesh['dp'=16,'tensor'=2] {'dp'}, dimensions={0}, use_global_device_ids=true | all-gather | bytes 104448 | tf_op jit(solution)/shard_map/all_gather | solution.py:517
  395.6 6.6 %fusion.62 = f32[1024,6,512]{2,0,1:T(8,128)} fusion(bf16[16,6,512]{2,1,0:T(8,128)(2,1)S(1)} %all-gather.2, bf16[16,1,1024]{2,1,0:T(2,128)(2,1)S(1)} %all-gather.1), kind=kOutput, calls=%fused_computation.101 | convolution fusion | flops 100663296 | bytes 12713984 | tf_op jit(solution)/shard_map/ld,lkc->dkc/dot_general | solution.py:518
  402.2 0.6 convert_reduce_fusion.2
  402.9 0.6 fusion.68
  403.5 4.4 convert_element_type.149
  407.9 4.4 convert_element_type.150
  412.4 47.0 %all-reduce.5.cloned.1.call-done = (bf16[1024,3,512]{2,0,1:T(8,128)(2,1)}, bf16[512,1024]{1,0:T(8,128)(2,1)}) async-done(((bf16[1024,3,512]{2,0,1:T(8,128)(2,1)}, bf16[512,1024]{1,0:T(8,128)(2,1)}), (bf16[1024,3,512]{2,0,1:T(8,128)(2,1)}, bf16[512,1024]{1,0:T(8,128)(2,1)})) %all-reduce.5.cloned.1.call-update) | async-done | bytes 4194320 | tf_op jit(solution)/shard_map/psum | solution.py:495
  459.4 2.9 convert_element_type.148
  462.3 3.6 convert_element_type.147
  (103 shorter events, 4.9 us)
Async XLA Ops:
  7.2 40.6 %copy-start = (bf16[1024,3,512]{2,0,1:T(8,128)(2,1)S(1)}, bf16[1024,3,512]{2,0,1:T(8,128)(2,1)}, u32[]{:S(2)}) copy-start(bf16[1024,3,512]{2,0,1:T(8,128)(2,1)} %param.13) | copy-start | bytes 9437188
  7.2 335.8 %all-reduce.7.cloned.1.call-start = ((), (), s32[]{:S(2)}) async-start(), calls=%async_computation.1 | async-start | bytes 16777216 | tf_op jit(solution)/shard_map/psum | solution.py:466
  8.7 3.7 copy-start.22
  8.7 3.7 copy-start.25
  12.4 6.2 %collective-permute-start = (f32[6,512]{1,0:T(8,128)S(1)}, f32[6,512]{1,0:T(8,128)S(1)}, u32[]{:S(2)}, u32[]{:S(2)}) collective-permute-start(f32[6,512]{1,0:T(8,128)S(1)} %bitcast_add_fusion.1), channel_id=1, source_target_pairs={{0,1},{1,0},{2,3},{3,2},{4,5},{5,4},{6,7},{7,6},{8,9},{9,8},{10,11... | collective-permute-start | bytes 36872 | tf_op jit(solution)/shard_map/ppermute | solution.py:372
  15.5 24.9 %collective-permute-start.1 = (bf16[512,1024]{1,0:T(8,128)(2,1)}, bf16[512,1024]{1,0:T(8,128)(2,1)}, u32[]{:S(2)}, u32[]{:S(2)}) collective-permute-start(bf16[512,1024]{1,0:T(8,128)(2,1)} %bitcast), channel_id=1, source_target_pairs={{0,1},{1,0},{2,3},{3,2},{4,5},{5,4},{6,7},{7,6},{8,9},{9,8},{10,11... | collective-permute-start | bytes 3145736 | tf_op jit(solution)/shard_map/ppermute | solution.py:372
  18.7 24.8 %copy-start.30 = (bf16[512,1024]{1,0:T(8,128)(2,1)S(1)}, bf16[512,1024]{1,0:T(8,128)(2,1)}, u32[]{:S(2)}) copy-start(bf16[512,1024]{1,0:T(8,128)(2,1)} %param.14) | copy-start | bytes 3145732
  43.5 48.8 %collective-permute-start.4 = (bf16[512,1024]{1,0:T(8,128)(2,1)S(1)}, bf16[512,1024]{1,0:T(8,128)(2,1)S(1)}, u32[]{:S(2)}, u32[]{:S(2)}) collective-permute-start(bf16[512,1024]{1,0:T(8,128)(2,1)S(1)} %copy-done.30), channel_id=1, source_target_pairs={{0,1},{1,0},{2,3},{3,2},{4,5},{5,4},{6,7},{7,6},{8,9},{9,8},{10,11... | collective-permute-start | bytes 3145736 | tf_op jit(solution)/shard_map/ppermute | solution.py:372
  46.4 1.0 copy-start.17
  46.5 1.3 copy-start.19
  52.5 9.6 %copy-start.6 = (bf16[3,1024,512]{2,1,0:T(8,128)(2,1)}, bf16[3,1024,512]{2,1,0:T(8,128)(2,1)S(1)}, u32[]{:S(2)}) copy-start(bf16[3,1024,512]{2,1,0:T(8,128)(2,1)S(1)} %convert_bitcast_fusion.qkv_ref) | copy-start | bytes 9437188
  60.5 31.8 %copy-start.1 = (bf16[1024,256]{1,0:T(8,128)(2,1)}, bf16[1024,256]{1,0:T(8,128)(2,1)S(1)}, u32[]{:S(2)}) copy-start(bf16[1024,256]{1,0:T(8,128)(2,1)S(1)} %get-tuple-element.26) | copy-start | bytes 1572868
  60.5 10.7 %copy-start.11 = (bf16[1,512,1024]{2,1,0:T(8,128)(2,1)S(1)}, bf16[1,512,1024]{2,1,0:T(8,128)(2,1)}, u32[]{:S(2)}) copy-start(bf16[1,512,1024]{2,1,0:T(8,128)(2,1)} %param.17) | copy-start | bytes 3145732
  60.5 20.4 %collective-permute-start.2 = (bf16[1024,256]{1,0:T(8,128)(2,1)S(1)}, bf16[1024,256]{1,0:T(8,128)(2,1)S(1)}, u32[]{:S(2)}, u32[]{:S(2)}) collective-permute-start(bf16[1024,256]{1,0:T(8,128)(2,1)S(1)} %get-tuple-element.26), channel_id=1, source_target_pairs={{0,1},{1,0},{2,3},{3,2},{4,5},{5,4},{6,7},{7,6},{8,9},{9,8},{10,11... | collective-permute-start | bytes 1572872 | tf_op jit(solution)/shard_map/ppermute | solution.py:372
  70.6 21.7 %copy-start.3 = (bf16[1024,256]{1,0:T(8,128)(2,1)}, bf16[1024,256]{1,0:T(8,128)(2,1)S(1)}, u32[]{:S(2)}) copy-start(bf16[1024,256]{1,0:T(8,128)(2,1)S(1)} %get-tuple-element.27) | copy-start | bytes 1572868
  70.6 21.5 %collective-permute-start.3 = (bf16[1024,256]{1,0:T(8,128)(2,1)S(1)}, bf16[1024,256]{1,0:T(8,128)(2,1)S(1)}, u32[]{:S(2)}, u32[]{:S(2)}) collective-permute-start(bf16[1024,256]{1,0:T(8,128)(2,1)S(1)} %get-tuple-element.27), channel_id=1, source_target_pairs={{0,1},{1,0},{2,3},{3,2},{4,5},{5,4},{6,7},{7,6},{8,9},{9,8},{10,11... | collective-permute-start | bytes 1572872 | tf_op jit(solution)/shard_map/ppermute | solution.py:372
  71.2 42.0 %collective-permute-start.5 = (bf16[512,1024]{1,0:T(8,128)(2,1)S(1)}, bf16[512,1024]{1,0:T(8,128)(2,1)S(1)}, u32[]{:S(2)}, u32[]{:S(2)}) collective-permute-start(bf16[512,1024]{1,0:T(8,128)(2,1)S(1)} %bitcast.81), channel_id=1, source_target_pairs={{0,1},{1,0},{2,3},{3,2},{4,5},{5,4},{6,7},{7,6},{8,9},{9,8},{10,11... | collective-permute-start | bytes 3145736 | tf_op jit(solution)/shard_map/ppermute | solution.py:372
  94.6 4.1 copy-start.9
  101.1 1.3 copy-start.7
  101.2 2.9 copy-start.26
  113.2 28.8 %copy-start.31 = (bf16[1024,2048]{1,0:T(8,128)(2,1)}, bf16[1024,2048]{1,0:T(8,128)(2,1)S(1)}, u32[]{:S(2)}) copy-start(bf16[1024,2048]{1,0:T(8,128)(2,1)S(1)} %get-tuple-element.74) | copy-start | bytes 12582916
  113.2 3.7 copy-start.27
  130.2 5.6 %copy-start.34 = (bf16[1024,2048]{1,0:T(8,128)(2,1)S(1)}, bf16[1024,2048]{1,0:T(8,128)(2,1)}, u32[]{:S(2)}) copy-start(bf16[1024,2048]{1,0:T(8,128)(2,1)} %fusion.6) | copy-start | bytes 12582916
  135.3 20.6 %collective-permute-start.6 = (bf16[512,1024]{1,0:T(8,128)(2,1)}, bf16[512,1024]{1,0:T(8,128)(2,1)}, u32[]{:S(2)}, u32[]{:S(2)}) collective-permute-start(bf16[512,1024]{1,0:T(8,128)(2,1)} %fusion.50), channel_id=1, source_target_pairs={{0,1},{1,0},{2,3},{3,2},{4,5},{5,4},{6,7},{7,6},{8,9},{9,8},{10,11... | collective-permute-start | bytes 3145736 | tf_op jit(solution)/shard_map/ppermute | solution.py:372
  148.1 14.5 %copy-start.8 = (f32[512,1024]{1,0:T(8,128)S(1)}, f32[512,1024]{1,0:T(8,128)}, u32[]{:S(2)}) copy-start(f32[512,1024]{1,0:T(8,128)} %copy-done.7) | copy-start | bytes 6291460
  162.6 2.3 copy-start.12
  162.6 5.4 %copy-start.32 = (bf16[1024,2048]{1,0:T(8,128)(2,1)S(1)}, bf16[1024,2048]{1,0:T(8,128)(2,1)}, u32[]{:S(2)}) copy-start(bf16[1024,2048]{1,0:T(8,128)(2,1)} %copy-done.31) | copy-start | bytes 12582916
  164.8 1.7 copy-start.10
  164.9 3.5 copy-start.28
  166.5 20.3 %collective-permute-start.7 = (bf16[512,1024]{1,0:T(8,128)(2,1)}, bf16[512,1024]{1,0:T(8,128)(2,1)}, u32[]{:S(2)}, u32[]{:S(2)}) collective-permute-start(bf16[512,1024]{1,0:T(8,128)(2,1)} %multiply_convert_fusion.1), channel_id=1, source_target_pairs={{0,1},{1,0},{2,3},{3,2},{4,5},{5,4},{6,7},{7,6},{8,9},{9,8},{10,11... | collective-permute-start | bytes 3145736 | tf_op jit(solution)/shard_map/ppermute | solution.py:372
  171.7 287.7 %all-reduce.5.cloned.1.call-start = ((), (), s32[]{:S(2)}) async-start(), calls=%async_computation | async-start | bytes 8388608 | tf_op jit(solution)/shard_map/psum | solution.py:495
  219.6 14.4 %copy-start.5 = (bf16[3,1024,512]{2,1,0:T(8,128)(2,1)}, bf16[3,1024,512]{2,1,0:T(8,128)(2,1)S(1)}, u32[]{:S(2)}) copy-start(bf16[3,1024,512]{2,1,0:T(8,128)(2,1)S(1)} %attn_bwd.1) | copy-start | bytes 9437188
  219.6 4.6 copy-start.29
  219.6 5.1 %copy-start.33 = (bf16[1024,2048]{1,0:T(8,128)(2,1)S(1)}, bf16[1024,2048]{1,0:T(8,128)(2,1)}, u32[]{:S(2)}) copy-start(bf16[1024,2048]{1,0:T(8,128)(2,1)} %copy-done.31) | copy-start | bytes 12582916
  222.4 7.7 %copy-start.2 = (bf16[1024,256]{1,0:T(8,128)(2,1)S(1)}, bf16[1024,256]{1,0:T(8,128)(2,1)}, u32[]{:S(2)}) copy-start(bf16[1024,256]{1,0:T(8,128)(2,1)} %copy-done.1) | copy-start | bytes 1572868
  222.4 7.7 %copy-start.4 = (bf16[1024,256]{1,0:T(8,128)(2,1)S(1)}, bf16[1024,256]{1,0:T(8,128)(2,1)}, u32[]{:S(2)}) copy-start(bf16[1024,256]{1,0:T(8,128)(2,1)} %copy-done.3) | copy-start | bytes 1572868
  222.4 26.4 %collective-permute-start.9 = (bf16[512,1024]{1,0:T(8,128)(2,1)}, bf16[512,1024]{1,0:T(8,128)(2,1)}, u32[]{:S(2)}, u32[]{:S(2)}) collective-permute-start(bf16[512,1024]{1,0:T(8,128)(2,1)} %bitcast_convert_fusion), channel_id=1, source_target_pairs={{0,1},{1,0},{2,3},{3,2},{4,5},{5,4},{6,7},{7,6},{8,9},{9,8},{10,11... | collective-permute-start | bytes 3145736 | tf_op jit(solution)/shard_map/ppermute | solution.py:372
  228.4 5.6 %copy-start.18 = (bf16[512,1024]{1,0:T(8,128)(2,1)S(1)}, bf16[512,1024]{1,0:T(8,128)(2,1)}, u32[]{:S(2)}) copy-start(bf16[512,1024]{1,0:T(8,128)(2,1)} %copy-done.17) | copy-start | bytes 3145732
  228.4 5.6 %copy-start.20 = (bf16[512,1024]{1,0:T(8,128)(2,1)S(1)}, bf16[512,1024]{1,0:T(8,128)(2,1)}, u32[]{:S(2)}) copy-start(bf16[512,1024]{1,0:T(8,128)(2,1)} %copy-done.19) | copy-start | bytes 3145732
  228.4 114.6 %collective-permute-start.8 = (bf16[512,1024]{1,0:T(8,128)(2,1)}, bf16[512,1024]{1,0:T(8,128)(2,1)}, u32[]{:S(2)}, u32[]{:S(2)}) collective-permute-start(bf16[512,1024]{1,0:T(8,128)(2,1)} %fusion.47), channel_id=1, source_target_pairs={{0,1},{1,0},{2,3},{3,2},{4,5},{5,4},{6,7},{7,6},{8,9},{9,8},{10,11... | collective-permute-start | bytes 3145736 | tf_op jit(solution)/shard_map/ppermute | solution.py:372
  252.8 1.3 copy-start.13
  343.0 8.7 %copy-start.24 = (bf16[1,1,1024]{2,1,0:T(2,128)(2,1)S(1)}, bf16[1,1,1024]{2,1,0:T(2,128)(2,1)}, u32[]{:S(2)}) copy-start(bf16[1,1,1024]{2,1,0:T(2,128)(2,1)} %get-tuple-element.53) | copy-start | bytes 6148
  350.2 22.5 %collective-permute-start.10 = (bf16[6,512]{1,0:T(8,128)(2,1)S(1)}, bf16[6,512]{1,0:T(8,128)(2,1)S(1)}, u32[]{:S(2)}, u32[]{:S(2)}) collective-permute-start(bf16[6,512]{1,0:T(8,128)(2,1)S(1)} %select_convert_fusion), channel_id=1, source_target_pairs={{0,1},{1,0},{2,3},{3,2},{4,5},{5,4},{6,7},{7,6},{8,9},{9,8},{10,11... | collective-permute-start | bytes 18440 | tf_op jit(solution)/shard_map/ppermute | solution.py:372
  377.2 25.6 %collective-permute-start.11 = (f32[1,1024]{1,0:T(1,128)S(1)}, f32[1,1024]{1,0:T(1,128)S(1)}, u32[]{:S(2)}, u32[]{:S(2)}) collective-permute-start(f32[1,1024]{1,0:T(1,128)S(1)} %convolution_bitcast_fusion), channel_id=1, source_target_pairs={{0,1},{1,0},{2,3},{3,2},{4,5},{5,4},{6,7},{7,6},{8,9},{9,8},{10,11... | collective-permute-start | bytes 12296 | tf_op jit(solution)/shard_map/ppermute | solution.py:372
  395.6 7.3 %copy-start.21 = (bf16[1,1024]{1,0:T(2,128)(2,1)S(1)}, bf16[1,1024]{1,0:T(2,128)(2,1)}, u32[]{:S(2)}) copy-start(bf16[1,1024]{1,0:T(2,128)(2,1)} %param.10) | copy-start | bytes 6148
  395.6 7.3 %copy-start.23 = (f32[1,1024]{1,0:T(1,128)S(1)}, f32[1,1024]{1,0:T(1,128)}, u32[]{:S(2)}) copy-start(f32[1,1024]{1,0:T(1,128)} %copy-done.22) | copy-start | bytes 12292
  395.6 7.9 %copy-start.15 = (bf16[1024,2048]{1,0:T(8,128)(2,1)S(1)}, bf16[1024,2048]{1,0:T(8,128)(2,1)}, u32[]{:S(2)}) copy-start(bf16[1024,2048]{1,0:T(8,128)(2,1)} %get-tuple-element.39) | copy-start | bytes 12582916
  403.5 4.5 copy-start.14
  459.4 2.9 copy-start.16
Sparse Core Ops, SparseCore 0:
  171.8 171.1 all-reduce.6
  347.8 111.5 all-reduce.4

commit v2 on v1

--- a/solution.py
+++ b/solution.py
@@ -372,6 +372,35 @@
     return lax.ppermute(values_in, "tensor", ((0, 1), (1, 0)))
 
 
+def sum_latents(values_in, order):
+    count = lax.axis_size("dp")
+    me = lax.axis_index("dp")
+    if count != 16 or values_in.shape[0] % 256 != 0:
+        return lax.psum(values_in, "dp").astype(jnp.float32)
+    part = values_in
+    for bit in order:
+        partners = [(i, i ^ bit) for i in range(count)]
+        half = part.shape[0] // 2
+        mine_at = jnp.where((me & bit) != 0, half, 0)
+        sent = lax.dynamic_slice_in_dim(part, half - mine_at, half, 0)
+        kept = lax.dynamic_slice_in_dim(part, mine_at, half, 0)
+        came = lax.ppermute(sent, "dp", partners)
+        part = (kept.astype(jnp.float32) + came.astype(jnp.float32)).astype(jnp.bfloat16)
+    for bit in reversed(order):
+        partners = [(i, i ^ bit) for i in range(count)]
+        came = lax.ppermute(part, "dp", partners)
+        part = jnp.where(
+            (me & bit) != 0,
+            jnp.concatenate((came, part), axis=0),
+            jnp.concatenate((part, came), axis=0),
+        )
+    return part.astype(jnp.float32)
+
+
+Y_FIRST = (1, 2, 4, 8)
+Z_FIRST = (1, 4, 8, 2)
+
+
 def dot_f32(left, right, dims):
     return lax.dot_general(left, right, (dims, ((), ())), preferred_element_type=jnp.float32)
 
@@ -463,7 +492,8 @@
     grad_down = dot_f32(hidden_act, grad_mlp, TN).astype(bf16)
     grad_up = dot_f32(normed_two, grad_pre, TN).astype(bf16)
     grad_down, grad_up, two_recv = lax.optimization_barrier((grad_down, grad_up, two_recv))
-    sum_down, sum_up = lax.psum((grad_down, grad_up), "dp")
+    sum_down = sum_latents(grad_down, Y_FIRST)
+    sum_up = sum_latents(grad_up, Z_FIRST)
     grad_normed_two = two_own + two_recv.astype(jnp.float32)
     middle_back, grad_shift_two, grad_scale_two = back_two(grad_normed_two)
     grad_middle = grad_out + middle_back
@@ -489,10 +519,15 @@
     grad_qkv_weight = jnp.einsum(
         "sd,ksc->dkc", normed_one, grad_qkv, preferred_element_type=jnp.float32
     ).astype(bf16)
-    grad_qkv_weight, grad_out_weight, sum_down, sum_up = lax.optimization_barrier(
-        (grad_qkv_weight, grad_out_weight, sum_down, sum_up)
-    )
-    sum_qkv, sum_out = lax.psum((grad_qkv_weight, grad_out_weight), "dp")
+    sum_out = sum_latents(grad_out_weight, Z_FIRST)
+    split = width // 2
+    sum_qkv = jnp.concatenate(
+        (
+            sum_latents(grad_qkv_weight[:split], Y_FIRST),
+            sum_latents(grad_qkv_weight[split:], Z_FIRST),
+        ),
+        axis=0,
+    )
     block_out = (middle_own + gate_two * branch_mlp).astype(bf16)
     grad_gate_two = jnp.sum(grad_out * branch_mlp, axis=0, keepdims=True)
     grad_normed_one = one_own + one_recv.astype(jnp.float32)
@@ -513,8 +548,14 @@
     mod_keep = jnp.where(mine == 0, left, right)
     mod_send = jnp.where(mine == 0, right, left).astype(bf16)
     grad_mod = (mod_keep + swap(mod_send).astype(jnp.float32)).astype(bf16)[None]
-    cond_all = lax.all_gather(cond_act, "dp", axis=0, tiled=True)
-    mod_all = lax.all_gather(grad_mod, "dp", axis=0, tiled=True)
+    factors = lax.all_gather(
+        jnp.concatenate((cond_act, grad_mod.reshape(1, 6 * local_cols)), axis=1),
+        "dp",
+        axis=0,
+        tiled=True,
+    )
+    cond_all = factors[:, :width]
+    mod_all = factors[:, width:].reshape(-1, 6, local_cols)
     grad_mod_weight = jnp.einsum(
         "ld,lkc->dkc", cond_all, mod_all, preferred_element_type=jnp.float32
     )
@@ -529,10 +570,10 @@
         grad_conditioning,
         grad_mod_weight,
         grad_mod_bias,
-        sum_qkv.astype(jnp.float32),
-        sum_out.astype(jnp.float32),
-        sum_up.astype(jnp.float32),
-        sum_down.astype(jnp.float32),
+        sum_qkv,
+        sum_out,
+        sum_up,
+        sum_down,
     )
 
 

time: 477 us -> 536 us (1.12)
  starting transfers between devices: 15.4 us -> 48 us
  other arithmetic: 47.6 us -> 69.8 us
  between operations: 14.9 us -> 1.86 us
  waiting for transfers between devices: 207 us -> 220 us
    ppermute x0 -> x40, waiting for transfers between devices: none -> 145 us  [the longest x20 74.1 us: sum_latents(): came = lax.ppermute(part, 'dp', partners)]
    psum x2 -> x0, waiting for transfers between devices: 134 us -> none  [the longest x1 86.5 us: body_pair(): sum_down, sum_up = lax.psum((grad_down, grad_up), 'dp')]
    ppermute x0 -> x40, starting transfers between devices: none -> 34.4 us  [the longest x20 17.8 us: sum_latents(): came = lax.ppermute(part, 'dp', partners)]
    select_n x0 -> x17, other arithmetic: none -> 14.2 us  [sum_latents(): jnp.where(me & bit != 0, jnp.concatenate((came, part), axis=0), jnp.conca...]
    convert_element_type x4 -> x24, other arithmetic: 15.4 us -> 28.3 us  [the longest x3 16.6 us: sum_latents(): return part.astype(jnp.float32)]
    dot_general x11, matrix products: 62.8 us -> 69.2 us  [dot_f32(): lax.dot_general(left, right, (dims, ((), ())), preferred_element_type=jnp...]
    dynamic_slice x0 -> x20, local copies, waits for them, and re-layouts: none -> 5.98 us  [sum_latents(): sent = lax.dynamic_slice_in_dim(part, half - mine_at, half, 0)]
    all_gather x2 -> x1, blocking collectives: 38.6 us -> 35.2 us  [body_pair(): lax.all_gather(jnp.concatenate((cond_act, grad_mod.reshape(1, 6 * local_c...]
  transfers between devices with their start and end apart: 14 -> 52, of which waited for: 8 -> 21; matrix products, arithmetic and copies ran while one was open for 21% -> 25% of each run, Pallas kernels for 10% -> 9%
where the time goes in v2:
time: 536 us; the launch traced here: 532 us
  waiting for transfers between devices  220 us (41%)
  matrix products  96.8 us (18%)
  other arithmetic  69.8 us (13%)
  starting transfers between devices  48 us (9%)
  Pallas kernels  47.4 us (9%)
  blocking collectives  35.2 us (7%)
  local copies, waits for them, and re-layouts  13.3 us (2%)
    ppermute x12, waiting for transfers between devices, swap(): return lax.ppermute(values_in, 'tensor', ((0, 1), (1, 0)))  74.9 us
    ppermute x20, waiting for transfers between devices, sum_latents(): came = lax.ppermute(part, 'dp', partners)  74.1 us
    ppermute x20, waiting for transfers between devices, sum_latents(): came = lax.ppermute(sent, 'dp', partners)  70.7 us
    dot_general x11, matrix products, dot_f32(): lax.dot_general(left, right, (dims, ((), ())), preferred_element_type=jnp...  69.2 us
    all_gather x1, blocking collectives, body_pair(): lax.all_gather(jnp.concatenate((cond_act, grad_mod.reshape(1, 6 * local_c...  35.2 us
    pallas_call x1, Pallas kernels, attn_backward(): pl.pallas_call(attn_bwd_kernel, grid=(pairs,), in_specs=[pl.BlockSpec((3,...  29.9 us
    ppermute x20, starting transfers between devices, sum_latents(): came = lax.ppermute(part, 'dp', partners)  17.8 us
    pallas_call x2, Pallas kernels, attn_forward(): pl.pallas_call(attn_fwd_kernel, grid=(pairs,), in_specs=[pl.BlockSpec((3,...  17.5 us
  transfers between devices with their start and end apart: 52, of which 21 were waited for; matrix products, arithmetic and copies ran while one was open for 25% of the time, Pallas kernels for 9%

profile of v2, /device:TPU:0, one launch (start us, length us, event | category | flops | bytes accessed | tf_op | source)
XLA Modules:
  0.0 532.1 jit_solution(321915896820945029)
XLA Ops:
  2.1 3.7 fusion.71
  5.8 3.0 collective-permute-start
  12.1 21.7 %collective-permute-done.1 = bf16[512,1024]{1,0:T(8,128)(2,1)} collective-permute-done((bf16[512,1024]{1,0:T(8,128)(2,1)}, bf16[512,1024]{1,0:T(8,128)(2,1)}, u32[]{:S(2)}, u32[]{:S(2)}) %collective-permute-start.1) | collective-permute-done | bytes 1048608 | tf_op jit(solution)/shard_map/ppermute | solution.py:372
  37.5 2.4 fusion.18
  41.2 4.9 convert_bitcast_fusion.qkv_ref
  46.1 8.7 %attn_fwd.2 = (bf16[1024,256]{1,0:T(8,128)(2,1)}, f32[2,8,1024]{2,1,0:T(8,128)S(1)}) custom-call(bf16[3,1024,512]{2,1,0:T(8,128)(2,1)S(1)} %convert_bitcast_fusion.qkv_ref), custom_call_target="tpu_custom_call" | custom-call | flops 4294967296 | bytes 2097152 | tf_op jit(solution)/shard_map/attn_fwd/pallas_call | solution.py:326
  56.3 8.8 %attn_fwd.3 = (bf16[1024,256]{1,0:T(8,128)(2,1)}, f32[2,8,1024]{2,1,0:T(8,128)S(1)}) custom-call(bf16[3,1024,512]{2,1,0:T(8,128)(2,1)S(1)} %convert_bitcast_fusion.qkv_ref), custom_call_target="tpu_custom_call" | custom-call | flops 4294967296 | bytes 2097152 | tf_op jit(solution)/shard_map/attn_fwd/pallas_call | solution.py:326
  67.2 7.4 %collective-permute-done.2 = bf16[1024,256]{1,0:T(8,128)(2,1)} collective-permute-done((bf16[1024,256]{1,0:T(8,128)(2,1)}, bf16[1024,256]{1,0:T(8,128)(2,1)}, u32[]{:S(2)}, u32[]{:S(2)}) %collective-permute-start.2) | collective-permute-done | bytes 524320 | tf_op jit(solution)/shard_map/ppermute | solution.py:372
  75.7 10.2 %collective-permute-done.3 = bf16[1024,256]{1,0:T(8,128)(2,1)} collective-permute-done((bf16[1024,256]{1,0:T(8,128)(2,1)}, bf16[1024,256]{1,0:T(8,128)(2,1)}, u32[]{:S(2)}, u32[]{:S(2)}) %collective-permute-start.3) | collective-permute-done | bytes 524320 | tf_op jit(solution)/shard_map/ppermute | solution.py:372
  87.0 4.2 fusion.36
  94.5 2.4 fusion.86
  99.1 9.8 %multiply_convert_fusion = (bf16[1024,2048]{1,0:T(8,128)(2,1)}, f32[1024,2048]{1,0:T(8,128)}) fusion(bf16[1024,2048]{1,0:T(8,128)(2,1)S(1)} %copy-done.21, bf16[512,1024]{1,0:T(8,128)(2,1)S(1)} %get-tuple-element.47, bf16[512,1024]{1,0:T(8,128)(2,1)S(1)} %add_convert_fusion.7), kind=kOutput, calls=%fused_computation.9 | convolution fusion | flops 4318035968 | bytes 18874368 | tf_op jit(solution)/shard_map/dot_general | solution.py:405
  109.5 14.3 %fusion.6 = bf16[1024,2048]{1,0:T(8,128)(2,1)} fusion(f32[1024,2048]{1,0:T(8,128)} %get-tuple-element.65, bf16[2048,1024]{1,0:T(8,128)(2,1)} %param.16, bf16[512,1024]{1,0:T(8,128)(2,1)S(1)} %get-tuple-element.63, bf16[512,1024]{1,0:T(8,128)(2,1)S(1)} %get-tuple-element.62), kind=kOutput, calls=%fused_computation.8 | convolution fusion | flops 4341104640 | bytes 18874368 | tf_op jit(solution)/shard_map/dot_general | solution.py:405
  123.8 4.0 fusion.52
  128.4 7.0 %convolution_convert_fusion.1 = bf16[2048,1024]{1,0:T(8,128)(2,1)S(1)} fusion(bf16[1024,2048]{1,0:T(8,128)(2,1)} %get-tuple-element.64, bf16[512,1024]{1,0:T(8,128)(2,1)S(1)} %get-tuple-element.63, bf16[512,1024]{1,0:T(8,128)(2,1)S(1)} %get-tuple-element.62), kind=kOutput, calls=%fused_computation.17 | convolution fusion | flops 4301258752 | bytes 10485760 | tf_op jit(solution)/shard_map/dot_general | solution.py:405
  135.4 7.6 %fusion.49 = bf16[512,1024]{1,0:T(8,128)(2,1)} fusion(bf16[2048,1024]{1,0:T(8,128)(2,1)} %param.16, bf16[1024,2048]{1,0:T(8,128)(2,1)} %get-tuple-element.64), kind=kOutput, calls=%fused_computation.102 | convolution fusion | flops 2148007936 | bytes 7340032 | tf_op jit(solution)/shard_map/dot_general | solution.py:405
  143.0 7.2 %convolution_convert_fusion = bf16[1024,2048]{1,0:T(8,128)(2,1)S(1)} fusion(bf16[1024,2048]{1,0:T(8,128)(2,1)} %fusion.6, bf16[512,1024]{1,0:T(8,128)(2,1)S(1)} %get-tuple-element.47, bf16[512,1024]{1,0:T(8,128)(2,1)S(1)} %add_convert_fusion.7), kind=kOutput, calls=%fused_computation.16 | convolution fusion | flops 4301258752 | bytes 10485760 | tf_op jit(solution)/shard_map/dot_general | solution.py:405
  150.3 6.0 %multiply_reduce_fusion = (f32[1024]{0:T(1024)S(1)}, f32[512]{0:T(512)S(1)}, f32[1024]{0:T(1024)S(1)}, f32[512,1024]{1,0:T(8,128)S(1)}) fusion(f32[512,1024]{1,0:T(8,128)S(1)} %get-tuple-element.44, f32[512]{0:T(512)S(1)} %fusion.74, f32[512]{0:T(512)S(1)} %broadcast_multiply_fusion.1, bf16[512,1024]{1,0:T(8,128)(2,1)S(1)} %collective-permute-done.6, ...), kind=kOutput, calls=%fused_computation.81 | convolution fusion | flops 2152723968 | bytes 11552768 | tf_op jit(solution)/shard_map/dot_general | solution.py:405
  160.1 3.7 fusion.34
  167.2 11.6 %collective-permute-done.7 = bf16[512,1024]{1,0:T(8,128)(2,1)S(1)} collective-permute-done((bf16[512,1024]{1,0:T(8,128)(2,1)S(1)}, bf16[512,1024]{1,0:T(8,128)(2,1)S(1)}, u32[]{:S(2)}, u32[]{:S(2)}) %collective-permute-start.7) | collective-permute-done | bytes 1048608 | tf_op jit(solution)/shard_map/ppermute | solution.py:372
  178.8 2.5 convolution_convert_fusion.3
  181.3 2.9 convolution_convert_fusion.4.grad_ref
  185.0 29.9 %attn_bwd.1 = bf16[3,1024,512]{2,1,0:T(8,128)(2,1)S(1)} custom-call(bf16[3,1024,512]{2,1,0:T(8,128)(2,1)} %copy-done.1, bf16[1024,512]{1,0:T(8,128)(2,1)S(1)} %convolution_convert_fusion.4.grad_ref, f32[4,8,1024]{2,1,0:T(8,128)S(1)} %pad_maximum_fusion.11.lse_ref), custom_call_target="tpu_custom_call" | custom-call | flops 21474836480 | bytes 7340032 | tf_op jit(solution)/shard_map/attn_bwd/pallas_call | solution.py:351
  214.9 5.6 %convolution_convert_fusion.2 = bf16[1024,3,512]{2,0,1:T(8,128)(2,1)S(1)} fusion(bf16[3,1024,512]{2,1,0:T(8,128)(2,1)S(1)} %attn_bwd.1, bf16[512,1024]{1,0:T(8,128)(2,1)} %copy-done.15, bf16[512,1024]{1,0:T(8,128)(2,1)} %copy-done.14), kind=kOutput, calls=%fused_computation.39 | convolution fusion | flops 3226992640 | bytes 8388608 | tf_op jit(solution)/shard_map/sd,ksc->dkc/dot_general | solution.py:519
  223.4 1.8 bitcast_convert_fusion
  225.2 5.7 %collective-permute-done.29 = bf16[128,1024]{1,0:T(8,128)(2,1)S(1)} collective-permute-done((bf16[128,1024]{1,0:T(8,128)(2,1)S(1)}, bf16[128,1024]{1,0:T(8,128)(2,1)S(1)}, u32[]{:S(2)}, u32[]{:S(2)}) %collective-permute-start.29) | collective-permute-done | bytes 262176 | tf_op jit(solution)/shard_map/ppermute | solution.py:387
  233.4 2.2 collective-permute-start.30
  236.8 5.0 collective-permute-done.30
  243.8 2.4 collective-permute-done.31
  246.4 10.6 %collective-permute-done.9 = bf16[512,1024]{1,0:T(8,128)(2,1)S(1)} collective-permute-done((bf16[512,1024]{1,0:T(8,128)(2,1)S(1)}, bf16[512,1024]{1,0:T(8,128)(2,1)S(1)}, u32[]{:S(2)}, u32[]{:S(2)}) %collective-permute-start.9) | collective-permute-done | bytes 1048608 | tf_op jit(solution)/shard_map/ppermute | solution.py:372
  258.1 3.3 fusion.25
  262.4 2.3 fusion.19
  264.7 13.5 %collective-permute-done.8 = bf16[512,1024]{1,0:T(8,128)(2,1)S(1)} collective-permute-done((bf16[512,1024]{1,0:T(8,128)(2,1)S(1)}, bf16[512,1024]{1,0:T(8,128)(2,1)S(1)}, u32[]{:S(2)}, u32[]{:S(2)}) %collective-permute-start.8) | collective-permute-done | bytes 1048608 | tf_op jit(solution)/shard_map/ppermute | solution.py:372
  278.2 2.2 collective-permute-start.33
  280.4 3.8 fusion.27
  285.3 3.4 add_convert_fusion
  290.4 2.5 add_convert_fusion.1
  296.4 35.2 %all-gather = bf16[16,1,4096]{2,1,0:T(2,128)(2,1)S(1)} all-gather(bf16[1,1,4096]{2,1,0:T(2,128)(2,1)S(1)} %maximum_bitcast_fusion.3), channel_id=1, replica_groups=mesh['dp'=16,'tensor'=2] {'dp'}, dimensions={0}, use_global_device_ids=true | all-gather | bytes 139264 | tf_op jit(solution)/shard_map/all_gather | solution.py:551
  334.8 3.0 collective-permute-start.38
  338.9 2.1 collective-permute-start.14
  341.5 27.4 %collective-permute-done.38 = bf16[128,2048]{1,0:T(8,128)(2,1)S(1)} collective-permute-done((bf16[128,2048]{1,0:T(8,128)(2,1)S(1)}, bf16[128,2048]{1,0:T(8,128)(2,1)S(1)}, u32[]{:S(2)}, u32[]{:S(2)}) %collective-permute-start.38) | collective-permute-done | bytes 524320 | tf_op jit(solution)/shard_map/ppermute | solution.py:387
  369.0 12.9 %collective-permute-done.46 = bf16[256,1024]{1,0:T(8,128)(2,1)S(1)} collective-permute-done((bf16[256,1024]{1,0:T(8,128)(2,1)S(1)}, bf16[256,1024]{1,0:T(8,128)(2,1)S(1)}, u32[]{:S(2)}, u32[]{:S(2)}) %collective-permute-start.46) | collective-permute-done | bytes 524320 | tf_op jit(solution)/shard_map/ppermute | solution.py:387
  382.1 6.3 %collective-permute-done.39 = bf16[64,2048]{1,0:T(8,128)(2,1)S(1)} collective-permute-done((bf16[64,2048]{1,0:T(8,128)(2,1)S(1)}, bf16[64,2048]{1,0:T(8,128)(2,1)S(1)}, u32[]{:S(2)}, u32[]{:S(2)}) %collective-permute-start.39) | collective-permute-done | bytes 262176 | tf_op jit(solution)/shard_map/ppermute | solution.py:387
  389.4 11.1 %collective-permute-done.47 = bf16[128,1024]{1,0:T(8,128)(2,1)S(1)} collective-permute-done((bf16[128,1024]{1,0:T(8,128)(2,1)S(1)}, bf16[128,1024]{1,0:T(8,128)(2,1)S(1)}, u32[]{:S(2)}, u32[]{:S(2)}) %collective-permute-start.47) | collective-permute-done | bytes 262176 | tf_op jit(solution)/shard_map/ppermute | solution.py:387
  400.8 3.0 collective-permute-start.41
  404.5 20.3 %collective-permute-done.48 = bf16[128,1024]{1,0:T(8,128)(2,1)S(1)} collective-permute-done((bf16[128,1024]{1,0:T(8,128)(2,1)S(1)}, bf16[128,1024]{1,0:T(8,128)(2,1)S(1)}, u32[]{:S(2)}, u32[]{:S(2)}) %collective-permute-start.48) | collective-permute-done | bytes 262176 | tf_op jit(solution)/shard_map/ppermute | solution.py:391
  425.0 11.0 %collective-permute-done.41 = bf16[128,2048]{1,0:T(8,128)(2,1)S(1)} collective-permute-done((bf16[128,2048]{1,0:T(8,128)(2,1)S(1)}, bf16[128,2048]{1,0:T(8,128)(2,1)S(1)}, u32[]{:S(2)}, u32[]{:S(2)}) %collective-permute-start.41) | collective-permute-done | bytes 524320 | tf_op jit(solution)/shard_map/ppermute | solution.py:391
  436.3 3.0 collective-permute-start.42
  439.3 10.0 %collective-permute-done.49 = bf16[256,1024]{1,0:T(8,128)(2,1)S(1)} collective-permute-done((bf16[256,1024]{1,0:T(8,128)(2,1)S(1)}, bf16[256,1024]{1,0:T(8,128)(2,1)S(1)}, u32[]{:S(2)}, u32[]{:S(2)}) %collective-permute-start.49) | collective-permute-done | bytes 524320 | tf_op jit(solution)/shard_map/ppermute | solution.py:391
  452.0 3.0 collective-permute-done.24
  455.5 8.2 %collective-permute-done.16 = bf16[32,3,512]{2,0,1:T(8,128)(2,1)S(1)} collective-permute-done((bf16[32,3,512]{2,0,1:T(8,128)(2,1)S(1)}, bf16[32,3,512]{2,0,1:T(8,128)(2,1)S(1)}, u32[]{:S(2)}, u32[]{:S(2)}) %collective-permute-start.16) | collective-permute-done | bytes 98336 | tf_op jit(solution)/shard_map/ppermute | solution.py:391
  463.7 3.4 collective-permute-start.25
  468.2 6.9 %collective-permute-done.25 = bf16[64,3,512]{2,0,1:T(8,128)(2,1)S(1)} collective-permute-done((bf16[64,3,512]{2,0,1:T(8,128)(2,1)S(1)}, bf16[64,3,512]{2,0,1:T(8,128)(2,1)S(1)}, u32[]{:S(2)}, u32[]{:S(2)}) %collective-permute-start.25) | collective-permute-done | bytes 196640 | tf_op jit(solution)/shard_map/ppermute | solution.py:391
  475.2 7.1 %collective-permute-done.17 = bf16[64,3,512]{2,0,1:T(8,128)(2,1)S(1)} collective-permute-done((bf16[64,3,512]{2,0,1:T(8,128)(2,1)S(1)}, bf16[64,3,512]{2,0,1:T(8,128)(2,1)S(1)}, u32[]{:S(2)}, u32[]{:S(2)}) %collective-permute-start.17) | collective-permute-done | bytes 196640 | tf_op jit(solution)/shard_map/ppermute | solution.py:391
  483.3 2.4 maximum_select_fusion.2
  485.7 7.6 %collective-permute-done.26 = bf16[128,3,512]{2,0,1:T(8,128)(2,1)S(1)} collective-permute-done((bf16[128,3,512]{2,0,1:T(8,128)(2,1)S(1)}, bf16[128,3,512]{2,0,1:T(8,128)(2,1)S(1)}, u32[]{:S(2)}, u32[]{:S(2)}) %collective-permute-start.26) | collective-permute-done | bytes 393248 | tf_op jit(solution)/shard_map/ppermute | solution.py:391
  495.0 2.3 maximum_select_fusion.3
  499.0 6.6 %fusion.65 = f32[1024,6,512]{2,0,1:T(8,128)} fusion(bf16[2,6,8,512]{3,2,1,0:T(8,128)(2,1)S(1)} %bitcast.96, bf16[16,4096]{1,0:T(8,128)(2,1)S(1)} %bitcast.94), kind=kOutput, calls=%fused_computation.146 | convolution fusion | flops 100663296 | bytes 12713984 | tf_op jit(solution)/shard_map/ld,lkc->dkc/dot_general | solution.py:559
  506.9 3.4 fusion.62
  510.3 2.4 maximum_select_fusion.5
  512.6 2.5 maximum_select_fusion.4
  515.1 3.6 maximum_convert_fusion
  518.7 6.8 %fusion.7 = f32[1024,2048]{1,0:T(8,128)} fusion(bf16[512,2048]{1,0:T(8,128)(2,1)} %maximum_select_fusion.2, bf16[512,2048]{1,0:T(8,128)(2,1)} %collective-permute-done.43, pred[]{:T(512)S(6)} %ne.8), kind=kLoop, calls=%fused_computation.11 | loop fusion | flops 20971520 | bytes 12582913 | tf_op jit(solution)/shard_map/convert_element_type | solution.py:397
  525.5 6.4 %fusion.8 = f32[2048,1024]{1,0:T(8,128)} fusion(bf16[1024,1024]{1,0:T(8,128)(2,1)} %maximum_select_fusion.3, bf16[1024,1024]{1,0:T(8,128)(2,1)} %collective-permute-done.51, pred[]{:T(512)S(6)} %ne.8), kind=kLoop, calls=%fused_computation.13 | loop fusion | flops 20971520 | bytes 12582913 | tf_op jit(solution)/shard_map/convert_element_type | solution.py:397
  (224 shorter events, 64.7 us)
Async XLA Ops:
  0.6 40.5 %copy-start = (bf16[1024,3,512]{2,0,1:T(8,128)(2,1)S(1)}, bf16[1024,3,512]{2,0,1:T(8,128)(2,1)}, u32[]{:S(2)}) copy-start(bf16[1024,3,512]{2,0,1:T(8,128)(2,1)} %param.13) | copy-start | bytes 9437188
  5.8 6.2 %collective-permute-start = (f32[6,512]{1,0:T(8,128)S(1)}, f32[6,512]{1,0:T(8,128)S(1)}, u32[]{:S(2)}, u32[]{:S(2)}) collective-permute-start(f32[6,512]{1,0:T(8,128)S(1)} %bitcast_add_fusion.1), channel_id=1, source_target_pairs={{0,1},{1,0},{2,3},{3,2},{4,5},{5,4},{6,7},{7,6},{8,9},{9,8},{10,11... | collective-permute-start | bytes 36872 | tf_op jit(solution)/shard_map/ppermute | solution.py:372
  8.9 24.9 %collective-permute-start.1 = (bf16[512,1024]{1,0:T(8,128)(2,1)}, bf16[512,1024]{1,0:T(8,128)(2,1)}, u32[]{:S(2)}, u32[]{:S(2)}) collective-permute-start(bf16[512,1024]{1,0:T(8,128)(2,1)} %bitcast), channel_id=1, source_target_pairs={{0,1},{1,0},{2,3},{3,2},{4,5},{5,4},{6,7},{7,6},{8,9},{9,8},{10,11... | collective-permute-start | bytes 3145736 | tf_op jit(solution)/shard_map/ppermute | solution.py:372
  36.9 50.1 %collective-permute-start.4 = (bf16[512,1024]{1,0:T(8,128)(2,1)}, bf16[512,1024]{1,0:T(8,128)(2,1)}, u32[]{:S(2)}, u32[]{:S(2)}) collective-permute-start(bf16[512,1024]{1,0:T(8,128)(2,1)} %param.14), channel_id=1, source_target_pairs={{0,1},{1,0},{2,3},{3,2},{4,5},{5,4},{6,7},{7,6},{8,9},{9,8},{10,11... | collective-permute-start | bytes 3145736 | tf_op jit(solution)/shard_map/ppermute | solution.py:372
  46.1 10.2 %copy-start.1 = (bf16[3,1024,512]{2,1,0:T(8,128)(2,1)}, bf16[3,1024,512]{2,1,0:T(8,128)(2,1)S(1)}, u32[]{:S(2)}) copy-start(bf16[3,1024,512]{2,1,0:T(8,128)(2,1)S(1)} %convert_bitcast_fusion.qkv_ref) | copy-start | bytes 9437188
  54.8 19.8 %collective-permute-start.2 = (bf16[1024,256]{1,0:T(8,128)(2,1)}, bf16[1024,256]{1,0:T(8,128)(2,1)}, u32[]{:S(2)}, u32[]{:S(2)}) collective-permute-start(bf16[1024,256]{1,0:T(8,128)(2,1)} %get-tuple-element.22), channel_id=1, source_target_pairs={{0,1},{1,0},{2,3},{3,2},{4,5},{5,4},{6,7},{7,6},{8,9},{9,8},{10,11... | collective-permute-start | bytes 1572872 | tf_op jit(solution)/shard_map/ppermute | solution.py:372
  65.1 20.7 %collective-permute-start.3 = (bf16[1024,256]{1,0:T(8,128)(2,1)}, bf16[1024,256]{1,0:T(8,128)(2,1)}, u32[]{:S(2)}, u32[]{:S(2)}) collective-permute-start(bf16[1024,256]{1,0:T(8,128)(2,1)} %get-tuple-element.23), channel_id=1, source_target_pairs={{0,1},{1,0},{2,3},{3,2},{4,5},{5,4},{6,7},{7,6},{8,9},{9,8},{10,11... | collective-permute-start | bytes 1572872 | tf_op jit(solution)/shard_map/ppermute | solution.py:372
  65.7 43.2 %collective-permute-start.5 = (bf16[512,1024]{1,0:T(8,128)(2,1)}, bf16[512,1024]{1,0:T(8,128)(2,1)S(1)}, u32[]{:S(2)}, u32[]{:S(2)}) collective-permute-start(bf16[512,1024]{1,0:T(8,128)(2,1)} %bitcast.92), channel_id=1, source_target_pairs={{0,1},{1,0},{2,3},{3,2},{4,5},{5,4},{6,7},{7,6},{8,9},{9,8},{10,11... | collective-permute-start | bytes 3145736 | tf_op jit(solution)/shard_map/ppermute | solution.py:372
  99.1 9.8 %copy-start.2 = (bf16[1,512,1024]{2,1,0:T(8,128)(2,1)S(1)}, bf16[1,512,1024]{2,1,0:T(8,128)(2,1)}, u32[]{:S(2)}) copy-start(bf16[1,512,1024]{2,1,0:T(8,128)(2,1)} %param.17) | copy-start | bytes 3145732
  127.8 22.5 %collective-permute-start.6 = (bf16[512,1024]{1,0:T(8,128)(2,1)S(1)}, bf16[512,1024]{1,0:T(8,128)(2,1)S(1)}, u32[]{:S(2)}, u32[]{:S(2)}) collective-permute-start(bf16[512,1024]{1,0:T(8,128)(2,1)S(1)} %fusion.52), channel_id=1, source_target_pairs={{0,1},{1,0},{2,3},{3,2},{4,5},{5,4},{6,7},{7,6},{8,9},{9,8},{10,11... | collective-permute-start | bytes 3145736 | tf_op jit(solution)/shard_map/ppermute | solution.py:372
  135.4 28.4 %copy-start.6 = (bf16[2048,1024]{1,0:T(8,128)(2,1)}, bf16[2048,1024]{1,0:T(8,128)(2,1)S(1)}, u32[]{:S(2)}) copy-start(bf16[2048,1024]{1,0:T(8,128)(2,1)S(1)} %convolution_convert_fusion.1) | copy-start | bytes 12582916
  150.3 15.0 %copy-start.4 = (bf16[1024,2048]{1,0:T(8,128)(2,1)}, bf16[1024,2048]{1,0:T(8,128)(2,1)S(1)}, u32[]{:S(2)}) copy-start(bf16[1024,2048]{1,0:T(8,128)(2,1)S(1)} %convolution_convert_fusion) | copy-start | bytes 12582916
  157.6 21.1 %collective-permute-start.7 = (bf16[512,1024]{1,0:T(8,128)(2,1)S(1)}, bf16[512,1024]{1,0:T(8,128)(2,1)S(1)}, u32[]{:S(2)}, u32[]{:S(2)}) collective-permute-start(bf16[512,1024]{1,0:T(8,128)(2,1)S(1)} %multiply_convert_fusion.1), channel_id=1, source_target_pairs={{0,1},{1,0},{2,3},{3,2},{4,5},{5,4},{6,7},{7,6},{8,9},{9,8},{10,11... | collective-permute-start | bytes 3145736 | tf_op jit(solution)/shard_map/ppermute | solution.py:372
  165.2 119.0 %collective-permute-start.44 = (bf16[1024,1024]{1,0:T(8,128)(2,1)}, bf16[1024,1024]{1,0:T(8,128)(2,1)}, u32[]{:S(2)}, u32[]{:S(2)}) collective-permute-start(bf16[1024,1024]{1,0:T(8,128)(2,1)} %constant_dynamic-slice_fusion.3), channel_id=1, source_target_pairs={{0,2},{2,0},{4,6},{6,4},{8,10},{10,8},{12,14},{14,12},{16,18},{18,... | collective-permute-start | bytes 6291464 | tf_op jit(solution)/shard_map/ppermute | solution.py:387
  166.7 122.1 %collective-permute-start.36 = (bf16[512,2048]{1,0:T(8,128)(2,1)}, bf16[512,2048]{1,0:T(8,128)(2,1)}, u32[]{:S(2)}, u32[]{:S(2)}) collective-permute-start(bf16[512,2048]{1,0:T(8,128)(2,1)} %constant_dynamic-slice_fusion.7), channel_id=1, source_target_pairs={{0,2},{2,0},{4,6},{6,4},{8,10},{10,8},{12,14},{14,12},{16,18},{18,... | collective-permute-start | bytes 6291464 | tf_op jit(solution)/shard_map/ppermute | solution.py:387
  185.0 36.5 %collective-permute-start.28 = (bf16[256,1024]{1,0:T(8,128)(2,1)}, bf16[256,1024]{1,0:T(8,128)(2,1)S(1)}, u32[]{:S(2)}, u32[]{:S(2)}) collective-permute-start(bf16[256,1024]{1,0:T(8,128)(2,1)} %constant_dynamic-slice_fusion.11), channel_id=1, source_target_pairs={{0,2},{2,0},{4,6},{6,4},{8,10},{10,8},{12,14},{14,12},{16,18},{18,... | collective-permute-start | bytes 1572872 | tf_op jit(solution)/shard_map/ppermute | solution.py:387
  220.8 10.8 %collective-permute-start.20 = (bf16[256,3,512]{2,0,1:T(8,128)(2,1)S(1)}, bf16[256,3,512]{2,0,1:T(8,128)(2,1)S(1)}, u32[]{:S(2)}, u32[]{:S(2)}) collective-permute-start(bf16[256,3,512]{2,0,1:T(8,128)(2,1)S(1)} %constant_dynamic-slice_fusion.15), channel_id=1, source_target_pairs={{0,2},{2,0},{4,6},{6,4},{8,10},{10,8},{12,14},{14,12},{16,18},{18,... | collective-permute-start | bytes 2359304 | tf_op jit(solution)/shard_map/ppermute | solution.py:387
  221.4 12.0 %collective-permute-start.12 = (bf16[256,3,512]{2,0,1:T(8,128)(2,1)S(1)}, bf16[256,3,512]{2,0,1:T(8,128)(2,1)S(1)}, u32[]{:S(2)}, u32[]{:S(2)}) collective-permute-start(bf16[256,3,512]{2,0,1:T(8,128)(2,1)S(1)} %constant_dynamic-slice_fusion.19), channel_id=1, source_target_pairs={{0,2},{2,0},{4,6},{6,4},{8,10},{10,8},{12,14},{14,12},{16,18},{18,... | collective-permute-start | bytes 2359304 | tf_op jit(solution)/shard_map/ppermute | solution.py:387
  222.2 9.4 %copy-start.23 = (bf16[512,1024]{1,0:T(8,128)(2,1)S(1)}, bf16[512,1024]{1,0:T(8,128)(2,1)}, u32[]{:S(2)}) copy-start(bf16[512,1024]{1,0:T(8,128)(2,1)} %fusion.49) | copy-start | bytes 3145732
  222.2 8.8 %collective-permute-start.29 = (bf16[128,1024]{1,0:T(8,128)(2,1)S(1)}, bf16[128,1024]{1,0:T(8,128)(2,1)S(1)}, u32[]{:S(2)}, u32[]{:S(2)}) collective-permute-start(bf16[128,1024]{1,0:T(8,128)(2,1)S(1)} %constant_dynamic-slice_fusion.10), channel_id=1, source_target_pairs={{0,8},{2,10},{4,12},{6,14},{8,0},{10,2},{12,4},{14,6},{16,24},{18,... | collective-permute-start | bytes 786440 | tf_op jit(solution)/shard_map/ppermute | solution.py:387
  230.9 26.1 %collective-permute-start.9 = (bf16[512,1024]{1,0:T(8,128)(2,1)S(1)}, bf16[512,1024]{1,0:T(8,128)(2,1)S(1)}, u32[]{:S(2)}, u32[]{:S(2)}) collective-permute-start(bf16[512,1024]{1,0:T(8,128)(2,1)S(1)} %bitcast_convert_fusion), channel_id=1, source_target_pairs={{0,1},{1,0},{2,3},{3,2},{4,5},{5,4},{6,7},{7,6},{8,9},{9,8},{10,11... | collective-permute-start | bytes 3145736 | tf_op jit(solution)/shard_map/ppermute | solution.py:372
  231.6 46.6 %collective-permute-start.8 = (bf16[512,1024]{1,0:T(8,128)(2,1)S(1)}, bf16[512,1024]{1,0:T(8,128)(2,1)S(1)}, u32[]{:S(2)}, u32[]{:S(2)}) collective-permute-start(bf16[512,1024]{1,0:T(8,128)(2,1)S(1)} %copy-done.23), channel_id=1, source_target_pairs={{0,1},{1,0},{2,3},{3,2},{4,5},{5,4},{6,7},{7,6},{8,9},{9,8},{10,11... | collective-permute-start | bytes 3145736 | tf_op jit(solution)/shard_map/ppermute | solution.py:372
  233.4 10.4 %copy-start.9 = (bf16[256,3,512]{2,0,1:T(8,128)(2,1)}, bf16[256,3,512]{2,0,1:T(8,128)(2,1)S(1)}, u32[]{:S(2)}) copy-start(bf16[256,3,512]{2,0,1:T(8,128)(2,1)S(1)} %add_convert_fusion.8) | copy-start | bytes 2359300
  233.4 8.3 %collective-permute-start.30 = (bf16[64,1024]{1,0:T(8,128)(2,1)S(1)}, bf16[64,1024]{1,0:T(8,128)(2,1)S(1)}, u32[]{:S(2)}, u32[]{:S(2)}) collective-permute-start(bf16[64,1024]{1,0:T(8,128)(2,1)S(1)} %constant_dynamic-slice_fusion.9), channel_id=1, source_target_pairs={{0,16},{2,18},{4,20},{6,22},{8,24},{10,26},{12,28},{14,30},{16,0},... | collective-permute-start | bytes 393224 | tf_op jit(solution)/shard_map/ppermute | solution.py:387
  235.9 21.1 %copy-start.7 = (bf16[256,3,512]{2,0,1:T(8,128)(2,1)}, bf16[256,3,512]{2,0,1:T(8,128)(2,1)S(1)}, u32[]{:S(2)}) copy-start(bf16[256,3,512]{2,0,1:T(8,128)(2,1)S(1)} %add_convert_fusion.9) | copy-start | bytes 2359300
  241.8 4.3 collective-permute-start.31
  246.1 86.9 %collective-permute-start.21 = (bf16[128,3,512]{2,0,1:T(8,128)(2,1)}, bf16[128,3,512]{2,0,1:T(8,128)(2,1)}, u32[]{:S(2)}, u32[]{:S(2)}) collective-permute-start(bf16[128,3,512]{2,0,1:T(8,128)(2,1)} %constant_dynamic-slice_fusion.14), channel_id=1, source_target_pairs={{0,8},{2,10},{4,12},{6,14},{8,0},{10,2},{12,4},{14,6},{16,24},{18,... | collective-permute-start | bytes 1179656 | tf_op jit(solution)/shard_map/ppermute | solution.py:387
  257.0 4.4 collective-permute-start.32
  261.4 19.0 %copy-start.3 = (bf16[1,512,1024]{2,1,0:T(8,128)(2,1)S(1)}, bf16[1,512,1024]{2,1,0:T(8,128)(2,1)}, u32[]{:S(2)}) copy-start(bf16[1,512,1024]{2,1,0:T(8,128)(2,1)} %param.17) | copy-start | bytes 3145732
  261.4 19.0 %copy-start.11 = (f32[512,1024]{1,0:T(8,128)S(1)}, f32[512,1024]{1,0:T(8,128)}, u32[]{:S(2)}) copy-start(f32[512,1024]{1,0:T(8,128)} %fusion.34) | copy-start | bytes 6291460
  261.4 73.4 %collective-permute-start.13 = (bf16[128,3,512]{2,0,1:T(8,128)(2,1)}, bf16[128,3,512]{2,0,1:T(8,128)(2,1)}, u32[]{:S(2)}, u32[]{:S(2)}) collective-permute-start(bf16[128,3,512]{2,0,1:T(8,128)(2,1)} %constant_dynamic-slice_fusion.18), channel_id=1, source_target_pairs={{0,4},{2,6},{4,0},{6,2},{8,12},{10,14},{12,8},{14,10},{16,20},{18,... | collective-permute-start | bytes 1179656 | tf_op jit(solution)/shard_map/ppermute | solution.py:387
  278.2 53.6 %collective-permute-start.33 = (bf16[64,1024]{1,0:T(8,128)(2,1)S(1)}, bf16[64,1024]{1,0:T(8,128)(2,1)S(1)}, u32[]{:S(2)}, u32[]{:S(2)}) collective-permute-start(bf16[64,1024]{1,0:T(8,128)(2,1)S(1)} %maximum_select_fusion.19), channel_id=1, source_target_pairs={{0,16},{2,18},{4,20},{6,22},{8,24},{10,26},{12,28},{14,30},{16,0},... | collective-permute-start | bytes 393224 | tf_op jit(solution)/shard_map/ppermute | solution.py:391
  284.3 8.7 %collective-permute-start.10 = (bf16[6,512]{1,0:T(8,128)(2,1)S(1)}, bf16[6,512]{1,0:T(8,128)(2,1)S(1)}, u32[]{:S(2)}, u32[]{:S(2)}) collective-permute-start(bf16[6,512]{1,0:T(8,128)(2,1)S(1)} %select_convert_fusion), channel_id=1, source_target_pairs={{0,1},{1,0},{2,3},{3,2},{4,5},{5,4},{6,7},{7,6},{8,9},{9,8},{10,11... | collective-permute-start | bytes 18440 | tf_op jit(solution)/shard_map/ppermute | solution.py:372
  285.3 9.4 %slice-start = ((s8[6291456]{0:T(1024)(128)(4,1)}), s8[4194304]{0:T(1024)(128)(4,1)S(1)}, s32[]{:S(2)}) async-start(s8[6291456]{0:T(1024)(128)(4,1)} %bitcast.90), calls=%async_computation | async-start | bytes 8388608
  288.8 50.2 %collective-permute-start.45 = (bf16[512,1024]{1,0:T(8,128)(2,1)S(1)}, bf16[512,1024]{1,0:T(8,128)(2,1)S(1)}, u32[]{:S(2)}, u32[]{:S(2)}) collective-permute-start(bf16[512,1024]{1,0:T(8,128)(2,1)S(1)} %constant_dynamic-slice_fusion.2), channel_id=1, source_target_pairs={{0,4},{2,6},{4,0},{6,2},{8,12},{10,14},{12,8},{14,10},{16,20},{18,... | collective-permute-start | bytes 3145736 | tf_op jit(solution)/shard_map/ppermute | solution.py:387
  293.0 41.3 %collective-permute-start.37 = (bf16[256,2048]{1,0:T(8,128)(2,1)S(1)}, bf16[256,2048]{1,0:T(8,128)(2,1)S(1)}, u32[]{:S(2)}, u32[]{:S(2)}) collective-permute-start(bf16[256,2048]{1,0:T(8,128)(2,1)S(1)} %constant_dynamic-slice_fusion.6), channel_id=1, source_target_pairs={{0,8},{2,10},{4,12},{6,14},{8,0},{10,2},{12,4},{14,6},{16,24},{18,... | collective-permute-start | bytes 3145736 | tf_op jit(solution)/shard_map/ppermute | solution.py:387
  294.7 38.4 %copy-start.10 = (bf16[256,3,512]{2,0,1:T(8,128)(2,1)S(1)}, bf16[256,3,512]{2,0,1:T(8,128)(2,1)}, u32[]{:S(2)}) copy-start(bf16[256,3,512]{2,0,1:T(8,128)(2,1)} %copy-done.9) | copy-start | bytes 2359300
  331.8 166.7 %collective-permute-start.11 = (f32[1,1024]{1,0:T(1,128)S(1)}, f32[1,1024]{1,0:T(1,128)S(1)}, u32[]{:S(2)}, u32[]{:S(2)}) collective-permute-start(f32[1,1024]{1,0:T(1,128)S(1)} %convolution_bitcast_fusion), channel_id=1, source_target_pairs={{0,1},{1,0},{2,3},{3,2},{4,5},{5,4},{6,7},{7,6},{8,9},{9,8},{10,11... | collective-permute-start | bytes 12296 | tf_op jit(solution)/shard_map/ppermute | solution.py:372
  333.0 134.1 %collective-permute-start.34 = (bf16[128,1024]{1,0:T(8,128)(2,1)S(1)}, bf16[128,1024]{1,0:T(8,128)(2,1)S(1)}, u32[]{:S(2)}, u32[]{:S(2)}) collective-permute-start(bf16[128,1024]{1,0:T(8,128)(2,1)S(1)} %maximum_select_fusion.16), channel_id=1, source_target_pairs={{0,8},{2,10},{4,12},{6,14},{8,0},{10,2},{12,4},{14,6},{16,24},{18,... | collective-permute-start | bytes 786440 | tf_op jit(solution)/shard_map/ppermute | solution.py:391
  334.3 54.8 %collective-permute-start.22 = (bf16[64,3,512]{2,0,1:T(8,128)(2,1)S(1)}, bf16[64,3,512]{2,0,1:T(8,128)(2,1)S(1)}, u32[]{:S(2)}, u32[]{:S(2)}) collective-permute-start(bf16[64,3,512]{2,0,1:T(8,128)(2,1)S(1)} %constant_dynamic-slice_fusion.13), channel_id=1, source_target_pairs={{0,16},{2,18},{4,20},{6,22},{8,24},{10,26},{12,28},{14,30},{16,0},... | collective-permute-start | bytes 589832 | tf_op jit(solution)/shard_map/ppermute | solution.py:387
  334.8 34.0 %collective-permute-start.38 = (bf16[128,2048]{1,0:T(8,128)(2,1)S(1)}, bf16[128,2048]{1,0:T(8,128)(2,1)S(1)}, u32[]{:S(2)}, u32[]{:S(2)}) collective-permute-start(bf16[128,2048]{1,0:T(8,128)(2,1)S(1)} %constant_dynamic-slice_fusion.5), channel_id=1, source_target_pairs={{0,16},{2,18},{4,20},{6,22},{8,24},{10,26},{12,28},{14,30},{16,0},... | collective-permute-start | bytes 1572872 | tf_op jit(solution)/shard_map/ppermute | solution.py:387
  338.9 64.8 %collective-permute-start.14 = (bf16[64,3,512]{2,0,1:T(8,128)(2,1)S(1)}, bf16[64,3,512]{2,0,1:T(8,128)(2,1)S(1)}, u32[]{:S(2)}, u32[]{:S(2)}) collective-permute-start(bf16[64,3,512]{2,0,1:T(8,128)(2,1)S(1)} %constant_dynamic-slice_fusion.17), channel_id=1, source_target_pairs={{0,8},{2,10},{4,12},{6,14},{8,0},{10,2},{12,4},{14,6},{16,24},{18,... | collective-permute-start | bytes 589832 | tf_op jit(solution)/shard_map/ppermute | solution.py:387
  368.8 13.1 %collective-permute-start.46 = (bf16[256,1024]{1,0:T(8,128)(2,1)S(1)}, bf16[256,1024]{1,0:T(8,128)(2,1)S(1)}, u32[]{:S(2)}, u32[]{:S(2)}) collective-permute-start(bf16[256,1024]{1,0:T(8,128)(2,1)S(1)} %constant_dynamic-slice_fusion.1), channel_id=1, source_target_pairs={{0,8},{2,10},{4,12},{6,14},{8,0},{10,2},{12,4},{14,6},{16,24},{18,... | collective-permute-start | bytes 1572872 | tf_op jit(solution)/shard_map/ppermute | solution.py:387
  381.9 6.5 %collective-permute-start.39 = (bf16[64,2048]{1,0:T(8,128)(2,1)S(1)}, bf16[64,2048]{1,0:T(8,128)(2,1)S(1)}, u32[]{:S(2)}, u32[]{:S(2)}) collective-permute-start(bf16[64,2048]{1,0:T(8,128)(2,1)S(1)} %constant_dynamic-slice_fusion.4), channel_id=1, source_target_pairs={{0,4},{2,6},{4,0},{6,2},{8,12},{10,14},{12,8},{14,10},{16,20},{18,... | collective-permute-start | bytes 786440 | tf_op jit(solution)/shard_map/ppermute | solution.py:387
  388.4 12.1 %collective-permute-start.47 = (bf16[128,1024]{1,0:T(8,128)(2,1)S(1)}, bf16[128,1024]{1,0:T(8,128)(2,1)S(1)}, u32[]{:S(2)}, u32[]{:S(2)}) collective-permute-start(bf16[128,1024]{1,0:T(8,128)(2,1)S(1)} %constant_dynamic-slice_fusion), channel_id=1, source_target_pairs={{0,16},{2,18},{4,20},{6,22},{8,24},{10,26},{12,28},{14,30},{16,0},... | collective-permute-start | bytes 786440 | tf_op jit(solution)/shard_map/ppermute | solution.py:387
  389.0 11.6 %collective-permute-start.40 = (bf16[64,2048]{1,0:T(8,128)(2,1)S(1)}, bf16[64,2048]{1,0:T(8,128)(2,1)S(1)}, u32[]{:S(2)}, u32[]{:S(2)}) collective-permute-start(bf16[64,2048]{1,0:T(8,128)(2,1)S(1)} %add_convert_fusion.16), channel_id=1, source_target_pairs={{0,4},{2,6},{4,0},{6,2},{8,12},{10,14},{12,8},{14,10},{16,20},{18,... | collective-permute-start | bytes 786440 | tf_op jit(solution)/shard_map/ppermute | solution.py:391
  400.6 24.2 %collective-permute-start.48 = (bf16[128,1024]{1,0:T(8,128)(2,1)S(1)}, bf16[128,1024]{1,0:T(8,128)(2,1)S(1)}, u32[]{:S(2)}, u32[]{:S(2)}) collective-permute-start(bf16[128,1024]{1,0:T(8,128)(2,1)S(1)} %add_convert_fusion.15), channel_id=1, source_target_pairs={{0,16},{2,18},{4,20},{6,22},{8,24},{10,26},{12,28},{14,30},{16,0},... | collective-permute-start | bytes 786440 | tf_op jit(solution)/shard_map/ppermute | solution.py:391
  400.8 35.2 %collective-permute-start.41 = (bf16[128,2048]{1,0:T(8,128)(2,1)S(1)}, bf16[128,2048]{1,0:T(8,128)(2,1)S(1)}, u32[]{:S(2)}, u32[]{:S(2)}) collective-permute-start(bf16[128,2048]{1,0:T(8,128)(2,1)S(1)} %maximum_select_fusion.12), channel_id=1, source_target_pairs={{0,16},{2,18},{4,20},{6,22},{8,24},{10,26},{12,28},{14,30},{16,0},... | collective-permute-start | bytes 1572872 | tf_op jit(solution)/shard_map/ppermute | solution.py:391
  403.8 32.5 %collective-permute-start.23 = (bf16[32,3,512]{2,0,1:T(8,128)(2,1)S(1)}, bf16[32,3,512]{2,0,1:T(8,128)(2,1)S(1)}, u32[]{:S(2)}, u32[]{:S(2)}) collective-permute-start(bf16[32,3,512]{2,0,1:T(8,128)(2,1)S(1)} %constant_dynamic-slice_fusion.12), channel_id=1, source_target_pairs={{0,4},{2,6},{4,0},{6,2},{8,12},{10,14},{12,8},{14,10},{16,20},{18,... | collective-permute-start | bytes 294920 | tf_op jit(solution)/shard_map/ppermute | solution.py:387
  424.9 24.4 %collective-permute-start.49 = (bf16[256,1024]{1,0:T(8,128)(2,1)S(1)}, bf16[256,1024]{1,0:T(8,128)(2,1)S(1)}, u32[]{:S(2)}, u32[]{:S(2)}) collective-permute-start(bf16[256,1024]{1,0:T(8,128)(2,1)S(1)} %maximum_select_fusion.13), channel_id=1, source_target_pairs={{0,8},{2,10},{4,12},{6,14},{8,0},{10,2},{12,4},{14,6},{16,24},{18,... | collective-permute-start | bytes 1572872 | tf_op jit(solution)/shard_map/ppermute | solution.py:391
  436.0 14.7 %collective-permute-start.15 = (bf16[32,3,512]{2,0,1:T(8,128)(2,1)S(1)}, bf16[32,3,512]{2,0,1:T(8,128)(2,1)S(1)}, u32[]{:S(2)}, u32[]{:S(2)}) collective-permute-start(bf16[32,3,512]{2,0,1:T(8,128)(2,1)S(1)} %constant_dynamic-slice_fusion.16), channel_id=1, source_target_pairs={{0,16},{2,18},{4,20},{6,22},{8,24},{10,26},{12,28},{14,30},{16,0},... | collective-permute-start | bytes 294920 | tf_op jit(solution)/shard_map/ppermute | solution.py:387
  436.3 46.1 %collective-permute-start.42 = (bf16[256,2048]{1,0:T(8,128)(2,1)S(1)}, bf16[256,2048]{1,0:T(8,128)(2,1)S(1)}, u32[]{:S(2)}, u32[]{:S(2)}) collective-permute-start(bf16[256,2048]{1,0:T(8,128)(2,1)S(1)} %maximum_select_fusion.7), channel_id=1, source_target_pairs={{0,8},{2,10},{4,12},{6,14},{8,0},{10,2},{12,4},{14,6},{16,24},{18,... | collective-permute-start | bytes 3145736 | tf_op jit(solution)/shard_map/ppermute | solution.py:391
  449.4 5.6 %collective-permute-start.24 = (bf16[32,3,512]{2,0,1:T(8,128)(2,1)S(1)}, bf16[32,3,512]{2,0,1:T(8,128)(2,1)S(1)}, u32[]{:S(2)}, u32[]{:S(2)}) collective-permute-start(bf16[32,3,512]{2,0,1:T(8,128)(2,1)S(1)} %add_convert_fusion.21), channel_id=1, source_target_pairs={{0,4},{2,6},{4,0},{6,2},{8,12},{10,14},{12,8},{14,10},{16,20},{18,... | collective-permute-start | bytes 294920 | tf_op jit(solution)/shard_map/ppermute | solution.py:391
  450.7 43.8 %collective-permute-start.50 = (bf16[512,1024]{1,0:T(8,128)(2,1)S(1)}, bf16[512,1024]{1,0:T(8,128)(2,1)S(1)}, u32[]{:S(2)}, u32[]{:S(2)}) collective-permute-start(bf16[512,1024]{1,0:T(8,128)(2,1)S(1)} %maximum_select_fusion.8), channel_id=1, source_target_pairs={{0,4},{2,6},{4,0},{6,2},{8,12},{10,14},{12,8},{14,10},{16,20},{18,... | collective-permute-start | bytes 3145736 | tf_op jit(solution)/shard_map/ppermute | solution.py:391
  455.0 8.7 %collective-permute-start.16 = (bf16[32,3,512]{2,0,1:T(8,128)(2,1)S(1)}, bf16[32,3,512]{2,0,1:T(8,128)(2,1)S(1)}, u32[]{:S(2)}, u32[]{:S(2)}) collective-permute-start(bf16[32,3,512]{2,0,1:T(8,128)(2,1)S(1)} %add_convert_fusion.22), channel_id=1, source_target_pairs={{0,16},{2,18},{4,20},{6,22},{8,24},{10,26},{12,28},{14,30},{16,0},... | collective-permute-start | bytes 294920 | tf_op jit(solution)/shard_map/ppermute | solution.py:391
  463.7 11.3 %collective-permute-start.25 = (bf16[64,3,512]{2,0,1:T(8,128)(2,1)S(1)}, bf16[64,3,512]{2,0,1:T(8,128)(2,1)S(1)}, u32[]{:S(2)}, u32[]{:S(2)}) collective-permute-start(bf16[64,3,512]{2,0,1:T(8,128)(2,1)S(1)} %maximum_select_fusion.18), channel_id=1, source_target_pairs={{0,16},{2,18},{4,20},{6,22},{8,24},{10,26},{12,28},{14,30},{16,0},... | collective-permute-start | bytes 589832 | tf_op jit(solution)/shard_map/ppermute | solution.py:391
  467.1 15.2 %collective-permute-start.17 = (bf16[64,3,512]{2,0,1:T(8,128)(2,1)S(1)}, bf16[64,3,512]{2,0,1:T(8,128)(2,1)S(1)}, u32[]{:S(2)}, u32[]{:S(2)}) collective-permute-start(bf16[64,3,512]{2,0,1:T(8,128)(2,1)S(1)} %maximum_select_fusion.17), channel_id=1, source_target_pairs={{0,8},{2,10},{4,12},{6,14},{8,0},{10,2},{12,4},{14,6},{16,24},{18,... | collective-permute-start | bytes 589832 | tf_op jit(solution)/shard_map/ppermute | solution.py:391
  475.0 31.9 %collective-permute-start.35 = (bf16[256,1024]{1,0:T(8,128)(2,1)}, bf16[256,1024]{1,0:T(8,128)(2,1)}, u32[]{:S(2)}, u32[]{:S(2)}) collective-permute-start(bf16[256,1024]{1,0:T(8,128)(2,1)} %maximum_select_fusion.11), channel_id=1, source_target_pairs={{0,2},{2,0},{4,6},{6,4},{8,10},{10,8},{12,14},{14,12},{16,18},{18,... | collective-permute-start | bytes 1572872 | tf_op jit(solution)/shard_map/ppermute | solution.py:391
  482.3 11.0 %collective-permute-start.26 = (bf16[128,3,512]{2,0,1:T(8,128)(2,1)S(1)}, bf16[128,3,512]{2,0,1:T(8,128)(2,1)S(1)}, u32[]{:S(2)}, u32[]{:S(2)}) collective-permute-start(bf16[128,3,512]{2,0,1:T(8,128)(2,1)S(1)} %maximum_select_fusion.15), channel_id=1, source_target_pairs={{0,8},{2,10},{4,12},{6,14},{8,0},{10,2},{12,4},{14,6},{16,24},{18,... | collective-permute-start | bytes 1179656 | tf_op jit(solution)/shard_map/ppermute | solution.py:391
  482.4 14.9 %collective-permute-start.18 = (bf16[128,3,512]{2,0,1:T(8,128)(2,1)S(1)}, bf16[128,3,512]{2,0,1:T(8,128)(2,1)S(1)}, u32[]{:S(2)}, u32[]{:S(2)}) collective-permute-start(bf16[128,3,512]{2,0,1:T(8,128)(2,1)S(1)} %maximum_select_fusion.14), channel_id=1, source_target_pairs={{0,4},{2,6},{4,0},{6,2},{8,12},{10,14},{12,8},{14,10},{16,20},{18,... | collective-permute-start | bytes 1179656 | tf_op jit(solution)/shard_map/ppermute | solution.py:391
  493.3 25.4 %collective-permute-start.43 = (bf16[512,2048]{1,0:T(8,128)(2,1)}, bf16[512,2048]{1,0:T(8,128)(2,1)}, u32[]{:S(2)}, u32[]{:S(2)}) collective-permute-start(bf16[512,2048]{1,0:T(8,128)(2,1)} %maximum_select_fusion.2), channel_id=1, source_target_pairs={{0,2},{2,0},{4,6},{6,4},{8,10},{10,8},{12,14},{14,12},{16,18},{18,... | collective-permute-start | bytes 6291464 | tf_op jit(solution)/shard_map/ppermute | solution.py:391
  494.5 15.8 %collective-permute-start.27 = (bf16[256,3,512]{2,0,1:T(8,128)(2,1)}, bf16[256,3,512]{2,0,1:T(8,128)(2,1)}, u32[]{:S(2)}, u32[]{:S(2)}) collective-permute-start(bf16[256,3,512]{2,0,1:T(8,128)(2,1)} %maximum_select_fusion.10), channel_id=1, source_target_pairs={{0,2},{2,0},{4,6},{6,4},{8,10},{10,8},{12,14},{14,12},{16,18},{18,... | collective-permute-start | bytes 2359304 | tf_op jit(solution)/shard_map/ppermute | solution.py:391
  497.3 28.2 %collective-permute-start.51 = (bf16[1024,1024]{1,0:T(8,128)(2,1)}, bf16[1024,1024]{1,0:T(8,128)(2,1)}, u32[]{:S(2)}, u32[]{:S(2)}) collective-permute-start(bf16[1024,1024]{1,0:T(8,128)(2,1)} %maximum_select_fusion.3), channel_id=1, source_target_pairs={{0,2},{2,0},{4,6},{6,4},{8,10},{10,8},{12,14},{14,12},{16,18},{18,... | collective-permute-start | bytes 6291464 | tf_op jit(solution)/shard_map/ppermute | solution.py:391
  498.5 14.1 %collective-permute-start.19 = (bf16[256,3,512]{2,0,1:T(8,128)(2,1)}, bf16[256,3,512]{2,0,1:T(8,128)(2,1)}, u32[]{:S(2)}, u32[]{:S(2)}) collective-permute-start(bf16[256,3,512]{2,0,1:T(8,128)(2,1)} %maximum_select_fusion.9), channel_id=1, source_target_pairs={{0,2},{2,0},{4,6},{6,4},{8,10},{10,8},{12,14},{14,12},{16,18},{18,... | collective-permute-start | bytes 2359304 | tf_op jit(solution)/shard_map/ppermute | solution.py:391
  (15 other events, 52.7 us)

commit v3 on v2

--- a/solution.py
+++ b/solution.py
@@ -397,6 +397,19 @@
     return part.astype(jnp.float32)
 
 
+def gather_latents(values_in):
+    count = lax.axis_size("dp")
+    if count & (count - 1) != 0:
+        return lax.all_gather(values_in, "dp", axis=0, tiled=True)
+    bit = 1
+    while bit < count:
+        partners = [(i, i ^ bit) for i in range(count)]
+        came = lax.ppermute(values_in, "dp", partners)
+        values_in = jnp.concatenate((values_in, came), axis=0)
+        bit *= 2
+    return values_in
+
+
 Y_FIRST = (1, 2, 4, 8)
 Z_FIRST = (1, 4, 8, 2)
 
@@ -492,8 +505,7 @@
     grad_down = dot_f32(hidden_act, grad_mlp, TN).astype(bf16)
     grad_up = dot_f32(normed_two, grad_pre, TN).astype(bf16)
     grad_down, grad_up, two_recv = lax.optimization_barrier((grad_down, grad_up, two_recv))
-    sum_down = sum_latents(grad_down, Y_FIRST)
-    sum_up = sum_latents(grad_up, Z_FIRST)
+    sum_down, sum_up = lax.psum((grad_down, grad_up), "dp")
     grad_normed_two = two_own + two_recv.astype(jnp.float32)
     middle_back, grad_shift_two, grad_scale_two = back_two(grad_normed_two)
     grad_middle = grad_out + middle_back
@@ -548,11 +560,8 @@
     mod_keep = jnp.where(mine == 0, left, right)
     mod_send = jnp.where(mine == 0, right, left).astype(bf16)
     grad_mod = (mod_keep + swap(mod_send).astype(jnp.float32)).astype(bf16)[None]
-    factors = lax.all_gather(
-        jnp.concatenate((cond_act, grad_mod.reshape(1, 6 * local_cols)), axis=1),
-        "dp",
-        axis=0,
-        tiled=True,
+    factors = gather_latents(
+        jnp.concatenate((cond_act, grad_mod.reshape(1, 6 * local_cols)), axis=1)
     )
     cond_all = factors[:, :width]
     mod_all = factors[:, width:].reshape(-1, 6, local_cols)
@@ -572,8 +581,8 @@
         grad_mod_bias,
         sum_qkv,
         sum_out,
-        sum_up,
-        sum_down,
+        sum_up.astype(jnp.float32),
+        sum_down.astype(jnp.float32),
     )
 
 

time: 536 us -> 425 us (0.79)
  waiting for transfers between devices: 220 us -> 156 us
  blocking collectives: 35.2 us -> 0 us
  between operations: 1.86 us -> 15.4 us
  other arithmetic: 69.8 us -> 57.3 us
  starting transfers between devices: 48 us -> 39.1 us
  matrix products: 96.8 us -> 90.4 us
    ppermute x20 -> x12, waiting for transfers between devices: 74.1 us -> 37.2 us  [sum_latents(): came = lax.ppermute(part, 'dp', partners)]
    all_gather x1 -> x0, blocking collectives: 35.2 us -> none  [body_pair(): lax.all_gather(jnp.concatenate((cond_act, grad_mod.reshape(1, 6 * local_c...]
    ppermute x20 -> x12, waiting for transfers between devices: 70.7 us -> 37.6 us  [sum_latents(): came = lax.ppermute(sent, 'dp', partners)]
    convert_element_type x3 -> x1, other arithmetic: 16.6 us -> 1.76 us  [sum_latents(): return part.astype(jnp.float32)]
    convert_element_type x0 -> x2, other arithmetic: none -> 11.2 us  [the longest x1 6.81 us: body_pair(): sum_up.astype(jnp.float32)]
    dot_general x11, matrix products: 69.2 us -> 61.7 us  [dot_f32(): lax.dot_general(left, right, (dims, ((), ())), preferred_element_type=jnp...]
    convert_element_type x20 -> x12, other arithmetic: 10.3 us -> 3.16 us  [sum_latents(): (kept.astype(jnp.float32) + came.astype(jnp.float32)).astype(jnp.bfloat16)]
    ppermute x20 -> x12, starting transfers between devices: 17.8 us -> 10.8 us  [sum_latents(): came = lax.ppermute(part, 'dp', partners)]
  transfers between devices with their start and end apart: 52 -> 41, of which waited for: 21 -> 21; matrix products, arithmetic and copies ran while one was open for 25% -> 26% of each run, Pallas kernels for 9% -> 11%
where the time goes in v3:
time: 425 us; the launch traced here: 421 us
  waiting for transfers between devices  156 us (37%)
  matrix products  90.4 us (21%)
  other arithmetic  57.3 us (13%)
  Pallas kernels  47.5 us (11%)
  starting transfers between devices  39.1 us (9%)
  local copies, waits for them, and re-layouts  15.5 us (4%)
  between operations  15.4 us (4%)
    ppermute x12, waiting for transfers between devices, swap(): return lax.ppermute(values_in, 'tensor', ((0, 1), (1, 0)))  80.9 us
    dot_general x11, matrix products, dot_f32(): lax.dot_general(left, right, (dims, ((), ())), preferred_element_type=jnp...  61.7 us
    ppermute x12, waiting for transfers between devices, sum_latents(): came = lax.ppermute(sent, 'dp', partners)  37.6 us
    ppermute x12, waiting for transfers between devices, sum_latents(): came = lax.ppermute(part, 'dp', partners)  37.2 us
    pallas_call x1, Pallas kernels, attn_backward(): pl.pallas_call(attn_bwd_kernel, grid=(pairs,), in_specs=[pl.BlockSpec((3,...  29.9 us
    pallas_call x2, Pallas kernels, attn_forward(): pl.pallas_call(attn_fwd_kernel, grid=(pairs,), in_specs=[pl.BlockSpec((3,...  17.5 us
    ppermute x12, starting transfers between devices, swap(): return lax.ppermute(values_in, 'tensor', ((0, 1), (1, 0)))  13.5 us
    ppermute x12, starting transfers between devices, sum_latents(): came = lax.ppermute(sent, 'dp', partners)  12.1 us
  transfers between devices with their start and end apart: 41, of which 21 were waited for; matrix products, arithmetic and copies ran while one was open for 26% of the time, Pallas kernels for 11%

profile of v3, /device:TPU:0, one launch (start us, length us, event | category | flops | bytes accessed | tf_op | source)
XLA Modules:
  0.0 420.8 jit_solution(8861078455092139584)
XLA Ops:
  8.7 3.7 fusion.69
  12.4 3.0 collective-permute-start
  17.0 1.6 fusion.22
  18.7 21.7 %collective-permute-done.1 = bf16[512,1024]{1,0:T(8,128)(2,1)} collective-permute-done((bf16[512,1024]{1,0:T(8,128)(2,1)}, bf16[512,1024]{1,0:T(8,128)(2,1)}, u32[]{:S(2)}, u32[]{:S(2)}) %collective-permute-start.1) | collective-permute-done | bytes 1048608 | tf_op jit(solution)/shard_map/ppermute | solution.py:372
  41.8 1.6 fusion.18
  44.1 2.4 fusion.16
  47.8 4.6 %convert_bitcast_fusion.qkv_ref = bf16[3,1024,512]{2,1,0:T(8,128)(2,1)S(1)} fusion(bf16[1024,3,512]{2,0,1:T(8,128)(2,1)S(1)} %copy-done, bf16[512,1024]{1,0:T(8,128)(2,1)S(1)} %get-tuple-element.63, bf16[512,1024]{1,0:T(8,128)(2,1)S(1)} %get-tuple-element.62), kind=kOutput, calls=%fused_computation.18 | convolution fusion | flops 3226992640 | bytes 8388608 | tf_op jit(solution)/shard_map/sd,dkc->ksc/dot_general | solution.py:468
  52.4 8.7 %attn_fwd.2 = (bf16[1024,256]{1,0:T(8,128)(2,1)}, f32[2,8,1024]{2,1,0:T(8,128)S(1)}) custom-call(bf16[3,1024,512]{2,1,0:T(8,128)(2,1)S(1)} %convert_bitcast_fusion.qkv_ref), custom_call_target="tpu_custom_call" | custom-call | flops 4294967296 | bytes 2097152 | tf_op jit(solution)/shard_map/attn_fwd/pallas_call | solution.py:326
  62.6 8.9 %attn_fwd.3 = (bf16[1024,256]{1,0:T(8,128)(2,1)}, f32[2,8,1024]{2,1,0:T(8,128)S(1)}) custom-call(bf16[3,1024,512]{2,1,0:T(8,128)(2,1)S(1)} %convert_bitcast_fusion.qkv_ref), custom_call_target="tpu_custom_call" | custom-call | flops 4294967296 | bytes 2097152 | tf_op jit(solution)/shard_map/attn_fwd/pallas_call | solution.py:326
  73.6 7.6 %collective-permute-done.2 = bf16[1024,256]{1,0:T(8,128)(2,1)} collective-permute-done((bf16[1024,256]{1,0:T(8,128)(2,1)}, bf16[1024,256]{1,0:T(8,128)(2,1)}, u32[]{:S(2)}, u32[]{:S(2)}) %collective-permute-start.2) | collective-permute-done | bytes 524320 | tf_op jit(solution)/shard_map/ppermute | solution.py:372
  82.3 10.2 %collective-permute-done.3 = bf16[1024,256]{1,0:T(8,128)(2,1)} collective-permute-done((bf16[1024,256]{1,0:T(8,128)(2,1)}, bf16[1024,256]{1,0:T(8,128)(2,1)}, u32[]{:S(2)}, u32[]{:S(2)}) %collective-permute-start.3) | collective-permute-done | bytes 524320 | tf_op jit(solution)/shard_map/ppermute | solution.py:372
  93.6 4.2 fusion.34
  97.8 2.4 fusion.61
  100.2 1.8 multiply_reduce_fusion.3
  102.0 2.5 fusion.84
  107.4 9.1 %multiply_convert_fusion = (bf16[1024,2048]{1,0:T(8,128)(2,1)S(1)}, f32[1024,2048]{1,0:T(8,128)}) fusion(bf16[1024,2048]{1,0:T(8,128)(2,1)S(1)} %copy-done.31, bf16[512,1024]{1,0:T(8,128)(2,1)S(1)} %get-tuple-element.49, bf16[512,1024]{1,0:T(8,128)(2,1)S(1)} %add_convert_fusion.3), kind=kOutput, calls=%fused_computation.9 | convolution fusion | flops 4318035968 | bytes 18874368 | tf_op jit(solution)/shard_map/dot_general | solution.py:418
  117.1 3.1 copy-done.32
  120.2 12.4 %fusion.6 = bf16[1024,2048]{1,0:T(8,128)(2,1)S(1)} fusion(f32[1024,2048]{1,0:T(8,128)} %get-tuple-element.67, bf16[2048,1024]{1,0:T(8,128)(2,1)S(1)} %copy-done.32, bf16[512,1024]{1,0:T(8,128)(2,1)S(1)} %get-tuple-element.65, bf16[512,1024]{1,0:T(8,128)(2,1)S(1)} %get-tuple-element.64), kind=kOutput, calls=%fused_computation.8 | convolution fusion | flops 4341104640 | bytes 18874368 | tf_op jit(solution)/shard_map/dot_general | solution.py:418
  132.6 3.3 fusion.50
  136.5 6.1 %convolution_convert_fusion = bf16[1024,2048]{1,0:T(8,128)(2,1)} fusion(bf16[1024,2048]{1,0:T(8,128)(2,1)S(1)} %fusion.6, bf16[512,1024]{1,0:T(8,128)(2,1)S(1)} %get-tuple-element.49, bf16[512,1024]{1,0:T(8,128)(2,1)S(1)} %add_convert_fusion.3), kind=kOutput, calls=%fused_computation.10 | convolution fusion | flops 4301258752 | bytes 10485760 | tf_op jit(solution)/shard_map/dot_general | solution.py:418
  142.7 6.4 %convolution_convert_fusion.1 = bf16[2048,1024]{1,0:T(8,128)(2,1)} fusion(bf16[1024,2048]{1,0:T(8,128)(2,1)S(1)} %get-tuple-element.66, bf16[512,1024]{1,0:T(8,128)(2,1)S(1)} %get-tuple-element.65, bf16[512,1024]{1,0:T(8,128)(2,1)S(1)} %get-tuple-element.64), kind=kOutput, calls=%fused_computation.11 | convolution fusion | flops 4301258752 | bytes 10485760 | tf_op jit(solution)/shard_map/dot_general | solution.py:418
  149.1 7.6 %collective-permute-done.6 = bf16[512,1024]{1,0:T(8,128)(2,1)} collective-permute-done((bf16[512,1024]{1,0:T(8,128)(2,1)}, bf16[512,1024]{1,0:T(8,128)(2,1)}, u32[]{:S(2)}, u32[]{:S(2)}) %collective-permute-start.6) | collective-permute-done | bytes 1048608 | tf_op jit(solution)/shard_map/ppermute | solution.py:372
  156.7 6.7 %multiply_reduce_fusion = (f32[1024]{0:T(1024)S(1)}, f32[512]{0:T(512)S(1)}, f32[1024]{0:T(1024)S(1)}, f32[512,1024]{1,0:T(8,128)S(1)}) fusion(f32[512,1024]{1,0:T(8,128)} %copy-done.2, f32[512]{0:T(512)S(1)} %fusion.72, f32[512]{0:T(512)S(1)} %broadcast_multiply_fusion.1, bf16[512,1024]{1,0:T(8,128)(2,1)} %collective-permute-done.6, ...), kind=kOutput, calls=%fused_computation.71 | convolution fusion | flops 2152723968 | bytes 11552768 | tf_op jit(solution)/shard_map/dot_general | solution.py:418
  163.4 2.2 fusion.83
  169.1 3.3 fusion.47
  172.5 3.7 fusion.32
  176.2 11.5 %collective-permute-done.7 = bf16[512,1024]{1,0:T(8,128)(2,1)} collective-permute-done((bf16[512,1024]{1,0:T(8,128)(2,1)}, bf16[512,1024]{1,0:T(8,128)(2,1)}, u32[]{:S(2)}, u32[]{:S(2)}) %collective-permute-start.7) | collective-permute-done | bytes 1048608 | tf_op jit(solution)/shard_map/ppermute | solution.py:372
  187.7 3.2 convolution_convert_fusion.3
  191.0 3.2 convolution_convert_fusion.4.grad_ref
  194.3 29.9 %attn_bwd.1 = bf16[3,1024,512]{2,1,0:T(8,128)(2,1)S(1)} custom-call(bf16[3,1024,512]{2,1,0:T(8,128)(2,1)} %copy-done.1, bf16[1024,512]{1,0:T(8,128)(2,1)S(1)} %convolution_convert_fusion.4.grad_ref, f32[4,8,1024]{2,1,0:T(8,128)S(1)} %pad_maximum_fusion.11.lse_ref), custom_call_target="tpu_custom_call" | custom-call | flops 21474836480 | bytes 7340032 | tf_op jit(solution)/shard_map/attn_bwd/pallas_call | solution.py:351
  224.3 4.0 convolution_convert_fusion.2
  230.4 1.8 bitcast_convert_fusion
  234.4 8.8 %collective-permute-done.33 = bf16[128,1024]{1,0:T(8,128)(2,1)S(1)} collective-permute-done((bf16[128,1024]{1,0:T(8,128)(2,1)S(1)}, bf16[128,1024]{1,0:T(8,128)(2,1)S(1)}, u32[]{:S(2)}, u32[]{:S(2)}) %collective-permute-start.33) | collective-permute-done | bytes 262176 | tf_op jit(solution)/shard_map/ppermute | solution.py:387
  243.2 2.5 collective-permute-start.34
  249.9 2.2 collective-permute-done.34
  252.2 6.1 %collective-permute-done.9 = bf16[512,1024]{1,0:T(8,128)(2,1)S(1)} collective-permute-done((bf16[512,1024]{1,0:T(8,128)(2,1)S(1)}, bf16[512,1024]{1,0:T(8,128)(2,1)S(1)}, u32[]{:S(2)}, u32[]{:S(2)}) %collective-permute-start.9) | collective-permute-done | bytes 1048608 | tf_op jit(solution)/shard_map/ppermute | solution.py:372
  258.4 3.4 fusion.23
  261.8 2.4 fusion.17
  264.3 15.5 %collective-permute-done.8 = bf16[512,1024]{1,0:T(8,128)(2,1)S(1)} collective-permute-done((bf16[512,1024]{1,0:T(8,128)(2,1)S(1)}, bf16[512,1024]{1,0:T(8,128)(2,1)S(1)}, u32[]{:S(2)}, u32[]{:S(2)}) %collective-permute-start.8) | collective-permute-done | bytes 1048608 | tf_op jit(solution)/shard_map/ppermute | solution.py:372
  279.8 4.1 fusion.25
  287.8 3.3 collective-permute-done.35
  293.4 2.1 collective-permute-done.36
  295.5 2.7 collective-permute-start.37
  298.8 4.6 %convolution_bitcast_fusion = f32[1,1024]{1,0:T(1,128)S(1)} fusion(bf16[1024,6,512]{2,0,1:T(8,128)(2,1)} %param.11, bf16[6,512,1]{1,0,2:T(8,128)(2,1)S(1)} %bitcast.96), kind=kOutput, calls=%fused_computation.96 | convolution fusion | flops 6291456 | bytes 6301696 | tf_op jit(solution)/shard_map/lkc,dkc->ld/dot_general | solution.py:572
  306.4 1.9 collective-permute-start.26
  309.4 1.7 collective-permute-start.18
  311.1 9.3 %collective-permute-done.26 = bf16[64,3,512]{2,0,1:T(8,128)(2,1)S(1)} collective-permute-done((bf16[64,3,512]{2,0,1:T(8,128)(2,1)S(1)}, bf16[64,3,512]{2,0,1:T(8,128)(2,1)S(1)}, u32[]{:S(2)}, u32[]{:S(2)}) %collective-permute-start.26) | collective-permute-done | bytes 196640 | tf_op jit(solution)/shard_map/ppermute | solution.py:387
  321.0 3.6 collective-permute-done.18
  325.0 2.2 collective-permute-done.27
  327.3 8.2 %collective-permute-done.19 = bf16[32,3,512]{2,0,1:T(8,128)(2,1)S(1)} collective-permute-done((bf16[32,3,512]{2,0,1:T(8,128)(2,1)S(1)}, bf16[32,3,512]{2,0,1:T(8,128)(2,1)S(1)}, u32[]{:S(2)}, u32[]{:S(2)}) %collective-permute-start.19) | collective-permute-done | bytes 98336 | tf_op jit(solution)/shard_map/ppermute | solution.py:387
  335.7 3.0 collective-permute-start.29
  338.6 7.2 %collective-permute-done.20 = bf16[32,3,512]{2,0,1:T(8,128)(2,1)S(1)} collective-permute-done((bf16[32,3,512]{2,0,1:T(8,128)(2,1)S(1)}, bf16[32,3,512]{2,0,1:T(8,128)(2,1)S(1)}, u32[]{:S(2)}, u32[]{:S(2)}) %collective-permute-start.20) | collective-permute-done | bytes 98336 | tf_op jit(solution)/shard_map/ppermute | solution.py:391
  346.7 2.0 collective-permute-start.38
  348.7 5.4 %collective-permute-done.29 = bf16[64,3,512]{2,0,1:T(8,128)(2,1)S(1)} collective-permute-done((bf16[64,3,512]{2,0,1:T(8,128)(2,1)S(1)}, bf16[64,3,512]{2,0,1:T(8,128)(2,1)S(1)}, u32[]{:S(2)}, u32[]{:S(2)}) %collective-permute-start.29) | collective-permute-done | bytes 196640 | tf_op jit(solution)/shard_map/ppermute | solution.py:391
  354.4 4.9 %collective-permute-done.21 = bf16[64,3,512]{2,0,1:T(8,128)(2,1)S(1)} collective-permute-done((bf16[64,3,512]{2,0,1:T(8,128)(2,1)S(1)}, bf16[64,3,512]{2,0,1:T(8,128)(2,1)S(1)}, u32[]{:S(2)}, u32[]{:S(2)}) %collective-permute-start.21) | collective-permute-done | bytes 196640 | tf_op jit(solution)/shard_map/ppermute | solution.py:391
  361.7 3.0 concatenate.152
  366.2 4.3 %collective-permute-done.38 = bf16[128,1024]{1,0:T(8,128)(2,1)} collective-permute-done((bf16[128,1024]{1,0:T(8,128)(2,1)}, bf16[128,1024]{1,0:T(8,128)(2,1)}, u32[]{:S(2)}, u32[]{:S(2)}) %collective-permute-start.38) | collective-permute-done | bytes 262176 | tf_op jit(solution)/shard_map/ppermute | solution.py:391
  372.1 13.2 %collective-permute-done.30 = bf16[128,3,512]{2,0,1:T(8,128)(2,1)} collective-permute-done((bf16[128,3,512]{2,0,1:T(8,128)(2,1)S(1)}, bf16[128,3,512]{2,0,1:T(8,128)(2,1)}, u32[]{:S(2)}, u32[]{:S(2)}) %collective-permute-start.30) | collective-permute-done | bytes 393248 | tf_op jit(solution)/shard_map/ppermute | solution.py:391
  386.7 1.7 maximum_select_fusion.3
  389.0 6.6 %fusion.63 = f32[1024,6,512]{2,0,1:T(8,128)} fusion(bf16[2,6,8,512]{3,2,1,0:T(8,128)(2,1)S(1)} %bitcast.86, bf16[16,4096]{1,0:T(8,128)(2,1)S(1)} %copy-done.22), kind=kOutput, calls=%fused_computation.127 | convolution fusion | flops 100663296 | bytes 12713984 | tf_op jit(solution)/shard_map/ld,lkc->dkc/dot_general | solution.py:568
  395.6 1.8 fusion.60
  398.7 3.6 maximum_convert_fusion
  402.3 6.8 %convert_element_type.292 = f32[1024,2048]{1,0:T(8,128)} convert(bf16[1024,2048]{1,0:T(8,128)(2,1)} %get-tuple-element.41) | non-fusion elementwise | flops 2097152 | bytes 12582912 | tf_op jit(solution)/shard_map/convert_element_type | solution.py:584
  409.1 4.4 %convert_element_type.293 = f32[2048,1024]{1,0:T(8,128)} convert(bf16[2048,1024]{1,0:T(8,128)(2,1)S(1)} %copy-done.12) | non-fusion elementwise | flops 2097152 | bytes 12582912 | tf_op jit(solution)/shard_map/convert_element_type | solution.py:585
  (205 shorter events, 50.4 us)
Async XLA Ops:
  7.2 40.6 %copy-start = (bf16[1024,3,512]{2,0,1:T(8,128)(2,1)S(1)}, bf16[1024,3,512]{2,0,1:T(8,128)(2,1)}, u32[]{:S(2)}) copy-start(bf16[1024,3,512]{2,0,1:T(8,128)(2,1)} %param.13) | copy-start | bytes 9437188
  7.2 395.1 %all-reduce.3.cloned.1.call-start = ((), (), s32[]{:S(2)}) async-start(), calls=%async_computation | async-start | bytes 16777216 | tf_op jit(solution)/shard_map/psum | solution.py:508
  12.4 6.2 %collective-permute-start = (f32[6,512]{1,0:T(8,128)S(1)}, f32[6,512]{1,0:T(8,128)S(1)}, u32[]{:S(2)}, u32[]{:S(2)}) collective-permute-start(f32[6,512]{1,0:T(8,128)S(1)} %bitcast_add_fusion.1), channel_id=1, source_target_pairs={{0,1},{1,0},{2,3},{3,2},{4,5},{5,4},{6,7},{7,6},{8,9},{9,8},{10,11... | collective-permute-start | bytes 36872 | tf_op jit(solution)/shard_map/ppermute | solution.py:372
  15.4 24.9 %collective-permute-start.1 = (bf16[512,1024]{1,0:T(8,128)(2,1)}, bf16[512,1024]{1,0:T(8,128)(2,1)}, u32[]{:S(2)}, u32[]{:S(2)}) collective-permute-start(bf16[512,1024]{1,0:T(8,128)(2,1)} %bitcast), channel_id=1, source_target_pairs={{0,1},{1,0},{2,3},{3,2},{4,5},{5,4},{6,7},{7,6},{8,9},{9,8},{10,11... | collective-permute-start | bytes 3145736 | tf_op jit(solution)/shard_map/ppermute | solution.py:372
  43.5 50.1 %collective-permute-start.4 = (bf16[512,1024]{1,0:T(8,128)(2,1)}, bf16[512,1024]{1,0:T(8,128)(2,1)}, u32[]{:S(2)}, u32[]{:S(2)}) collective-permute-start(bf16[512,1024]{1,0:T(8,128)(2,1)} %param.14), channel_id=1, source_target_pairs={{0,1},{1,0},{2,3},{3,2},{4,5},{5,4},{6,7},{7,6},{8,9},{9,8},{10,11... | collective-permute-start | bytes 3145736 | tf_op jit(solution)/shard_map/ppermute | solution.py:372
  52.4 10.2 %copy-start.1 = (bf16[3,1024,512]{2,1,0:T(8,128)(2,1)}, bf16[3,1024,512]{2,1,0:T(8,128)(2,1)S(1)}, u32[]{:S(2)}) copy-start(bf16[3,1024,512]{2,1,0:T(8,128)(2,1)S(1)} %convert_bitcast_fusion.qkv_ref) | copy-start | bytes 9437188
  61.1 20.1 %collective-permute-start.2 = (bf16[1024,256]{1,0:T(8,128)(2,1)}, bf16[1024,256]{1,0:T(8,128)(2,1)}, u32[]{:S(2)}, u32[]{:S(2)}) collective-permute-start(bf16[1024,256]{1,0:T(8,128)(2,1)} %get-tuple-element.22), channel_id=1, source_target_pairs={{0,1},{1,0},{2,3},{3,2},{4,5},{5,4},{6,7},{7,6},{8,9},{9,8},{10,11... | collective-permute-start | bytes 1572872 | tf_op jit(solution)/shard_map/ppermute | solution.py:372
  71.5 20.9 %collective-permute-start.3 = (bf16[1024,256]{1,0:T(8,128)(2,1)}, bf16[1024,256]{1,0:T(8,128)(2,1)}, u32[]{:S(2)}, u32[]{:S(2)}) collective-permute-start(bf16[1024,256]{1,0:T(8,128)(2,1)} %get-tuple-element.23), channel_id=1, source_target_pairs={{0,1},{1,0},{2,3},{3,2},{4,5},{5,4},{6,7},{7,6},{8,9},{9,8},{10,11... | collective-permute-start | bytes 1572872 | tf_op jit(solution)/shard_map/ppermute | solution.py:372
  72.1 44.5 %collective-permute-start.5 = (bf16[512,1024]{1,0:T(8,128)(2,1)}, bf16[512,1024]{1,0:T(8,128)(2,1)S(1)}, u32[]{:S(2)}, u32[]{:S(2)}) collective-permute-start(bf16[512,1024]{1,0:T(8,128)(2,1)} %bitcast.85), channel_id=1, source_target_pairs={{0,1},{1,0},{2,3},{3,2},{4,5},{5,4},{6,7},{7,6},{8,9},{9,8},{10,11... | collective-permute-start | bytes 3145736 | tf_op jit(solution)/shard_map/ppermute | solution.py:372
  107.4 9.1 %copy-start.9 = (bf16[1,512,1024]{2,1,0:T(8,128)(2,1)S(1)}, bf16[1,512,1024]{2,1,0:T(8,128)(2,1)}, u32[]{:S(2)}) copy-start(bf16[1,512,1024]{2,1,0:T(8,128)(2,1)} %param.17) | copy-start | bytes 3145732
  116.5 26.1 %copy-start.35 = (bf16[1024,2048]{1,0:T(8,128)(2,1)}, bf16[1024,2048]{1,0:T(8,128)(2,1)S(1)}, u32[]{:S(2)}) copy-start(bf16[1024,2048]{1,0:T(8,128)(2,1)S(1)} %get-tuple-element.66) | copy-start | bytes 12582916
  136.0 20.7 %collective-permute-start.6 = (bf16[512,1024]{1,0:T(8,128)(2,1)}, bf16[512,1024]{1,0:T(8,128)(2,1)}, u32[]{:S(2)}, u32[]{:S(2)}) collective-permute-start(bf16[512,1024]{1,0:T(8,128)(2,1)} %fusion.50), channel_id=1, source_target_pairs={{0,1},{1,0},{2,3},{3,2},{4,5},{5,4},{6,7},{7,6},{8,9},{9,8},{10,11... | collective-permute-start | bytes 3145736 | tf_op jit(solution)/shard_map/ppermute | solution.py:372
  149.1 14.3 %copy-start.3 = (f32[512,1024]{1,0:T(8,128)S(1)}, f32[512,1024]{1,0:T(8,128)}, u32[]{:S(2)}) copy-start(f32[512,1024]{1,0:T(8,128)} %copy-done.2) | copy-start | bytes 6291460
  167.3 20.4 %collective-permute-start.7 = (bf16[512,1024]{1,0:T(8,128)(2,1)}, bf16[512,1024]{1,0:T(8,128)(2,1)}, u32[]{:S(2)}, u32[]{:S(2)}) collective-permute-start(bf16[512,1024]{1,0:T(8,128)(2,1)} %multiply_convert_fusion.1), channel_id=1, source_target_pairs={{0,1},{1,0},{2,3},{3,2},{4,5},{5,4},{6,7},{7,6},{8,9},{9,8},{10,11... | collective-permute-start | bytes 3145736 | tf_op jit(solution)/shard_map/ppermute | solution.py:372
  194.2 30.0 %copy-start.19 = (bf16[512,1024]{1,0:T(8,128)(2,1)S(1)}, bf16[512,1024]{1,0:T(8,128)(2,1)}, u32[]{:S(2)}) copy-start(bf16[512,1024]{1,0:T(8,128)(2,1)} %copy-done.18) | copy-start | bytes 3145732
  194.2 30.0 %copy-start.21 = (bf16[512,1024]{1,0:T(8,128)(2,1)S(1)}, bf16[512,1024]{1,0:T(8,128)(2,1)}, u32[]{:S(2)}) copy-start(bf16[512,1024]{1,0:T(8,128)(2,1)} %copy-done.20) | copy-start | bytes 3145732
  194.2 35.0 %collective-permute-start.32 = (bf16[256,1024]{1,0:T(8,128)(2,1)S(1)}, bf16[256,1024]{1,0:T(8,128)(2,1)S(1)}, u32[]{:S(2)}, u32[]{:S(2)}) collective-permute-start(bf16[256,1024]{1,0:T(8,128)(2,1)S(1)} %constant_dynamic-slice_fusion.3), channel_id=1, source_target_pairs={{0,2},{2,0},{4,6},{6,4},{8,10},{10,8},{12,14},{14,12},{16,18},{18,... | collective-permute-start | bytes 1572872 | tf_op jit(solution)/shard_map/ppermute | solution.py:387
  228.5 17.2 %collective-permute-start.24 = (bf16[256,3,512]{2,0,1:T(8,128)(2,1)S(1)}, bf16[256,3,512]{2,0,1:T(8,128)(2,1)S(1)}, u32[]{:S(2)}, u32[]{:S(2)}) collective-permute-start(bf16[256,3,512]{2,0,1:T(8,128)(2,1)S(1)} %constant_dynamic-slice_fusion.7), channel_id=1, source_target_pairs={{0,2},{2,0},{4,6},{6,4},{8,10},{10,8},{12,14},{14,12},{16,18},{18,... | collective-permute-start | bytes 2359304 | tf_op jit(solution)/shard_map/ppermute | solution.py:387
  228.9 18.5 %collective-permute-start.16 = (bf16[256,3,512]{2,0,1:T(8,128)(2,1)S(1)}, bf16[256,3,512]{2,0,1:T(8,128)(2,1)S(1)}, u32[]{:S(2)}, u32[]{:S(2)}) collective-permute-start(bf16[256,3,512]{2,0,1:T(8,128)(2,1)S(1)} %constant_dynamic-slice_fusion.11), channel_id=1, source_target_pairs={{0,2},{2,0},{4,6},{6,4},{8,10},{10,8},{12,14},{14,12},{16,18},{18,... | collective-permute-start | bytes 2359304 | tf_op jit(solution)/shard_map/ppermute | solution.py:387
  229.5 13.7 %collective-permute-start.33 = (bf16[128,1024]{1,0:T(8,128)(2,1)S(1)}, bf16[128,1024]{1,0:T(8,128)(2,1)S(1)}, u32[]{:S(2)}, u32[]{:S(2)}) collective-permute-start(bf16[128,1024]{1,0:T(8,128)(2,1)S(1)} %constant_dynamic-slice_fusion.2), channel_id=1, source_target_pairs={{0,8},{2,10},{4,12},{6,14},{8,0},{10,2},{12,4},{14,6},{16,24},{18,... | collective-permute-start | bytes 786440 | tf_op jit(solution)/shard_map/ppermute | solution.py:387
  232.3 26.1 %collective-permute-start.9 = (bf16[512,1024]{1,0:T(8,128)(2,1)S(1)}, bf16[512,1024]{1,0:T(8,128)(2,1)S(1)}, u32[]{:S(2)}, u32[]{:S(2)}) collective-permute-start(bf16[512,1024]{1,0:T(8,128)(2,1)S(1)} %bitcast_convert_fusion), channel_id=1, source_target_pairs={{0,1},{1,0},{2,3},{3,2},{4,5},{5,4},{6,7},{7,6},{8,9},{9,8},{10,11... | collective-permute-start | bytes 3145736 | tf_op jit(solution)/shard_map/ppermute | solution.py:372
  233.8 46.0 %collective-permute-start.8 = (bf16[512,1024]{1,0:T(8,128)(2,1)S(1)}, bf16[512,1024]{1,0:T(8,128)(2,1)S(1)}, u32[]{:S(2)}, u32[]{:S(2)}) collective-permute-start(bf16[512,1024]{1,0:T(8,128)(2,1)S(1)} %copy-done.34), channel_id=1, source_target_pairs={{0,1},{1,0},{2,3},{3,2},{4,5},{5,4},{6,7},{7,6},{8,9},{9,8},{10,11... | collective-permute-start | bytes 3145736 | tf_op jit(solution)/shard_map/ppermute | solution.py:372
  243.2 8.9 %collective-permute-start.34 = (bf16[64,1024]{1,0:T(8,128)(2,1)S(1)}, bf16[64,1024]{1,0:T(8,128)(2,1)S(1)}, u32[]{:S(2)}, u32[]{:S(2)}) collective-permute-start(bf16[64,1024]{1,0:T(8,128)(2,1)S(1)} %constant_dynamic-slice_fusion.1), channel_id=1, source_target_pairs={{0,16},{2,18},{4,20},{6,22},{8,24},{10,26},{12,28},{14,30},{16,0},... | collective-permute-start | bytes 393224 | tf_op jit(solution)/shard_map/ppermute | solution.py:387
  246.8 58.4 %collective-permute-start.25 = (bf16[128,3,512]{2,0,1:T(8,128)(2,1)}, bf16[128,3,512]{2,0,1:T(8,128)(2,1)}, u32[]{:S(2)}, u32[]{:S(2)}) collective-permute-start(bf16[128,3,512]{2,0,1:T(8,128)(2,1)} %constant_dynamic-slice_fusion.6), channel_id=1, source_target_pairs={{0,8},{2,10},{4,12},{6,14},{8,0},{10,2},{12,4},{14,6},{16,24},{18,... | collective-permute-start | bytes 1179656 | tf_op jit(solution)/shard_map/ppermute | solution.py:387
  248.5 59.8 %collective-permute-start.17 = (bf16[128,3,512]{2,0,1:T(8,128)(2,1)}, bf16[128,3,512]{2,0,1:T(8,128)(2,1)}, u32[]{:S(2)}, u32[]{:S(2)}) collective-permute-start(bf16[128,3,512]{2,0,1:T(8,128)(2,1)} %constant_dynamic-slice_fusion.10), channel_id=1, source_target_pairs={{0,4},{2,6},{4,0},{6,2},{8,12},{10,14},{12,8},{14,10},{16,20},{18,... | collective-permute-start | bytes 1179656 | tf_op jit(solution)/shard_map/ppermute | solution.py:387
  258.4 21.4 %copy-start.6 = (f32[1024,1024]{1,0:T(8,128)S(1)}, f32[1024,1024]{1,0:T(8,128)}, u32[]{:S(2)}) copy-start(f32[1024,1024]{1,0:T(8,128)} %copy-done.5) | copy-start | bytes 12582916
  258.4 21.4 %copy-start.8 = (f32[512,1024]{1,0:T(8,128)S(1)}, f32[512,1024]{1,0:T(8,128)}, u32[]{:S(2)}) copy-start(f32[512,1024]{1,0:T(8,128)} %copy-done.7) | copy-start | bytes 6291460
  258.4 21.4 %copy-start.17 = (f32[512,1024]{1,0:T(8,128)S(1)}, f32[512,1024]{1,0:T(8,128)}, u32[]{:S(2)}) copy-start(f32[512,1024]{1,0:T(8,128)} %fusion.32) | copy-start | bytes 6291460
  261.8 18.0 %copy-start.4 = (f32[512,1024]{1,0:T(8,128)S(1)}, f32[512,1024]{1,0:T(8,128)}, u32[]{:S(2)}) copy-start(f32[512,1024]{1,0:T(8,128)} %copy-done.2) | copy-start | bytes 6291460
  261.8 18.0 %copy-start.11 = (bf16[1,512,1024]{2,1,0:T(8,128)(2,1)S(1)}, bf16[1,512,1024]{2,1,0:T(8,128)(2,1)}, u32[]{:S(2)}) copy-start(bf16[1,512,1024]{2,1,0:T(8,128)(2,1)} %param.17) | copy-start | bytes 3145732
  264.2 23.4 %copy-start.24 = (bf16[1,1024]{1,0:T(2,128)(2,1)S(1)}, bf16[1,1024]{1,0:T(2,128)(2,1)}, u32[]{:S(2)}) copy-start(bf16[1,1024]{1,0:T(2,128)(2,1)} %copy-done.23) | copy-start | bytes 6148
  283.9 3.7 collective-permute-start.10
  285.5 5.6 %collective-permute-start.35 = (bf16[32,1024]{1,0:T(8,128)(2,1)S(1)}, bf16[32,1024]{1,0:T(8,128)(2,1)S(1)}, u32[]{:S(2)}, u32[]{:S(2)}) collective-permute-start(bf16[32,1024]{1,0:T(8,128)(2,1)S(1)} %constant_dynamic-slice_fusion), channel_id=1, source_target_pairs={{0,4},{2,6},{4,0},{6,2},{8,12},{10,14},{12,8},{14,10},{16,20},{18,... | collective-permute-start | bytes 196616 | tf_op jit(solution)/shard_map/ppermute | solution.py:387
  287.7 7.8 %copy-start.27 = (bf16[1,4096]{1,0:T(2,128)(2,1)}, bf16[1,4096]{1,0:T(2,128)(2,1)S(1)}, u32[]{:S(2)}) copy-start(bf16[1,4096]{1,0:T(2,128)(2,1)S(1)} %pad_maximum_fusion.14) | copy-start | bytes 24580
  287.7 4.5 %collective-permute-start.12 = (bf16[1,4096]{1,0:T(2,128)(2,1)S(1)}, bf16[1,4096]{1,0:T(2,128)(2,1)S(1)}, u32[]{:S(2)}, u32[]{:S(2)}) collective-permute-start(bf16[1,4096]{1,0:T(2,128)(2,1)S(1)} %pad_maximum_fusion.14), channel_id=1, source_target_pairs={{0,2},{2,0},{4,6},{6,4},{8,10},{10,8},{12,14},{14,12},{16,18},{18,... | collective-permute-start | bytes 24584 | tf_op jit(solution)/shard_map/ppermute | solution.py:407
  291.1 4.3 %collective-permute-start.36 = (bf16[32,1024]{1,0:T(8,128)(2,1)S(1)}, bf16[32,1024]{1,0:T(8,128)(2,1)S(1)}, u32[]{:S(2)}, u32[]{:S(2)}) collective-permute-start(bf16[32,1024]{1,0:T(8,128)(2,1)S(1)} %add_convert_fusion.15), channel_id=1, source_target_pairs={{0,4},{2,6},{4,0},{6,2},{8,12},{10,14},{12,8},{14,10},{16,20},{18,... | collective-permute-start | bytes 196616 | tf_op jit(solution)/shard_map/ppermute | solution.py:391
  292.3 5.9 %collective-permute-start.13 = (bf16[2,4096]{1,0:T(2,128)(2,1)S(1)}, bf16[2,4096]{1,0:T(2,128)(2,1)S(1)}, u32[]{:S(2)}, u32[]{:S(2)}) collective-permute-start(bf16[2,4096]{1,0:T(2,128)(2,1)S(1)} %pad_maximum_fusion.15), channel_id=1, source_target_pairs={{0,4},{2,6},{4,0},{6,2},{8,12},{10,14},{12,8},{14,10},{16,20},{18,... | collective-permute-start | bytes 49160 | tf_op jit(solution)/shard_map/ppermute | solution.py:407
  295.5 50.5 %collective-permute-start.37 = (bf16[64,1024]{1,0:T(8,128)(2,1)S(1)}, bf16[64,1024]{1,0:T(8,128)(2,1)S(1)}, u32[]{:S(2)}, u32[]{:S(2)}) collective-permute-start(bf16[64,1024]{1,0:T(8,128)(2,1)S(1)} %maximum_select_fusion.11), channel_id=1, source_target_pairs={{0,16},{2,18},{4,20},{6,22},{8,24},{10,26},{12,28},{14,30},{16,0},... | collective-permute-start | bytes 393224 | tf_op jit(solution)/shard_map/ppermute | solution.py:391
  298.2 5.8 %copy-start.25 = (bf16[2,4096]{1,0:T(2,128)(2,1)}, bf16[2,4096]{1,0:T(2,128)(2,1)S(1)}, u32[]{:S(2)}) copy-start(bf16[2,4096]{1,0:T(2,128)(2,1)S(1)} %collective-permute-done.13) | copy-start | bytes 49156
  298.3 5.7 %collective-permute-start.14 = (bf16[4,4096]{1,0:T(4,128)(2,1)S(1)}, bf16[4,4096]{1,0:T(4,128)(2,1)S(1)}, u32[]{:S(2)}, u32[]{:S(2)}) collective-permute-start(bf16[4,4096]{1,0:T(4,128)(2,1)S(1)} %pad_maximum_fusion.13), channel_id=1, source_target_pairs={{0,8},{2,10},{4,12},{6,14},{8,0},{10,2},{12,4},{14,6},{16,24},{18,... | collective-permute-start | bytes 98312 | tf_op jit(solution)/shard_map/ppermute | solution.py:407
  298.8 6.5 %copy-start.16 = (bf16[256,3,512]{2,0,1:T(8,128)(2,1)S(1)}, bf16[256,3,512]{2,0,1:T(8,128)(2,1)}, u32[]{:S(2)}) copy-start(bf16[256,3,512]{2,0,1:T(8,128)(2,1)} %copy-done.15) | copy-start | bytes 2359300
  298.8 9.5 %copy-start.14 = (bf16[256,3,512]{2,0,1:T(8,128)(2,1)S(1)}, bf16[256,3,512]{2,0,1:T(8,128)(2,1)}, u32[]{:S(2)}) copy-start(bf16[256,3,512]{2,0,1:T(8,128)(2,1)} %copy-done.13) | copy-start | bytes 2359300
  303.4 57.7 %collective-permute-start.11 = (f32[1,1024]{1,0:T(1,128)S(1)}, f32[1,1024]{1,0:T(1,128)S(1)}, u32[]{:S(2)}, u32[]{:S(2)}) collective-permute-start(f32[1,1024]{1,0:T(1,128)S(1)} %convolution_bitcast_fusion), channel_id=1, source_target_pairs={{0,1},{1,0},{2,3},{3,2},{4,5},{5,4},{6,7},{7,6},{8,9},{9,8},{10,11... | collective-permute-start | bytes 12296 | tf_op jit(solution)/shard_map/ppermute | solution.py:372
  304.0 20.6 %copy-start.26 = (bf16[4,4096]{1,0:T(4,128)(2,1)}, bf16[4,4096]{1,0:T(4,128)(2,1)S(1)}, u32[]{:S(2)}) copy-start(bf16[4,4096]{1,0:T(4,128)(2,1)S(1)} %collective-permute-done.14) | copy-start | bytes 98308
  304.1 57.6 %collective-permute-start.15 = (bf16[8,4096]{1,0:T(8,128)(2,1)S(1)}, bf16[8,4096]{1,0:T(8,128)(2,1)}, u32[]{:S(2)}, u32[]{:S(2)}) collective-permute-start(bf16[8,4096]{1,0:T(8,128)(2,1)S(1)} %pad_maximum_fusion.12), channel_id=1, source_target_pairs={{0,16},{2,18},{4,20},{6,22},{8,24},{10,26},{12,28},{14,30},{16,0},... | collective-permute-start | bytes 196616 | tf_op jit(solution)/shard_map/ppermute | solution.py:407
  306.4 14.1 %collective-permute-start.26 = (bf16[64,3,512]{2,0,1:T(8,128)(2,1)S(1)}, bf16[64,3,512]{2,0,1:T(8,128)(2,1)S(1)}, u32[]{:S(2)}, u32[]{:S(2)}) collective-permute-start(bf16[64,3,512]{2,0,1:T(8,128)(2,1)S(1)} %constant_dynamic-slice_fusion.5), channel_id=1, source_target_pairs={{0,16},{2,18},{4,20},{6,22},{8,24},{10,26},{12,28},{14,30},{16,0},... | collective-permute-start | bytes 589832 | tf_op jit(solution)/shard_map/ppermute | solution.py:387
  309.4 15.1 %collective-permute-start.18 = (bf16[64,3,512]{2,0,1:T(8,128)(2,1)S(1)}, bf16[64,3,512]{2,0,1:T(8,128)(2,1)S(1)}, u32[]{:S(2)}, u32[]{:S(2)}) collective-permute-start(bf16[64,3,512]{2,0,1:T(8,128)(2,1)S(1)} %constant_dynamic-slice_fusion.9), channel_id=1, source_target_pairs={{0,8},{2,10},{4,12},{6,14},{8,0},{10,2},{12,4},{14,6},{16,24},{18,... | collective-permute-start | bytes 589832 | tf_op jit(solution)/shard_map/ppermute | solution.py:387
  320.5 40.6 %copy-start.28 = (bf16[1,1024]{1,0:T(2,128)(2,1)S(1)}, bf16[1,1024]{1,0:T(2,128)(2,1)}, u32[]{:S(2)}) copy-start(bf16[1,1024]{1,0:T(2,128)(2,1)} %param.10) | copy-start | bytes 6148
  320.6 40.6 %copy-start.29 = (f32[1,1024]{1,0:T(1,128)S(1)}, f32[1,1024]{1,0:T(1,128)}, u32[]{:S(2)}) copy-start(f32[1,1024]{1,0:T(1,128)} %get-tuple-element.48) | copy-start | bytes 12292
  320.6 6.6 %collective-permute-start.27 = (bf16[32,3,512]{2,0,1:T(8,128)(2,1)S(1)}, bf16[32,3,512]{2,0,1:T(8,128)(2,1)S(1)}, u32[]{:S(2)}, u32[]{:S(2)}) collective-permute-start(bf16[32,3,512]{2,0,1:T(8,128)(2,1)S(1)} %constant_dynamic-slice_fusion.4), channel_id=1, source_target_pairs={{0,4},{2,6},{4,0},{6,2},{8,12},{10,14},{12,8},{14,10},{16,20},{18,... | collective-permute-start | bytes 294920 | tf_op jit(solution)/shard_map/ppermute | solution.py:387
  324.7 10.8 %collective-permute-start.19 = (bf16[32,3,512]{2,0,1:T(8,128)(2,1)S(1)}, bf16[32,3,512]{2,0,1:T(8,128)(2,1)S(1)}, u32[]{:S(2)}, u32[]{:S(2)}) collective-permute-start(bf16[32,3,512]{2,0,1:T(8,128)(2,1)S(1)} %constant_dynamic-slice_fusion.8), channel_id=1, source_target_pairs={{0,16},{2,18},{4,20},{6,22},{8,24},{10,26},{12,28},{14,30},{16,0},... | collective-permute-start | bytes 294920 | tf_op jit(solution)/shard_map/ppermute | solution.py:387
  327.2 8.4 %collective-permute-start.28 = (bf16[32,3,512]{2,0,1:T(8,128)(2,1)S(1)}, bf16[32,3,512]{2,0,1:T(8,128)(2,1)S(1)}, u32[]{:S(2)}, u32[]{:S(2)}) collective-permute-start(bf16[32,3,512]{2,0,1:T(8,128)(2,1)S(1)} %add_convert_fusion.13), channel_id=1, source_target_pairs={{0,4},{2,6},{4,0},{6,2},{8,12},{10,14},{12,8},{14,10},{16,20},{18,... | collective-permute-start | bytes 294920 | tf_op jit(solution)/shard_map/ppermute | solution.py:391
  335.5 10.3 %collective-permute-start.20 = (bf16[32,3,512]{2,0,1:T(8,128)(2,1)S(1)}, bf16[32,3,512]{2,0,1:T(8,128)(2,1)S(1)}, u32[]{:S(2)}, u32[]{:S(2)}) collective-permute-start(bf16[32,3,512]{2,0,1:T(8,128)(2,1)S(1)} %add_convert_fusion.14), channel_id=1, source_target_pairs={{0,16},{2,18},{4,20},{6,22},{8,24},{10,26},{12,28},{14,30},{16,0},... | collective-permute-start | bytes 294920 | tf_op jit(solution)/shard_map/ppermute | solution.py:391
  335.7 18.5 %collective-permute-start.29 = (bf16[64,3,512]{2,0,1:T(8,128)(2,1)S(1)}, bf16[64,3,512]{2,0,1:T(8,128)(2,1)S(1)}, u32[]{:S(2)}, u32[]{:S(2)}) collective-permute-start(bf16[64,3,512]{2,0,1:T(8,128)(2,1)S(1)} %maximum_select_fusion.10), channel_id=1, source_target_pairs={{0,16},{2,18},{4,20},{6,22},{8,24},{10,26},{12,28},{14,30},{16,0},... | collective-permute-start | bytes 589832 | tf_op jit(solution)/shard_map/ppermute | solution.py:391
  345.9 13.3 %collective-permute-start.21 = (bf16[64,3,512]{2,0,1:T(8,128)(2,1)S(1)}, bf16[64,3,512]{2,0,1:T(8,128)(2,1)S(1)}, u32[]{:S(2)}, u32[]{:S(2)}) collective-permute-start(bf16[64,3,512]{2,0,1:T(8,128)(2,1)S(1)} %maximum_select_fusion.9), channel_id=1, source_target_pairs={{0,8},{2,10},{4,12},{6,14},{8,0},{10,2},{12,4},{14,6},{16,24},{18,... | collective-permute-start | bytes 589832 | tf_op jit(solution)/shard_map/ppermute | solution.py:391
  346.7 23.8 %collective-permute-start.38 = (bf16[128,1024]{1,0:T(8,128)(2,1)}, bf16[128,1024]{1,0:T(8,128)(2,1)}, u32[]{:S(2)}, u32[]{:S(2)}) collective-permute-start(bf16[128,1024]{1,0:T(8,128)(2,1)} %maximum_select_fusion.8), channel_id=1, source_target_pairs={{0,8},{2,10},{4,12},{6,14},{8,0},{10,2},{12,4},{14,6},{16,24},{18,... | collective-permute-start | bytes 786440 | tf_op jit(solution)/shard_map/ppermute | solution.py:391
  354.3 31.0 %collective-permute-start.30 = (bf16[128,3,512]{2,0,1:T(8,128)(2,1)S(1)}, bf16[128,3,512]{2,0,1:T(8,128)(2,1)}, u32[]{:S(2)}, u32[]{:S(2)}) collective-permute-start(bf16[128,3,512]{2,0,1:T(8,128)(2,1)S(1)} %maximum_select_fusion.7), channel_id=1, source_target_pairs={{0,8},{2,10},{4,12},{6,14},{8,0},{10,2},{12,4},{14,6},{16,24},{18,... | collective-permute-start | bytes 1179656 | tf_op jit(solution)/shard_map/ppermute | solution.py:391
  360.1 26.6 %collective-permute-start.22 = (bf16[128,3,512]{2,0,1:T(8,128)(2,1)}, bf16[128,3,512]{2,0,1:T(8,128)(2,1)}, u32[]{:S(2)}, u32[]{:S(2)}) collective-permute-start(bf16[128,3,512]{2,0,1:T(8,128)(2,1)} %maximum_select_fusion.6), channel_id=1, source_target_pairs={{0,4},{2,6},{4,0},{6,2},{8,12},{10,14},{12,8},{14,10},{16,20},{18,... | collective-permute-start | bytes 1179656 | tf_op jit(solution)/shard_map/ppermute | solution.py:391
  366.2 22.8 %copy-start.22 = (bf16[16,4096]{1,0:T(8,128)(2,1)S(1)}, bf16[16,4096]{1,0:T(8,128)(2,1)}, u32[]{:S(2)}) copy-start(bf16[16,4096]{1,0:T(8,128)(2,1)} %concatenate.152) | copy-start | bytes 393220
  366.2 22.8 %slice-start = ((bf16[16,4096]{1,0:T(8,128)(2,1)}), bf16[16,3072]{1,0:T(8,128)(2,1)S(1)}, s32[]{:S(2)}) async-start(bf16[16,4096]{1,0:T(8,128)(2,1)} %concatenate.152), calls=%async_computation.1 | async-start | bytes 196608 | tf_op jit(solution)/shard_map/slice | solution.py:567
  372.0 23.7 %collective-permute-start.39 = (bf16[256,1024]{1,0:T(8,128)(2,1)S(1)}, bf16[256,1024]{1,0:T(8,128)(2,1)S(1)}, u32[]{:S(2)}, u32[]{:S(2)}) collective-permute-start(bf16[256,1024]{1,0:T(8,128)(2,1)S(1)} %maximum_select_fusion.5), channel_id=1, source_target_pairs={{0,2},{2,0},{4,6},{6,4},{8,10},{10,8},{12,14},{14,12},{16,18},{18,... | collective-permute-start | bytes 1572872 | tf_op jit(solution)/shard_map/ppermute | solution.py:391
  386.6 10.8 %collective-permute-start.31 = (bf16[256,3,512]{2,0,1:T(8,128)(2,1)S(1)}, bf16[256,3,512]{2,0,1:T(8,128)(2,1)S(1)}, u32[]{:S(2)}, u32[]{:S(2)}) collective-permute-start(bf16[256,3,512]{2,0,1:T(8,128)(2,1)S(1)} %maximum_select_fusion.4), channel_id=1, source_target_pairs={{0,2},{2,0},{4,6},{6,4},{8,10},{10,8},{12,14},{14,12},{16,18},{18,... | collective-permute-start | bytes 2359304 | tf_op jit(solution)/shard_map/ppermute | solution.py:391
  388.5 9.6 %collective-permute-start.23 = (bf16[256,3,512]{2,0,1:T(8,128)(2,1)S(1)}, bf16[256,3,512]{2,0,1:T(8,128)(2,1)S(1)}, u32[]{:S(2)}, u32[]{:S(2)}) collective-permute-start(bf16[256,3,512]{2,0,1:T(8,128)(2,1)S(1)} %maximum_select_fusion.3), channel_id=1, source_target_pairs={{0,2},{2,0},{4,6},{6,4},{8,10},{10,8},{12,14},{14,12},{16,18},{18,... | collective-permute-start | bytes 2359304 | tf_op jit(solution)/shard_map/ppermute | solution.py:391
  402.2 6.8 %copy-start.12 = (bf16[2048,1024]{1,0:T(8,128)(2,1)S(1)}, bf16[2048,1024]{1,0:T(8,128)(2,1)}, u32[]{:S(2)}) copy-start(bf16[2048,1024]{1,0:T(8,128)(2,1)} %get-tuple-element.42) | copy-start | bytes 12582916
  (16 other events, 49.0 us)
Sparse Core Ops, SparseCore 0:
  176.3 222.1 all-reduce.2
